TPU v7x, 32 devices: a whole 2x2x4 slice. The times are simulated.
32 devices in a mesh: row: 8 (over y, x, core), col: 4 (over z).
Axes of the slice: x: 2, y: 2, z: 4, core: 2. Of those that a mesh axis runs over, the one named last changes fastest.
Arguments:
- queries: bfloat16 [1024, 3072], P('row'), may hold values from -30 to 30
- latent_pool: bfloat16 [128, 64, 576], P('col'), may hold values from -6 to 6
- block_table: int32 [128], P('col'), may hold values from 0 to 31, as said below
- page_len: int32 [128], P('col'), may hold values from 16 to 64
- group_offset: int32 [1], replicated, may hold values from 0 to 7168
- hidden: bfloat16 [1024, 2048], P('row'), may hold values from -4 to 4
- latent_up: bfloat16 [512, 4096], replicated, may hold values from -0.25 to 0.25
- output_weight: bfloat16 [2048, 2048], P('col'), may hold values from -0.1875 to 0.1875
- gate_weight: bfloat16 [2048, 10944], P('row', 'col'), may hold values from -0.125 to 0.125
- up_weight: bfloat16 [2048, 10944], P('row', 'col'), may hold values from -0.125 to 0.125
- down_weight: bfloat16 [10944, 2048], P('col', 'row'), may hold values from -0.078125 to 0.078125
Outputs:
- attended: bfloat16 [1024, 2048], P('row')
- block_out: bfloat16 [1024, 2048], P('row', 'col')
Inputs may be any that keep to these rules, and one draw needn't show every extreme that they name: `block_table`: the 32 logical pages of one col index name its 32 pool pages, each once.
All inputs are finite; a program needn't handle non-finite values.
Results may differ from a plain program's by a relative error of at most 0.015.
Values may be sent and summed in bfloat16 or wider, within the bound.
No kernel may reach another device: no remote copies, remote signals or barrier semaphores. Data moves between devices by JAX's collectives and lax.ppermute only.
A program may use at most 128 MiB of HBM per device.

v0:
```python
import math

import jax
import jax.numpy as jnp
from jax import lax
from jax.sharding import PartitionSpec as P

H = 16
NOPE = 128
VDIM = 128
LATENT = 512
QK = 192


def on_device(
    queries,
    latent_pool,
    block_table,
    page_len,
    group_offset,
    hidden,
    latent_up,
    output_weight,
    gate_weight,
    up_weight,
    down_weight,
):
    col_count = lax.axis_size("col")
    col_index = lax.axis_index("col")
    row_index = lax.axis_index("row")
    query_rows = queries.shape[0]
    page_count, page_size, cache_width = latent_pool.shape
    key_count = page_count * page_size
    latent = latent_pool[block_table].reshape(key_count, cache_width)
    key_index = jnp.arange(key_count, dtype=jnp.int32)
    positions = col_index * key_count + key_index
    lengths = jnp.broadcast_to(page_len[:, None], (page_count, page_size)).reshape(key_count)
    key_valid = key_index % page_size < lengths
    query_pos = group_offset[0] + row_index * query_rows + jnp.arange(query_rows, dtype=jnp.int32)
    visible = key_valid[None, :] & (positions[None, :] <= query_pos[:, None])
    latent_part = latent[:, :LATENT]
    rope_keys = latent[:, LATENT:]
    per_head = queries.reshape(query_rows, H, QK)
    score_scale = 1.0 / math.sqrt(QK)

    def one_head(head_index):
        columns = lax.dynamic_slice_in_dim(latent_up, head_index * (NOPE + VDIM), NOPE + VDIM, 1)
        expanded = jnp.dot(latent_part, columns, preferred_element_type=jnp.float32).astype(
            jnp.bfloat16
        )
        key_rows = jnp.concatenate([expanded[:, :NOPE], rope_keys], axis=1)
        values = expanded[:, NOPE:]
        head_queries = lax.dynamic_index_in_dim(per_head, head_index, 1, keepdims=False)
        scores = jnp.dot(head_queries, key_rows.T, preferred_element_type=jnp.float32) * score_scale
        row_max = jnp.max(jnp.where(visible, scores, -1e30), axis=1)
        weights = jnp.where(visible, jnp.exp(scores - row_max[:, None]), 0.0)
        totals = jnp.sum(weights, axis=1)
        outputs = jnp.dot(weights.astype(jnp.bfloat16), values, preferred_element_type=jnp.float32)
        return (row_max, totals, outputs)

    head_max, head_total, head_out = lax.map(one_head, jnp.arange(H, dtype=jnp.int32))
    heads_here = H // col_count
    out_rows = output_weight.reshape(heads_here, VDIM, output_weight.shape[1])
    part_max = lax.all_to_all(head_max[None], "col", split_axis=1, concat_axis=0, tiled=True)
    part_total = lax.all_to_all(head_total[None], "col", split_axis=1, concat_axis=0, tiled=True)
    part_out = lax.all_to_all(head_out[None], "col", split_axis=1, concat_axis=0, tiled=True)
    row_max = jnp.max(part_max, axis=0)
    scales = jnp.exp(part_max - row_max[None])
    totals = jnp.sum(scales * part_total, axis=0)
    outputs = jnp.sum(scales[..., None] * part_out, axis=0)
    head_mix = (outputs / totals[..., None]).astype(jnp.bfloat16)
    partial_value = jnp.einsum(
        "hqv,hvd->qd", head_mix, out_rows, preferred_element_type=jnp.float32
    )
    width_here = hidden.shape[1] // col_count
    projected = lax.psum(partial_value, "col")
    attended = (hidden.astype(jnp.float32) + projected).astype(jnp.bfloat16)
    wide = attended.astype(jnp.float32)
    mean_square = jnp.mean(wide * wide, axis=1, keepdims=True)
    normed = (wide * lax.rsqrt(mean_square + 1e-06)).astype(jnp.bfloat16)
    gate_piece = lax.all_gather(gate_weight, "row", axis=0, tiled=True)
    up_piece = lax.all_gather(up_weight, "row", axis=0, tiled=True)
    gate_next = jnp.dot(normed, gate_piece, preferred_element_type=jnp.float32)
    up_next = jnp.dot(normed, up_piece, preferred_element_type=jnp.float32)
    activated = (jax.nn.silu(gate_next) * up_next).astype(jnp.bfloat16)
    mlp_terms = jnp.dot(
        activated,
        lax.all_gather(down_weight, "row", axis=1, tiled=True),
        preferred_element_type=jnp.float32,
    )
    mlp_share = lax.psum_scatter(mlp_terms, "col", scatter_dimension=1, tiled=True)
    attended_part = lax.dynamic_slice_in_dim(wide, col_index * width_here, width_here, 1)
    block_out = (attended_part + mlp_share).astype(jnp.bfloat16)
    return (attended, block_out)


def solution(mesh):
    placed = (
        P("row", None),
        P("col", None, None),
        P("col"),
        P("col"),
        P(),
        P("row", None),
        P(),
        P("col", None),
        P("row", "col"),
        P("row", "col"),
        P("col", "row"),
    )
    return jax.shard_map(
        on_device,
        mesh=mesh,
        in_specs=placed,
        out_specs=(P("row", None), P("row", "col")),
        check_vma=False,
    )
```

profile of v0, /device:TPU:0, one launch (start us, length us, event | category | flops | bytes accessed | tf_op | source)
XLA Modules:
  0.0 489.9 jit_solution(11954969272634571519)
XLA Ops:
  12.2 3.1 slice.20
  19.7 155.3 %while.15 = (s32[]{:T(128)}, f32[16,128]{1,0:T(8,128)S(1)}, f32[16,128]{1,0:T(8,128)S(1)}, f32[16,128,128]{2,1,0:T(8,128)}, s32[16]{0:T(128)S(1)}, /*index=5*/bf...) while((s32[]{:T(128)}, f32[16,128]{1,0:T(8,128)S(1)}, ...), condition=%wide.region_3.4_spmd.clone, body=%wide.region_0.3_spmd.clone.sunk | while | flops 710672128 | bytes 17453376 | solution.py:61
  20.9 2.5 fusion.49
  40.3 2.5 fusion.49
  50.0 2.5 fusion.49
  59.7 2.5 fusion.49
  79.1 2.5 fusion.49
  88.9 2.5 fusion.49
  108.3 2.5 fusion.49
  127.7 2.5 fusion.49
  166.5 2.5 fusion.49
  175.0 11.7 %all_to_all.36 = f32[1,16,128]{2,0,1:T(1,128)S(1)} all-to-all(f32[1,16,128]{2,0,1:T(1,128)S(1)} %bitcast.56), channel_id=1, replica_groups=mesh['row'=8,'col'=4] {'col'}, dimensions={1} | all-to-all | bytes 16384 | tf_op jit(solution)/shard_map/all_to_all | solution.py:64
  186.7 7.9 %all_to_all.37 = f32[1,16,128]{2,0,1:T(1,128)S(1)} all-to-all(f32[1,16,128]{2,0,1:T(1,128)S(1)} %bitcast.57), channel_id=1, replica_groups=mesh['row'=8,'col'=4] {'col'}, dimensions={1} | all-to-all | bytes 16384 | tf_op jit(solution)/shard_map/all_to_all | solution.py:65
  194.6 4.2 all-to-all-start.1
  199.0 23.4 %all-to-all-done.1 = f32[1,16,128,128]{3,2,0,1:T(8,128)} async-done(((f32[1,16,128,128]{3,2,0,1:T(8,128)}), f32[1,16,128,128]{3,2,0,1:T(8,128)}, u32[]{:S(2)}, u32[]{:S(2)}) %all-to-all-start.1) | async-done | bytes 1048608 | tf_op jit(solution)/shard_map/all_to_all | solution.py:66
  224.0 3.1 convolution_bitcast_fusion.1
  229.0 49.1 %all-reduce.2.cloned.1.call-done = f32[128,2048]{1,0:T(8,128)} async-done(((f32[128,2048]{1,0:T(8,128)}), f32[128,2048]{1,0:T(8,128)}) %all-reduce.2.cloned.1.call-update) | async-done | bytes 1048592 | tf_op jit(solution)/shard_map/psum | solution.py:76
  278.1 2.6 fusion.32
  280.9 16.1 %all-gather.4.cloned.1.call-done = bf16[2048,2736]{0,1:T(8,128)(2,1)} async-done(((bf16[256,2736]{0,1:T(8,128)(2,1)}), bf16[2048,2736]{0,1:T(8,128)(2,1)}) %all-gather.4.cloned.1.call-update) | async-done | bytes 11206672 | tf_op jit(solution)/shard_map/all_gather | solution.py:81
  297.0 7.1 %fusion.25 = f32[128,2736]{0,1:T(8,128)} fusion(bf16[2048,2736]{0,1:T(8,128)(2,1)} %all-gather.4.cloned.1.call-done, f32[128]{0:T(128)S(1)} %add_rsqrt_fusion, bf16[128,2048]{1,0:T(8,128)(2,1)S(1)} %get-tuple-element.149), kind=kOutput, calls=%fused_computation.38 | convolution fusion | flops 1435238400 | bytes 13132288 | tf_op jit(solution)/shard_map/dot_general | solution.py:83
  304.1 63.1 %all-gather.6.cloned.1.call-done = bf16[2048,2736]{0,1:T(8,128)(2,1)} async-done(((bf16[256,2736]{0,1:T(8,128)(2,1)}), bf16[2048,2736]{0,1:T(8,128)(2,1)}) %all-gather.6.cloned.1.call-update) | async-done | bytes 11206672 | tf_op jit(solution)/shard_map/all_gather | solution.py:82
  367.2 70.2 %all-gather.8.cloned.1.call-done = bf16[2736,2048]{1,0:T(8,128)(2,1)} async-done(((bf16[2736,256]{1,0:T(8,128)(2,1)}), bf16[2736,2048]{1,0:T(8,128)(2,1)}) %all-gather.8.cloned.1.call-update) | async-done | bytes 11206672 | tf_op jit(solution)/shard_map/all_gather | solution.py:88
  437.4 15.9 %fusion.24 = f32[128,2048]{1,0:T(8,128)} fusion(bf16[2736,2048]{1,0:T(8,128)(2,1)} %all-gather.8.cloned.1.call-done, bf16[2048,2736]{0,1:T(8,128)(2,1)} %all-gather.6.cloned.1.call-done, f32[128,2736]{0,1:T(8,128)} %fusion.25, f32[128]{0:T(128)S(1)} %add_rsqrt_fusion, bf16[128,2048]{1,0:T(8,128)(2,1)S(1)} %get-tuple-element.149), kind=kOutput, calls=%fused_computation.35 | convolution fusion | flops 2871791616 | bytes 25387520 | tf_op jit(solution)/shard_map/dot_general | solution.py:86
  453.3 27.3 %reduce-scatter.2.cloned.1.call-done = f32[128,512]{1,0:T(8,128)} async-done(((f32[128,2048]{1,0:T(8,128)}), f32[128,512]{1,0:T(8,128)}) %reduce-scatter.2.cloned.1.call-update) | async-done | bytes 262160 | tf_op jit(solution)/shard_map/reduce_scatter | solution.py:91
  (220 shorter events, 104.2 us)
Async XLA Ops:
  8.0 1.8 copy-start
  15.2 4.3 copy-start.4
  26.4 1.4 copy-start.2
  36.0 1.4 copy-start.2
  55.4 1.4 copy-start.2
  65.1 1.4 copy-start.2
  74.9 1.4 copy-start.2
  84.6 1.4 copy-start.2
  94.3 1.4 copy-start.2
  104.0 1.4 copy-start.2
  113.7 1.4 copy-start.2
  123.4 1.4 copy-start.2
  133.1 1.4 copy-start.2
  142.8 1.4 copy-start.2
  152.5 1.4 copy-start.2
  162.2 1.4 copy-start.2
  171.9 1.4 copy-start.2
  194.6 27.8 %all-to-all-start.1 = ((f32[1,16,128,128]{3,2,0,1:T(8,128)}), f32[1,16,128,128]{3,2,0,1:T(8,128)}, u32[]{:S(2)}, u32[]{:S(2)}) async-start(f32[1,16,128,128]{3,2,0,1:T(8,128)} %bitcast.49), calls=%async_computation.1 | async-start | bytes 2097152 | tf_op jit(solution)/shard_map/all_to_all | solution.py:66
  198.9 79.3 %all-reduce.2.cloned.1.call-start = ((), (), s32[]{:S(2)}) async-start(), calls=%async_computation.4 | async-start | bytes 2097152 | tf_op jit(solution)/shard_map/psum | solution.py:76
  227.1 69.9 %all-gather.4.cloned.1.call-start = ((), (), s32[]{:S(2)}) async-start(), calls=%async_computation.5 | async-start | bytes 12607488 | tf_op jit(solution)/shard_map/all_gather | solution.py:81
  227.6 139.5 %all-gather.6.cloned.1.call-start = ((), (), s32[]{:S(2)}) async-start(), calls=%async_computation.6 | async-start | bytes 12607488 | tf_op jit(solution)/shard_map/all_gather | solution.py:82
  228.2 209.1 %all-gather.8.cloned.1.call-start = ((), (), s32[]{:S(2)}) async-start(), calls=%async_computation.7 | async-start | bytes 12607488 | tf_op jit(solution)/shard_map/all_gather | solution.py:88
  228.8 251.8 %reduce-scatter.2.cloned.1.call-start = ((), (), s32[]{:S(2)}) async-start(), calls=%async_computation.8 | async-start | bytes 1310720 | tf_op jit(solution)/shard_map/reduce_scatter | solution.py:91
  280.7 156.7 %copy-start.3 = (bf16[128,2048]{1,0:T(8,128)(2,1)}, bf16[128,2048]{1,0:T(8,128)(2,1)S(1)}, u32[]{:S(2)}) copy-start(bf16[128,2048]{1,0:T(8,128)(2,1)S(1)} %get-tuple-element.149) | copy-start | bytes 1572868
  (17 other events, 17.1 us)
Sparse Core Ops, SparseCore 0:
  227.2 50.9 all-reduce.1
  453.4 27.1 reduce-scatter.1
Sparse Core Ops, SparseCore 1:
  229.6 67.4 all-gather.3
  298.9 68.2 all-gather.5
  369.1 68.2 all-gather.7
where the time goes:
time: 492 us; the launch traced here: 490 us
  waiting for transfers between devices  251 us (51%)
  matrix products  105 us (21%)
  loops' own time  42.4 us (9%)
  local copies, waits for them, and re-layouts  36.8 us (7%)
  blocking collectives  19.6 us (4%)
  between operations  16.4 us (3%)
  other arithmetic  14.1 us (3%)
    all_gather x1, waiting for transfers between devices, on_device(): lax.all_gather(down_weight, 'row', axis=1, tiled=True)  70.2 us
    all_gather x1, waiting for transfers between devices, on_device(): up_piece = lax.all_gather(up_weight, 'row', axis=0, tiled=True)  63.1 us
    psum x1, waiting for transfers between devices, on_device(): projected = lax.psum(partial_value, 'col')  49.1 us
    another operation x1, loops' own time, on_device(): lax.map(one_head, jnp.arange(H, dtype=jnp.int32))  42.4 us
    dot_general x16, matrix products, one_head(): jnp.dot(latent_part, columns, preferred_element_type=jnp.float32)  39.3 us
    reduce_scatter x1, waiting for transfers between devices, on_device(): lax.psum_scatter(mlp_terms, 'col', scatter_dimension=1, tiled=True)  27.3 us
    all_to_all x1, waiting for transfers between devices, on_device(): lax.all_to_all(head_out[None], 'col', split_axis=1, concat_axis=0, tiled=...  23.4 us
    dot_general x16, matrix products, one_head(): jnp.dot(head_queries, key_rows.T, preferred_element_type=jnp.float32)  22.2 us
  transfers between devices with their start and end apart: 6, of which 6 were waited for; matrix products, arithmetic and copies ran while one was open for 2% of the time, Pallas kernels for 0%

commit v1 on v0

v1 whole, which is shorter than its diff:
```python
import functools
import math

import jax
import jax.numpy as jnp
from jax import lax
from jax.experimental import pallas as pl
from jax.experimental.pallas import tpu as pltpu
from jax.sharding import PartitionSpec as P

H = 16
NOPE = 128
ROPE = 64
VDIM = 128
LATENT = 512
QK = NOPE + ROPE
HEAD_UP = NOPE + VDIM
LANES = 128
TAIL = 16
HIDDEN_SCORE = -1e30
LOG2_SCALE = math.log2(math.e) / math.sqrt(QK)
NT = (((1,), (1,)), ((), ()))


def exchange(x, axis, step):
    count = lax.axis_size(axis)
    return lax.ppermute(x, axis, [(i, i ^ step) for i in range(count)])


def rotate(x, axis, step):
    count = lax.axis_size(axis)
    return lax.ppermute(x, axis, [(i, (i + step) % count) for i in range(count)])


def attention_kernel(
    groups, table_ref, len_ref, meta_ref, queries_ref, pool_ref, up_ref, *refs
):
    outs = refs[:groups]
    pages_ref, keys_ref, q_ref, sem = refs[groups:]
    page_count, page_size, _ = pages_ref.shape
    query_rows = queries_ref.shape[0]
    heads_here = H // groups
    first_query = meta_ref[0]
    first_key = meta_ref[1]
    col_index = meta_ref[2]

    def page_copy(p):
        return pltpu.make_async_copy(pool_ref.at[table_ref[p]], pages_ref.at[p], sem.at[p])

    for p in range(page_count):
        page_copy(p).start()

    eye = (
        lax.broadcasted_iota(jnp.int32, (query_rows, query_rows), 0)
        == lax.broadcasted_iota(jnp.int32, (query_rows, query_rows), 1)
    ).astype(jnp.bfloat16)
    for h in range(H):
        rows = pl.ds(h * query_rows, query_rows)
        q_nope = queries_ref[:, h * QK : h * QK + NOPE]
        up_k = up_ref[:, h * HEAD_UP : h * HEAD_UP + NOPE]
        absorbed = lax.dot_general(q_nope, up_k, NT, preferred_element_type=jnp.float32)
        q_ref[rows, :LATENT] = absorbed.astype(jnp.bfloat16)
        q_rope = queries_ref[:, h * QK + NOPE : (h + 1) * QK]
        q_ref[rows, LATENT : LATENT + LANES] = jnp.concatenate(
            [q_rope, jnp.zeros((query_rows, LANES - ROPE), jnp.bfloat16)], axis=1
        )
        q_ref[rows, LATENT + LANES :] = eye

    slot = lax.broadcasted_iota(jnp.int32, (page_size, query_rows), 0)
    query_pos = first_query + lax.broadcasted_iota(jnp.int32, (page_size, query_rows), 1)
    for p in range(page_count):
        page_copy(p).wait()
        rows = pl.ds(p * page_size, page_size)
        page = pages_ref[p]
        keys_ref[rows, :LATENT] = page[:, :LATENT]
        keys_ref[rows, LATENT : LATENT + LANES] = jnp.concatenate(
            [page[:, LATENT:], jnp.zeros((page_size, LANES - ROPE), jnp.bfloat16)], axis=1
        )
        seen = (slot < len_ref[p]) & (first_key + p * page_size + slot <= query_pos)
        keys_ref[rows, LATENT + LANES :] = jnp.where(seen, 0.0, HIDDEN_SCORE).astype(jnp.bfloat16)

    for step in range(groups):
        group = lax.rem(col_index + step, groups)
        block = heads_here * query_rows
        q_rows = q_ref[pl.ds(pl.multiple_of(group * block, block), block), :]
        scores = lax.dot_general(q_rows, keys_ref[...], NT, preferred_element_type=jnp.float32)
        row_max = jnp.max(scores, axis=1, keepdims=True)
        weights = jnp.exp2((scores - row_max) * LOG2_SCALE)
        totals = jnp.sum(weights, axis=1, keepdims=True)
        context = jnp.dot(
            weights.astype(jnp.bfloat16), keys_ref[:, :LATENT], preferred_element_type=jnp.float32
        )
        context = (context / totals).astype(jnp.bfloat16)
        log_sum = row_max * LOG2_SCALE + jnp.log2(totals)
        out_ref = outs[step]
        tail = []
        for j in range(heads_here):
            own = slice(j * query_rows, (j + 1) * query_rows)
            at = pl.multiple_of((group * heads_here + j) * HEAD_UP + NOPE, LANES)
            up_v = up_ref[:, pl.ds(at, VDIM)]
            mixed = jnp.dot(context[own], up_v, preferred_element_type=jnp.float32)
            out_ref[:query_rows, j * VDIM : (j + 1) * VDIM] = mixed.astype(jnp.bfloat16)
            wide = jnp.broadcast_to(log_sum[own], (query_rows, LANES))
            tail.append(jnp.transpose(wide)[:1])
        tail = jnp.concatenate(tail, axis=1)
        high = tail.astype(jnp.bfloat16)
        rest = tail - high.astype(jnp.float32)
        middle = rest.astype(jnp.bfloat16)
        low = (rest - middle.astype(jnp.float32)).astype(jnp.bfloat16)
        width = tail.shape[1]
        parts = [high.astype(jnp.float32), middle.astype(jnp.float32), low.astype(jnp.float32)]
        parts.append(jnp.zeros((TAIL - 3, width), jnp.float32))
        out_ref[query_rows:, :] = jnp.concatenate(parts, axis=0).astype(jnp.bfloat16)


def attention(queries, latent_pool, block_table, page_len, latent_up, meta, groups):
    query_rows = queries.shape[0]
    page_count, page_size, cache_width = latent_pool.shape
    keys = page_count * page_size
    width = LATENT + LANES + query_rows
    heads_here = H // groups
    vmem = pl.BlockSpec(memory_space=pltpu.VMEM)
    smem = pl.BlockSpec(memory_space=pltpu.SMEM)
    payload = jax.ShapeDtypeStruct((query_rows + TAIL, heads_here * VDIM), jnp.bfloat16)
    return pl.pallas_call(
        functools.partial(attention_kernel, groups),
        out_shape=[payload] * groups,
        in_specs=[smem, smem, smem, vmem, pl.BlockSpec(memory_space=pl.ANY), vmem],
        out_specs=[vmem] * groups,
        scratch_shapes=[
            pltpu.VMEM((page_count, page_size, cache_width), jnp.bfloat16),
            pltpu.VMEM((keys, width), jnp.bfloat16),
            pltpu.VMEM((H * query_rows, width), jnp.bfloat16),
            pltpu.SemaphoreType.DMA((page_count,)),
        ],
        compiler_params=pltpu.CompilerParams(vmem_limit_bytes=48 * 1024 * 1024),
        cost_estimate=pl.CostEstimate(
            flops=2 * H * query_rows * keys * (width + LATENT),
            bytes_accessed=16 * 1024 * 1024,
            transcendentals=H * query_rows * keys,
        ),
        name="attention",
    )(block_table, page_len, meta, queries, latent_pool, latent_up)


def project_kernel(groups, meta_ref, weight_ref, *refs):
    parts, outs = refs[:groups], refs[groups:]
    query_rows = outs[0].shape[0]
    width = outs[0].shape[1]
    heads_here = parts[0].shape[1] // VDIM
    col_index = meta_ref[2]
    mixed = []
    for j in range(heads_here):
        lanes = slice(j * VDIM, (j + 1) * VDIM)
        logs = []
        for part in parts:
            tail = part[query_rows:, lanes].astype(jnp.float32)
            line = tail[0:1] + tail[1:2] + tail[2:3]
            logs.append(jnp.transpose(jnp.broadcast_to(line, (LANES, query_rows))))
        top = functools.reduce(jnp.maximum, logs)
        scales = [jnp.exp2(v - top) for v in logs]
        total = functools.reduce(jnp.add, scales)
        value = functools.reduce(
            jnp.add, [s * part[:query_rows, lanes].astype(jnp.float32) for s, part in zip(scales, parts)]
        )
        mixed.append((value / total).astype(jnp.bfloat16))
    mixed = jnp.concatenate(mixed, axis=1)
    for step in range(groups):
        at = pl.multiple_of(lax.rem(col_index + step, groups) * width, width)
        columns = weight_ref[:, pl.ds(at, width)]
        outs[step][...] = jnp.dot(mixed, columns, preferred_element_type=jnp.float32).astype(
            jnp.bfloat16
        )


def project(parts, output_weight, meta, query_rows):
    groups = len(parts)
    vmem = pl.BlockSpec(memory_space=pltpu.VMEM)
    width = output_weight.shape[1] // groups
    return pl.pallas_call(
        functools.partial(project_kernel, groups),
        out_shape=[jax.ShapeDtypeStruct((query_rows, width), jnp.bfloat16)] * groups,
        in_specs=[pl.BlockSpec(memory_space=pltpu.SMEM)] + [vmem] * (1 + groups),
        out_specs=[vmem] * groups,
        compiler_params=pltpu.CompilerParams(vmem_limit_bytes=32 * 1024 * 1024),
        name="project",
    )(meta, output_weight, *parts)


def on_device(
    queries,
    latent_pool,
    block_table,
    page_len,
    group_offset,
    hidden,
    latent_up,
    output_weight,
    gate_weight,
    up_weight,
    down_weight,
):
    cols = lax.axis_size("col")
    chips = lax.axis_size("row") // 2
    col_index = lax.axis_index("col")
    row_index = lax.axis_index("row")
    chip_index = row_index // 2
    core_index = row_index % 2
    query_rows, model = hidden.shape
    keys_here = latent_pool.shape[0] * latent_pool.shape[1]
    depth, units = gate_weight.shape
    share = -(-units // (chips * LANES)) * LANES
    width = model // cols

    pad = chips * share - units
    gate_padded = jnp.pad(gate_weight, ((0, 0), (0, pad)))
    up_padded = jnp.pad(up_weight, ((0, 0), (0, pad)))
    down_padded = jnp.pad(down_weight, ((0, pad), (0, 0)))
    ins, downs = [], []
    for step in range(chips):
        at = (chip_index ^ step) * share
        gate_up = jnp.concatenate(
            [
                lax.dynamic_slice_in_dim(gate_padded, at, share, 1),
                lax.dynamic_slice_in_dim(up_padded, at, share, 1),
            ],
            axis=0,
        )
        down = lax.dynamic_slice_in_dim(down_padded, at, share, 0)
        ins.append(exchange(gate_up, "row", 2 * step) if step else gate_up)
        downs.append(exchange(down, "row", 2 * step) if step else down)
    ins = jnp.stack(ins)
    downs = jnp.stack(downs)
    ins = jnp.stack([ins, exchange(ins, "row", 1)])
    downs = jnp.stack([downs, exchange(downs, "row", 1)])
    order = jnp.arange(chips, dtype=jnp.int32) ^ chip_index
    cores = jnp.arange(2, dtype=jnp.int32) ^ core_index
    ins = ins[cores[None, :], order[:, None]].reshape(2 * chips, 2, depth, share)
    gate_all = ins[:, 0].reshape(model, share)
    up_all = ins[:, 1].reshape(model, share)
    downs = downs[cores[None, :], order[:, None]].reshape(2 * chips, share, depth)
    down_all = downs.transpose(1, 0, 2).reshape(share, model)

    meta = jnp.stack(
        [group_offset[0] + row_index * query_rows, col_index * keys_here, col_index]
    ).astype(jnp.int32)
    payloads = attention(queries, latent_pool, block_table, page_len, latent_up, meta, cols)
    parts = [payloads[0]] + [rotate(payloads[s], "col", s) for s in range(1, cols)]
    terms = project(parts, output_weight, meta, query_rows)
    here = lax.dynamic_slice_in_dim(hidden, col_index * width, width, 1).astype(jnp.float32)
    here = here + terms[0].astype(jnp.float32)
    for s in range(1, cols):
        here = here + rotate(terms[s], "col", s).astype(jnp.float32)
    here = here.astype(jnp.bfloat16)
    pieces = jnp.stack([here] + [rotate(here, "col", s) for s in range(1, cols)])
    col_order = (col_index - jnp.arange(cols, dtype=jnp.int32)) % cols
    attended = pieces[col_order].transpose(1, 0, 2).reshape(query_rows, model)

    wide = attended.astype(jnp.float32)
    mean_square = jnp.mean(wide * wide, axis=1, keepdims=True)
    normed = (wide * lax.rsqrt(mean_square + 1e-06)).astype(jnp.bfloat16)
    tokens = jnp.concatenate(
        [normed] + [exchange(normed, "row", 2 * s) for s in range(1, chips)], axis=0
    )
    gate_sum = jnp.dot(tokens, gate_all, preferred_element_type=jnp.float32)
    up_sum = jnp.dot(tokens, up_all, preferred_element_type=jnp.float32)
    activated = (jax.nn.silu(gate_sum) * up_sum).astype(jnp.bfloat16)
    out = jnp.dot(activated, down_all, preferred_element_type=jnp.float32).astype(jnp.bfloat16)
    out = out.reshape(chips, query_rows, model)
    summed = out[0].astype(jnp.float32)
    for s in range(1, chips):
        summed = summed + exchange(out[s], "row", 2 * s).astype(jnp.float32)

    def chunk(s):
        at = ((col_index + s) % cols) * width
        return lax.dynamic_slice_in_dim(summed, at, width, 1)

    total = here.astype(jnp.float32) + chunk(0)
    for s in range(1, cols):
        total = total + rotate(chunk(s).astype(jnp.bfloat16), "col", s).astype(jnp.float32)
    return (attended, total.astype(jnp.bfloat16))


def solution(mesh):
    placed = (
        P("row", None),
        P("col", None, None),
        P("col"),
        P("col"),
        P(),
        P("row", None),
        P(),
        P("col", None),
        P("row", "col"),
        P("row", "col"),
        P("col", "row"),
    )
    return jax.shard_map(
        on_device,
        mesh=mesh,
        in_specs=placed,
        out_specs=(P("row", None), P("row", "col")),
        check_vma=False,
    )
```

time: 492 us -> 210 us (0.43)
  waiting for transfers between devices: 251 us -> 85 us
  matrix products: 105 us -> 13.1 us
  loops' own time: 42.4 us -> 0 us
  starting transfers between devices: 4.63 us -> 36.6 us
  Pallas kernels: 0 us -> 22.8 us
  blocking collectives: 19.6 us -> 0 us
  between operations: 16.4 us -> 1.56 us
  other arithmetic: 14.1 us -> 21.3 us
  local copies, waits for them, and re-layouts: 36.8 us -> 29.6 us
    all_gather x3 -> x0, waiting for transfers between devices: 149 us -> none  [the longest x1 70.2 us: on_device(): lax.all_gather(down_weight, 'row', axis=1, tiled=True)]
    dot_general x51 -> x2, matrix products: 105 us -> 13.1 us  [the longest x1 8.46 us: on_device(): jnp.dot(activated, down_all, preferred_element_type=jnp.float32)]
    ppermute x0 -> x26, waiting for transfers between devices: none -> 85 us  [the longest x14 54.6 us: exchange(): return lax.ppermute(x, axis, [(i, i ^ step) for i in range(count)])]
    psum x1 -> x0, waiting for transfers between devices: 49.1 us -> none  [on_device(): projected = lax.psum(partial_value, 'col')]
    another operation x1 -> x0, loops' own time: 42.4 us -> none  [on_device(): lax.map(one_head, jnp.arange(H, dtype=jnp.int32))]
    ppermute x0 -> x26, starting transfers between devices: none -> 36.6 us  [the longest x12 21.7 us: rotate(): lax.ppermute(x, axis, [(i, (i + step) % count) for i in range(count)])]
    reduce_scatter x1 -> x0, waiting for transfers between devices: 27.3 us -> none  [on_device(): lax.psum_scatter(mlp_terms, 'col', scatter_dimension=1, tiled=True)]
    all_to_all x1 -> x0, waiting for transfers between devices: 23.4 us -> none  [on_device(): lax.all_to_all(head_out[None], 'col', split_axis=1, concat_axis=0, tiled=...]
  transfers between devices with their start and end apart: 6 -> 26, of which waited for: 6 -> 14; matrix products, arithmetic and copies ran while one was open for 2% -> 17% of each run, Pallas kernels for 0% -> 11%
where the time goes in v1:
time: 210 us
  waiting for transfers between devices  85 us (40%)
  starting transfers between devices  36.6 us (17%)
  local copies, waits for them, and re-layouts  29.6 us (14%)
  Pallas kernels  22.8 us (11%)
  other arithmetic  21.3 us (10%)
  matrix products  13.1 us (6%)
    ppermute x14, waiting for transfers between devices, exchange(): return lax.ppermute(x, axis, [(i, i ^ step) for i in range(count)])  54.6 us
    ppermute x12, waiting for transfers between devices, rotate(): lax.ppermute(x, axis, [(i, (i + step) % count) for i in range(count)])  30.3 us
    ppermute x12, starting transfers between devices, rotate(): lax.ppermute(x, axis, [(i, (i + step) % count) for i in range(count)])  21.7 us
    pallas_call x1, Pallas kernels, attention(): pl.pallas_call(functools.partial(attention_kernel, groups), out_shape=[pa...  21.3 us
    ppermute x14, starting transfers between devices, exchange(): return lax.ppermute(x, axis, [(i, i ^ step) for i in range(count)])  14.9 us
    another operation x2, other arithmetic, on_device(): ins = jnp.stack([ins, exchange(ins, 'row', 1)])  9.12 us
    dot_general x1, matrix products, on_device(): jnp.dot(activated, down_all, preferred_element_type=jnp.float32)  8.46 us
    gather x1, local copies, waits for them, and re-layouts, on_device(): ins[cores[None, :], order[:, None]].reshape(2 * chips, 2, depth, share)  6.38 us
  transfers between devices with their start and end apart: 26, of which 14 were waited for; matrix products, arithmetic and copies ran while one was open for 17% of the time, Pallas kernels for 11%

profile of v1, /device:TPU:0, one launch (start us, length us, event | category | flops | bytes accessed | tf_op | source)
XLA Modules:
  0.0 209.8 jit_solution(16566214658710848196)
XLA Ops:
  6.5 2.9 %collective-permute-start.12 = (bf16[512,768]{1,0:T(8,128)(2,1)}, bf16[512,768]{1,0:T(8,128)(2,1)S(1)}, u32[]{:S(2)}, u32[]{:S(2)}) collective-permute-start(bf16[512,768]{1,0:T(8,128)(2,1)} %pad_maximum_fusion.5), channel_id=1, source_target_pairs={{0,8},{4,12},{8,0},{12,4},{16,24},{20,28},{24,16},{28,20},{1,9},{5... | collective-permute-start | bytes 2359304 | tf_op jit(solution)/shard_map/ppermute | solution.py:27
  13.6 14.4 %collective-permute-done.12 = bf16[512,768]{1,0:T(8,128)(2,1)S(1)} collective-permute-done((bf16[512,768]{1,0:T(8,128)(2,1)}, bf16[512,768]{1,0:T(8,128)(2,1)S(1)}, u32[]{:S(2)}, u32[]{:S(2)}) %collective-permute-start.12) | collective-permute-done | bytes 786464 | tf_op jit(solution)/shard_map/ppermute | solution.py:27
  28.0 18.4 %collective-permute-done.13 = bf16[512,768]{1,0:T(8,128)(2,1)S(1)} collective-permute-done((bf16[512,768]{1,0:T(8,128)(2,1)}, bf16[512,768]{1,0:T(8,128)(2,1)S(1)}, u32[]{:S(2)}, u32[]{:S(2)}) %collective-permute-start.13) | collective-permute-done | bytes 786464 | tf_op jit(solution)/shard_map/ppermute | solution.py:27
  46.5 4.0 %fusion.15 = (bf16[1,4,512,768]{3,2,1,0:T(8,128)(2,1)}, bf16[4,512,768]{2,1,0:T(8,128)(2,1)}) fusion(bf16[1,512,768]{2,1,0:T(8,128)(2,1)} %bitcast.14, bf16[1,512,768]{2,1,0:T(8,128)(2,1)S(1)} %bitcast.50, bf16[1,512,768]{2,1,0:T(8,128)(2,1)S(1)} %bitcast.49, bf16[1,512,768]{2,1,0:T(8,128)(2,1)S(1)} %maximum_bitcast_fusion), kind=kLoop, calls=%fused_computation.59 | loop fusion | flops 4718592 | bytes 9437184 | tf_op jit(solution)/shard_map/stack | solution.py:234
  50.5 21.3 %attention.1 = (bf16[144,512]{1,0:T(8,128)(2,1)S(1)}, bf16[144,512]{1,0:T(8,128)(2,1)S(1)}, bf16[144,512]{1,0:T(8,128)(2,1)S(1)}, bf16[144,512]{1,0:T(8,128)(2,1)S(1)}) custom-call(s32[32]{0:T(128)S(1)} %copy-done.3, s32[32]{0:T(128)S(1)} %copy-done.4, s32[3]{0:T(128)S(1)} %pad_add_fusion.meta_ref, bf16[128,3072]{1,0:T(8,128)(2,1)S(1)} %copy-done.2, ...), custom_call_target="tpu_custom_call" | custom-call | flops 10737418240 | bytes 16777216 | tf_op jit(solution)/shard_map/attention/pallas_call | solution.py:125
  81.5 7.5 %collective-permute-done.1.refs_2_ = bf16[144,512]{1,0:T(8,128)(2,1)S(1)} collective-permute-done((bf16[144,512]{1,0:T(8,128)(2,1)S(1)}, bf16[144,512]{1,0:T(8,128)(2,1)S(1)}, u32[]{:S(2)}, u32[]{:S(2)}) %collective-permute-start.1) | collective-permute-done | bytes 147488 | tf_op jit(solution)/shard_map/ppermute | solution.py:32
  89.0 2.3 %collective-permute-start.2 = (bf16[144,512]{1,0:T(8,128)(2,1)S(1)}, bf16[144,512]{1,0:T(8,128)(2,1)S(1)}, u32[]{:S(2)}, u32[]{:S(2)}) collective-permute-start(bf16[144,512]{1,0:T(8,128)(2,1)S(1)} %get-tuple-element.13), channel_id=1, source_target_pairs={{0,3},{1,0},{2,1},{3,2},{4,7},{5,4},{6,5},{7,6},{8,11},{9,8},{10,9... | collective-permute-start | bytes 442376 | tf_op jit(solution)/shard_map/ppermute | solution.py:32
  91.4 3.5 %collective-permute-done.2.refs_3_ = bf16[144,512]{1,0:T(8,128)(2,1)S(1)} collective-permute-done((bf16[144,512]{1,0:T(8,128)(2,1)S(1)}, bf16[144,512]{1,0:T(8,128)(2,1)S(1)}, u32[]{:S(2)}, u32[]{:S(2)}) %collective-permute-start.2) | collective-permute-done | bytes 147488 | tf_op jit(solution)/shard_map/ppermute | solution.py:32
  96.3 4.6 %collective-permute-start.4 = (bf16[128,512]{1,0:T(8,128)(2,1)S(1)}, bf16[128,512]{1,0:T(8,128)(2,1)S(1)}, u32[]{:S(2)}, u32[]{:S(2)}) collective-permute-start(bf16[128,512]{1,0:T(8,128)(2,1)S(1)} %get-tuple-element.16), channel_id=1, source_target_pairs={{0,2},{1,3},{2,0},{3,1},{4,6},{5,7},{6,4},{7,5},{8,10},{9,11},{10,... | collective-permute-start | bytes 393224 | tf_op jit(solution)/shard_map/ppermute | solution.py:32
  100.9 2.6 %fusion.14 = (bf16[1,4,768,256]{3,2,1,0:T(8,128)(2,1)}, bf16[4,768,256]{2,1,0:T(8,128)(2,1)S(1)}) fusion(bf16[1,768,256]{2,1,0:T(8,128)(2,1)} %bitcast.23, bf16[1,768,256]{2,1,0:T(8,128)(2,1)} %bitcast.22, bf16[1,768,256]{2,1,0:T(8,128)(2,1)} %bitcast.21, bf16[1,768,256]{2,1,0:T(8,128)(2,1)S(1)} %get-tuple-element.41), kind=kLoop, calls=%fused_computation.58 | loop fusion | flops 2359296 | bytes 4718592 | tf_op jit(solution)/shard_map/stack | solution.py:235
  104.9 3.9 %collective-permute-done.4 = bf16[128,512]{1,0:T(8,128)(2,1)S(1)} collective-permute-done((bf16[128,512]{1,0:T(8,128)(2,1)S(1)}, bf16[128,512]{1,0:T(8,128)(2,1)S(1)}, u32[]{:S(2)}, u32[]{:S(2)}) %collective-permute-start.4) | collective-permute-done | bytes 131104 | tf_op jit(solution)/shard_map/ppermute | solution.py:32
  109.9 3.2 %collective-permute-start.6 = (bf16[128,512]{1,0:T(8,128)(2,1)S(1)}, bf16[128,512]{1,0:T(8,128)(2,1)S(1)}, u32[]{:S(2)}, u32[]{:S(2)}) collective-permute-start(bf16[128,512]{1,0:T(8,128)(2,1)S(1)} %add_convert_fusion.1), channel_id=1, source_target_pairs={{0,1},{1,2},{2,3},{3,0},{4,5},{5,6},{6,7},{7,4},{8,9},{9,10},{10,1... | collective-permute-start | bytes 393224 | tf_op jit(solution)/shard_map/ppermute | solution.py:32
  117.9 4.8 %collective-permute-done.7 = bf16[128,512]{1,0:T(8,128)(2,1)S(1)} collective-permute-done((bf16[128,512]{1,0:T(8,128)(2,1)S(1)}, bf16[128,512]{1,0:T(8,128)(2,1)S(1)}, u32[]{:S(2)}, u32[]{:S(2)}) %collective-permute-start.7) | collective-permute-done | bytes 131104 | tf_op jit(solution)/shard_map/ppermute | solution.py:32
  130.4 2.5 %gather_fusion.2 = bf16[8,768,256]{2,1,0:T(8,128)(2,1)} fusion(bf16[2,4,768,256]{3,2,1,0:T(8,128)(2,1)S(1)} %pad_maximum_fusion.2, s32[8]{0:T(128)S(1)} %reshape.115), kind=kCustom, calls=%fused_computation.2 | custom fusion | bytes 6291520 | tf_op jit(solution)/shard_map/gather | solution.py:241
  132.9 4.8 %copy.21 = bf16[768,8,256]{0,2,1:T(8,128)(2,1)} copy(bf16[768,8,256]{2,0,1:T(8,128)(2,1)} %bitcast.42) | data formatting | bytes 6291456 | tf_op jit(solution)/shard_map/transpose | solution.py:242
  137.7 5.1 %pad_maximum_fusion = bf16[2,4,512,768]{3,2,1,0:T(8,128)(2,1)} fusion(bf16[1,4,512,768]{3,2,1,0:T(8,128)(2,1)} %bitcast.16, bf16[1,4,512,768]{3,2,1,0:T(8,128)(2,1)S(1)} %copy-done.5), kind=kLoop, calls=%fused_computation.3 | loop fusion | flops 3145728 | bytes 12582912 | tf_op jit(solution)/shard_map/stack | solution.py:234
  142.9 6.4 %gather_fusion.1 = bf16[8,512,768]{2,1,0:T(8,128)(2,1)} fusion(bf16[2,4,512,768]{3,2,1,0:T(8,128)(2,1)} %pad_maximum_fusion, s32[8]{0:T(128)S(1)} %reshape.115), kind=kCustom, calls=%fused_computation.1 | custom fusion | bytes 12582976 | tf_op jit(solution)/shard_map/gather | solution.py:238
  149.3 5.0 %fusion.16 = (bf16[8,1,256,768]{3,2,1,0:T(8,128)(2,1)}, bf16[8,1,256,768]{3,2,1,0:T(8,128)(2,1)S(1)}) fusion(bf16[8,2,256,768]{3,2,1,0:T(8,128)(2,1)} %bitcast.41), kind=kLoop, calls=%fused_computation.60 | loop fusion | bytes 12582912 | tf_op jit(solution)/shard_map/slice | solution.py:239
  154.3 4.7 %fusion.2 = f32[512,768]{1,0:T(8,128)} fusion(bf16[2048,768]{1,0:T(8,128)(2,1)S(1)} %bitcast.47, bf16[128,2048]{0,1:T(8,128)(2,1)} %collective-permute-done.11, bf16[128,2048]{0,1:T(8,128)(2,1)} %collective-permute-done.10, bf16[128,2048]{0,1:T(8,128)(2,1)} %collective-permute-done.9, bf16[128,2048]{0,1:T(8,128)(2,1)} %multiply_convert_fusion.1), kind=kOutput, calls=%fused_computation.32 | convolution fusion | flops 1619001344 | bytes 6815744 | tf_op jit(solution)/shard_map/dot_general | solution.py:266
  159.0 8.5 %convolution_convert_fusion = bf16[512,2048]{1,0:T(8,128)(2,1)} fusion(bf16[768,2048]{0,1:T(8,128)(2,1)S(1)} %bitcast.45, f32[512,768]{1,0:T(8,128)} %fusion.2, bf16[2048,768]{1,0:T(8,128)(2,1)} %bitcast.46, bf16[128,2048]{0,1:T(8,128)(2,1)} %collective-permute-done.11, bf16[128,2048]{0,1:T(8,128)(2,1)} %collective-permute-done.10, ...), kind=kOutput, calls=%fused_computation.6 | convolution fusion | flops 3233021952 | bytes 12058624 | tf_op jit(solution)/shard_map/dot_general | solution.py:268
  173.2 11.6 %collective-permute-done.20 = bf16[128,2048]{1,0:T(8,128)(2,1)S(1)} collective-permute-done((bf16[128,2048]{1,0:T(8,128)(2,1)}, bf16[128,2048]{1,0:T(8,128)(2,1)S(1)}, u32[]{:S(2)}, u32[]{:S(2)}) %collective-permute-start.20) | collective-permute-done | bytes 524320 | tf_op jit(solution)/shard_map/ppermute | solution.py:27
  184.8 10.2 %collective-permute-done.22 = bf16[128,2048]{1,0:T(8,128)(2,1)S(1)} collective-permute-done((bf16[128,2048]{1,0:T(8,128)(2,1)S(1)}, bf16[128,2048]{1,0:T(8,128)(2,1)S(1)}, u32[]{:S(2)}, u32[]{:S(2)}) %collective-permute-start.22) | collective-permute-done | bytes 524320 | tf_op jit(solution)/shard_map/ppermute | solution.py:27
  196.4 3.4 %collective-permute-start.23 = (bf16[128,512]{1,0:T(8,128)(2,1)S(1)}, bf16[128,512]{1,0:T(8,128)(2,1)S(1)}, u32[]{:S(2)}, u32[]{:S(2)}) collective-permute-start(bf16[128,512]{1,0:T(8,128)(2,1)S(1)} %get-tuple-element.45), channel_id=1, source_target_pairs={{0,1},{1,2},{2,3},{3,0},{4,5},{5,6},{6,7},{7,4},{8,9},{9,10},{10,1... | collective-permute-start | bytes 393224 | tf_op jit(solution)/shard_map/ppermute | solution.py:32
  205.4 3.7 %collective-permute-done.24 = bf16[128,512]{1,0:T(8,128)(2,1)S(1)} collective-permute-done((bf16[128,512]{1,0:T(8,128)(2,1)S(1)}, bf16[128,512]{1,0:T(8,128)(2,1)S(1)}, u32[]{:S(2)}, u32[]{:S(2)}) %collective-permute-start.24) | collective-permute-done | bytes 131104 | tf_op jit(solution)/shard_map/ppermute | solution.py:32
  (89 shorter events, 49.0 us)
Async XLA Ops:
  6.5 21.5 %collective-permute-start.12 = (bf16[512,768]{1,0:T(8,128)(2,1)}, bf16[512,768]{1,0:T(8,128)(2,1)S(1)}, u32[]{:S(2)}, u32[]{:S(2)}) collective-permute-start(bf16[512,768]{1,0:T(8,128)(2,1)} %pad_maximum_fusion.5), channel_id=1, source_target_pairs={{0,8},{4,12},{8,0},{12,4},{16,24},{20,28},{24,16},{28,20},{1,9},{5... | collective-permute-start | bytes 2359304 | tf_op jit(solution)/shard_map/ppermute | solution.py:27
  10.4 36.1 %collective-permute-start.13 = (bf16[512,768]{1,0:T(8,128)(2,1)}, bf16[512,768]{1,0:T(8,128)(2,1)S(1)}, u32[]{:S(2)}, u32[]{:S(2)}) collective-permute-start(bf16[512,768]{1,0:T(8,128)(2,1)} %pad_maximum_fusion.6), channel_id=1, source_target_pairs={{0,16},{4,20},{8,24},{12,28},{16,0},{20,4},{24,8},{28,12},{1,17},{... | collective-permute-start | bytes 2359304 | tf_op jit(solution)/shard_map/ppermute | solution.py:27
  12.8 33.6 %collective-permute-start.14 = (bf16[512,768]{1,0:T(8,128)(2,1)}, bf16[512,768]{1,0:T(8,128)(2,1)}, u32[]{:S(2)}, u32[]{:S(2)}) collective-permute-start(bf16[512,768]{1,0:T(8,128)(2,1)} %pad_maximum_fusion.7), channel_id=1, source_target_pairs={{0,24},{4,28},{8,16},{12,20},{16,8},{20,12},{24,0},{28,4},{1,25},{... | collective-permute-start | bytes 2359304 | tf_op jit(solution)/shard_map/ppermute | solution.py:27
  50.5 87.3 %collective-permute-start.15 = (bf16[4,512,768]{2,1,0:T(8,128)(2,1)}, bf16[4,512,768]{2,1,0:T(8,128)(2,1)}, u32[]{:S(2)}, u32[]{:S(2)}) collective-permute-start(bf16[4,512,768]{2,1,0:T(8,128)(2,1)} %get-tuple-element.27), channel_id=1, source_target_pairs={{0,4},{4,0},{8,12},{12,8},{16,20},{20,16},{24,28},{28,24},{1,5},{5... | collective-permute-start | bytes 9437192 | tf_op jit(solution)/shard_map/ppermute | solution.py:27
  71.9 8.3 %collective-permute-start = (bf16[144,512]{1,0:T(8,128)(2,1)S(1)}, bf16[144,512]{1,0:T(8,128)(2,1)S(1)}, u32[]{:S(2)}, u32[]{:S(2)}) collective-permute-start(bf16[144,512]{1,0:T(8,128)(2,1)S(1)} %get-tuple-element.11), channel_id=1, source_target_pairs={{0,1},{1,2},{2,3},{3,0},{4,5},{5,6},{6,7},{7,4},{8,9},{9,10},{10,1... | collective-permute-start | bytes 442376 | tf_op jit(solution)/shard_map/ppermute | solution.py:32
  75.4 20.9 %collective-permute-start.16 = (bf16[768,256]{1,0:T(8,128)(2,1)}, bf16[768,256]{1,0:T(8,128)(2,1)}, u32[]{:S(2)}, u32[]{:S(2)}) collective-permute-start(bf16[768,256]{1,0:T(8,128)(2,1)} %get-tuple-element.42), channel_id=1, source_target_pairs={{0,8},{4,12},{8,0},{12,4},{16,24},{20,28},{24,16},{28,20},{1,9},{5... | collective-permute-start | bytes 1179656 | tf_op jit(solution)/shard_map/ppermute | solution.py:27
  76.0 24.9 %collective-permute-start.17 = (bf16[768,256]{1,0:T(8,128)(2,1)}, bf16[768,256]{1,0:T(8,128)(2,1)}, u32[]{:S(2)}, u32[]{:S(2)}) collective-permute-start(bf16[768,256]{1,0:T(8,128)(2,1)} %get-tuple-element.43), channel_id=1, source_target_pairs={{0,16},{4,20},{8,24},{12,28},{16,0},{20,4},{24,8},{28,12},{1,17},{... | collective-permute-start | bytes 1179656 | tf_op jit(solution)/shard_map/ppermute | solution.py:27
  77.5 23.4 %collective-permute-start.18 = (bf16[768,256]{1,0:T(8,128)(2,1)}, bf16[768,256]{1,0:T(8,128)(2,1)}, u32[]{:S(2)}, u32[]{:S(2)}) collective-permute-start(bf16[768,256]{1,0:T(8,128)(2,1)} %get-tuple-element.44), channel_id=1, source_target_pairs={{0,24},{4,28},{8,16},{12,20},{16,8},{20,12},{24,0},{28,4},{1,25},{... | collective-permute-start | bytes 1179656 | tf_op jit(solution)/shard_map/ppermute | solution.py:27
  80.1 8.9 %collective-permute-start.1 = (bf16[144,512]{1,0:T(8,128)(2,1)S(1)}, bf16[144,512]{1,0:T(8,128)(2,1)S(1)}, u32[]{:S(2)}, u32[]{:S(2)}) collective-permute-start(bf16[144,512]{1,0:T(8,128)(2,1)S(1)} %get-tuple-element.12), channel_id=1, source_target_pairs={{0,2},{1,3},{2,0},{3,1},{4,6},{5,7},{6,4},{7,5},{8,10},{9,11},{10,... | collective-permute-start | bytes 442376 | tf_op jit(solution)/shard_map/ppermute | solution.py:32
  96.3 8.6 %collective-permute-start.3 = (bf16[128,512]{1,0:T(8,128)(2,1)S(1)}, bf16[128,512]{1,0:T(8,128)(2,1)S(1)}, u32[]{:S(2)}, u32[]{:S(2)}) collective-permute-start(bf16[128,512]{1,0:T(8,128)(2,1)S(1)} %get-tuple-element.15), channel_id=1, source_target_pairs={{0,1},{1,2},{2,3},{3,0},{4,5},{5,6},{6,7},{7,4},{8,9},{9,10},{10,1... | collective-permute-start | bytes 393224 | tf_op jit(solution)/shard_map/ppermute | solution.py:32
  96.3 12.4 %collective-permute-start.4 = (bf16[128,512]{1,0:T(8,128)(2,1)S(1)}, bf16[128,512]{1,0:T(8,128)(2,1)S(1)}, u32[]{:S(2)}, u32[]{:S(2)}) collective-permute-start(bf16[128,512]{1,0:T(8,128)(2,1)S(1)} %get-tuple-element.16), channel_id=1, source_target_pairs={{0,2},{1,3},{2,0},{3,1},{4,6},{5,7},{6,4},{7,5},{8,10},{9,11},{10,... | collective-permute-start | bytes 393224 | tf_op jit(solution)/shard_map/ppermute | solution.py:32
  100.9 8.0 %collective-permute-start.5 = (bf16[128,512]{1,0:T(8,128)(2,1)S(1)}, bf16[128,512]{1,0:T(8,128)(2,1)S(1)}, u32[]{:S(2)}, u32[]{:S(2)}) collective-permute-start(bf16[128,512]{1,0:T(8,128)(2,1)S(1)} %get-tuple-element.17), channel_id=1, source_target_pairs={{0,3},{1,0},{2,1},{3,2},{4,7},{5,4},{6,5},{7,6},{8,11},{9,8},{10,9... | collective-permute-start | bytes 393224 | tf_op jit(solution)/shard_map/ppermute | solution.py:32
  103.5 24.7 %collective-permute-start.19 = (bf16[4,768,256]{2,1,0:T(8,128)(2,1)S(1)}, bf16[4,768,256]{2,1,0:T(8,128)(2,1)}, u32[]{:S(2)}, u32[]{:S(2)}) collective-permute-start(bf16[4,768,256]{2,1,0:T(8,128)(2,1)S(1)} %get-tuple-element.32), channel_id=1, source_target_pairs={{0,4},{4,0},{8,12},{12,8},{16,20},{20,16},{24,28},{28,24},{1,5},{5... | collective-permute-start | bytes 4718600 | tf_op jit(solution)/shard_map/ppermute | solution.py:27
  109.9 8.0 %collective-permute-start.6 = (bf16[128,512]{1,0:T(8,128)(2,1)S(1)}, bf16[128,512]{1,0:T(8,128)(2,1)S(1)}, u32[]{:S(2)}, u32[]{:S(2)}) collective-permute-start(bf16[128,512]{1,0:T(8,128)(2,1)S(1)} %add_convert_fusion.1), channel_id=1, source_target_pairs={{0,1},{1,2},{2,3},{3,0},{4,5},{5,6},{6,7},{7,4},{8,9},{9,10},{10,1... | collective-permute-start | bytes 393224 | tf_op jit(solution)/shard_map/ppermute | solution.py:32
  113.1 9.6 %collective-permute-start.7 = (bf16[128,512]{1,0:T(8,128)(2,1)S(1)}, bf16[128,512]{1,0:T(8,128)(2,1)S(1)}, u32[]{:S(2)}, u32[]{:S(2)}) collective-permute-start(bf16[128,512]{1,0:T(8,128)(2,1)S(1)} %add_convert_fusion.1), channel_id=1, source_target_pairs={{0,2},{1,3},{2,0},{3,1},{4,6},{5,7},{6,4},{7,5},{8,10},{9,11},{10,... | collective-permute-start | bytes 393224 | tf_op jit(solution)/shard_map/ppermute | solution.py:32
  113.3 9.4 %collective-permute-start.8 = (bf16[128,512]{1,0:T(8,128)(2,1)S(1)}, bf16[128,512]{1,0:T(8,128)(2,1)S(1)}, u32[]{:S(2)}, u32[]{:S(2)}) collective-permute-start(bf16[128,512]{1,0:T(8,128)(2,1)S(1)} %add_convert_fusion.1), channel_id=1, source_target_pairs={{0,3},{1,0},{2,1},{3,2},{4,7},{5,4},{6,5},{7,6},{8,11},{9,8},{10,9... | collective-permute-start | bytes 393224 | tf_op jit(solution)/shard_map/ppermute | solution.py:32
  124.8 29.5 %collective-permute-start.10 = (bf16[128,2048]{0,1:T(8,128)(2,1)}, bf16[128,2048]{0,1:T(8,128)(2,1)}, u32[]{:S(2)}, u32[]{:S(2)}) collective-permute-start(bf16[128,2048]{0,1:T(8,128)(2,1)} %multiply_convert_fusion.1), channel_id=1, source_target_pairs={{0,16},{4,20},{8,24},{12,28},{16,0},{20,4},{24,8},{28,12},{1,17},{... | collective-permute-start | bytes 1572872 | tf_op jit(solution)/shard_map/ppermute | solution.py:27
  126.3 28.0 %collective-permute-start.11 = (bf16[128,2048]{0,1:T(8,128)(2,1)}, bf16[128,2048]{0,1:T(8,128)(2,1)}, u32[]{:S(2)}, u32[]{:S(2)}) collective-permute-start(bf16[128,2048]{0,1:T(8,128)(2,1)} %multiply_convert_fusion.1), channel_id=1, source_target_pairs={{0,24},{4,28},{8,16},{12,20},{16,8},{20,12},{24,0},{28,4},{1,25},{... | collective-permute-start | bytes 1572872 | tf_op jit(solution)/shard_map/ppermute | solution.py:27
  126.6 27.7 %collective-permute-start.9 = (bf16[128,2048]{0,1:T(8,128)(2,1)}, bf16[128,2048]{0,1:T(8,128)(2,1)}, u32[]{:S(2)}, u32[]{:S(2)}) collective-permute-start(bf16[128,2048]{0,1:T(8,128)(2,1)} %multiply_convert_fusion.1), channel_id=1, source_target_pairs={{0,8},{4,12},{8,0},{12,4},{16,24},{20,28},{24,16},{28,20},{1,9},{5... | collective-permute-start | bytes 1572872 | tf_op jit(solution)/shard_map/ppermute | solution.py:27
  169.7 15.1 %collective-permute-start.20 = (bf16[128,2048]{1,0:T(8,128)(2,1)}, bf16[128,2048]{1,0:T(8,128)(2,1)S(1)}, u32[]{:S(2)}, u32[]{:S(2)}) collective-permute-start(bf16[128,2048]{1,0:T(8,128)(2,1)} %get-tuple-element.28), channel_id=1, source_target_pairs={{0,8},{4,12},{8,0},{12,4},{16,24},{20,28},{24,16},{28,20},{1,9},{5... | collective-permute-start | bytes 1572872 | tf_op jit(solution)/shard_map/ppermute | solution.py:27
  170.0 14.7 %collective-permute-start.21 = (bf16[128,2048]{1,0:T(8,128)(2,1)S(1)}, bf16[128,2048]{1,0:T(8,128)(2,1)S(1)}, u32[]{:S(2)}, u32[]{:S(2)}) collective-permute-start(bf16[128,2048]{1,0:T(8,128)(2,1)S(1)} %get-tuple-element.30), channel_id=1, source_target_pairs={{0,16},{4,20},{8,24},{12,28},{16,0},{20,4},{24,8},{28,12},{1,17},{... | collective-permute-start | bytes 1572872 | tf_op jit(solution)/shard_map/ppermute | solution.py:27
  171.5 23.4 %collective-permute-start.22 = (bf16[128,2048]{1,0:T(8,128)(2,1)S(1)}, bf16[128,2048]{1,0:T(8,128)(2,1)S(1)}, u32[]{:S(2)}, u32[]{:S(2)}) collective-permute-start(bf16[128,2048]{1,0:T(8,128)(2,1)S(1)} %get-tuple-element.29), channel_id=1, source_target_pairs={{0,24},{4,28},{8,16},{12,20},{16,8},{20,12},{24,0},{28,4},{1,25},{... | collective-permute-start | bytes 1572872 | tf_op jit(solution)/shard_map/ppermute | solution.py:27
  196.4 9.0 %collective-permute-start.23 = (bf16[128,512]{1,0:T(8,128)(2,1)S(1)}, bf16[128,512]{1,0:T(8,128)(2,1)S(1)}, u32[]{:S(2)}, u32[]{:S(2)}) collective-permute-start(bf16[128,512]{1,0:T(8,128)(2,1)S(1)} %get-tuple-element.45), channel_id=1, source_target_pairs={{0,1},{1,2},{2,3},{3,0},{4,5},{5,6},{6,7},{7,4},{8,9},{9,10},{10,1... | collective-permute-start | bytes 393224 | tf_op jit(solution)/shard_map/ppermute | solution.py:32
  199.8 9.3 %collective-permute-start.24 = (bf16[128,512]{1,0:T(8,128)(2,1)S(1)}, bf16[128,512]{1,0:T(8,128)(2,1)S(1)}, u32[]{:S(2)}, u32[]{:S(2)}) collective-permute-start(bf16[128,512]{1,0:T(8,128)(2,1)S(1)} %get-tuple-element.47), channel_id=1, source_target_pairs={{0,2},{1,3},{2,0},{3,1},{4,6},{5,7},{6,4},{7,5},{8,10},{9,11},{10,... | collective-permute-start | bytes 393224 | tf_op jit(solution)/shard_map/ppermute | solution.py:32
  (13 other events, 130.6 us)

commit v2 on v1

v2 whole, which is shorter than its diff:
```python
import functools
import math

import jax
import jax.numpy as jnp
from jax import lax
from jax.experimental import pallas as pl
from jax.experimental.pallas import tpu as pltpu
from jax.sharding import PartitionSpec as P

H = 16
NOPE = 128
ROPE = 64
VDIM = 128
LATENT = 512
QK = NOPE + ROPE
HEAD_UP = NOPE + VDIM
LANES = 128
TAIL = 16
HIDDEN_SCORE = -1e30
VMEM_LIMIT = 24 * 1024 * 1024
PREPARE_LIMIT = 12 * 1024 * 1024
SUBLANES = 16
META = 6
LOG2_SCALE = math.log2(math.e) / math.sqrt(QK)
NT = (((1,), (1,)), ((), ()))


def exchange(x, axis, step):
    count = lax.axis_size(axis)
    return lax.ppermute(x, axis, [(i, i ^ step) for i in range(count)])


def rotate(x, axis, step):
    count = lax.axis_size(axis)
    return lax.ppermute(x, axis, [(i, (i + step) % count) for i in range(count)])


def rows_of(ref, index, size):
    return ref[pl.ds(pl.multiple_of(index * size, size), size), :]


def prepare_kernel(
    chips, meta_ref, queries_hbm, pool_hbm, up_hbm, gate_hbm, unit_hbm, down_hbm, *refs
):
    q_ref, keys_ref, up_ref = refs[:3]
    shares, refs = refs[3 : 3 + chips], refs[3 + chips :]
    pages_ref, queries_ref, page_sem, share_sem, sem = refs
    page_count, page_size, _ = pages_ref.shape
    query_rows = queries_ref.shape[0]
    first_query = meta_ref[0]
    first_key = meta_ref[1]
    share = shares[0].shape[0] // 3
    table_at = META + chips
    len_at = table_at + page_count

    queries_copy = pltpu.make_async_copy(queries_hbm, queries_ref, sem.at[0])
    up_copy = pltpu.make_async_copy(up_hbm, up_ref, sem.at[1])
    page_copies = [
        pltpu.make_async_copy(pool_hbm.at[meta_ref[table_at + p]], pages_ref.at[p], page_sem.at[p])
        for p in range(page_count)
    ]
    share_copies = []
    for step in range(chips):
        rows = pl.ds(pl.multiple_of(meta_ref[META + step], SUBLANES), share)
        for i, source in enumerate((gate_hbm, unit_hbm, down_hbm)):
            target = shares[step].at[pl.ds(i * share, share), :]
            share_copies.append(
                pltpu.make_async_copy(source.at[rows, :], target, share_sem.at[3 * step + i])
            )
    for copy in page_copies + [queries_copy, up_copy] + share_copies:
        copy.start()

    slot = lax.broadcasted_iota(jnp.int32, (page_size, query_rows), 0)
    query_pos = first_query + lax.broadcasted_iota(jnp.int32, (page_size, query_rows), 1)
    for p in range(page_count):
        page_copies[p].wait()
        rows = pl.ds(p * page_size, page_size)
        page = pages_ref[p]
        keys_ref[rows, :LATENT] = page[:, :LATENT]
        keys_ref[rows, LATENT : LATENT + LANES] = jnp.concatenate(
            [page[:, LATENT:], jnp.zeros((page_size, LANES - ROPE), jnp.bfloat16)], axis=1
        )
        seen = (slot < meta_ref[len_at + p]) & (first_key + p * page_size + slot <= query_pos)
        keys_ref[rows, LATENT + LANES :] = jnp.where(seen, 0.0, HIDDEN_SCORE).astype(jnp.bfloat16)

    eye = (
        lax.broadcasted_iota(jnp.int32, (query_rows, query_rows), 0)
        == lax.broadcasted_iota(jnp.int32, (query_rows, query_rows), 1)
    ).astype(jnp.bfloat16)
    queries_copy.wait()
    up_copy.wait()
    for h in range(H):
        rows = pl.ds(h * query_rows, query_rows)
        q_nope = queries_ref[:, h * QK : h * QK + NOPE]
        up_k = up_ref[:, h * HEAD_UP : h * HEAD_UP + NOPE]
        absorbed = lax.dot_general(q_nope, up_k, NT, preferred_element_type=jnp.float32)
        q_ref[rows, :LATENT] = absorbed.astype(jnp.bfloat16)
        q_rope = queries_ref[:, h * QK + NOPE : (h + 1) * QK]
        q_ref[rows, LATENT : LATENT + LANES] = jnp.concatenate(
            [q_rope, jnp.zeros((query_rows, LANES - ROPE), jnp.bfloat16)], axis=1
        )
        q_ref[rows, LATENT + LANES :] = eye
    for copy in share_copies:
        copy.wait()


def prepare(queries, latent_pool, latent_up, by_unit, meta, chips, share):
    query_rows = queries.shape[0]
    page_count, page_size, cache_width = latent_pool.shape
    keys = page_count * page_size
    width = LATENT + LANES + query_rows
    vmem = pl.BlockSpec(memory_space=pltpu.VMEM)
    smem = pl.BlockSpec(memory_space=pltpu.SMEM)
    hbm = pl.BlockSpec(memory_space=pltpu.HBM)
    sources = (queries, latent_pool, latent_up, *by_unit)
    out = pl.pallas_call(
        functools.partial(prepare_kernel, chips),
        out_shape=[
            pltpu.VMEM((H * query_rows, width), jnp.bfloat16),
            pltpu.VMEM((keys, width), jnp.bfloat16),
            pltpu.VMEM(latent_up.shape, jnp.bfloat16),
        ]
        + [pltpu.VMEM((3 * share, by_unit[0].shape[1]), jnp.bfloat16)] * chips,
        in_specs=[smem] + [hbm] * 6,
        out_specs=[vmem] * (3 + chips),
        scratch_shapes=[
            pltpu.VMEM((page_count, page_size, cache_width), jnp.bfloat16),
            pltpu.VMEM(queries.shape, jnp.bfloat16),
            pltpu.SemaphoreType.DMA((page_count,)),
            pltpu.SemaphoreType.DMA((3 * chips,)),
            pltpu.SemaphoreType.DMA((2,)),
        ],
        compiler_params=pltpu.CompilerParams(vmem_limit_bytes=PREPARE_LIMIT),
        cost_estimate=pl.CostEstimate(flops=0, bytes_accessed=0, transcendentals=0),
        name="prepare",
    )(meta, *[pltpu.with_memory_space_constraint(x, pltpu.HBM) for x in sources])
    return out[0], out[1], out[2], out[3:]


def attend_kernel(step, groups, meta_ref, q_ref, keys_ref, up_ref, out_ref):
    heads_here = H // groups
    query_rows = q_ref.shape[0] // H
    group = lax.rem(meta_ref[2] + step, groups)
    q_rows = rows_of(q_ref, group, heads_here * query_rows)
    scores = lax.dot_general(q_rows, keys_ref[...], NT, preferred_element_type=jnp.float32)
    row_max = jnp.max(scores, axis=1, keepdims=True)
    weights = jnp.exp2((scores - row_max) * LOG2_SCALE)
    totals = jnp.sum(weights, axis=1, keepdims=True)
    context = jnp.dot(
        weights.astype(jnp.bfloat16), keys_ref[:, :LATENT], preferred_element_type=jnp.float32
    )
    context = (context / totals).astype(jnp.bfloat16)
    log_sum = row_max * LOG2_SCALE + jnp.log2(totals)
    tail = []
    for j in range(heads_here):
        own = slice(j * query_rows, (j + 1) * query_rows)
        at = pl.multiple_of((group * heads_here + j) * HEAD_UP + NOPE, LANES)
        up_v = up_ref[:, pl.ds(at, VDIM)]
        mixed = jnp.dot(context[own], up_v, preferred_element_type=jnp.float32)
        out_ref[:query_rows, j * VDIM : (j + 1) * VDIM] = mixed.astype(jnp.bfloat16)
        wide = jnp.broadcast_to(log_sum[own], (query_rows, LANES))
        tail.append(jnp.transpose(wide)[:1])
    tail = jnp.concatenate(tail, axis=1)
    high = tail.astype(jnp.bfloat16)
    rest = tail - high.astype(jnp.float32)
    middle = rest.astype(jnp.bfloat16)
    low = (rest - middle.astype(jnp.float32)).astype(jnp.bfloat16)
    parts = [high.astype(jnp.float32), middle.astype(jnp.float32), low.astype(jnp.float32)]
    parts.append(jnp.zeros((TAIL - 3, tail.shape[1]), jnp.float32))
    out_ref[query_rows:, :] = jnp.concatenate(parts, axis=0).astype(jnp.bfloat16)


def attend(step, groups, meta, q, keys, latent_up):
    query_rows = q.shape[0] // H
    heads_here = H // groups
    vmem = pl.BlockSpec(memory_space=pltpu.VMEM)
    return pl.pallas_call(
        functools.partial(attend_kernel, step, groups),
        out_shape=jax.ShapeDtypeStruct((query_rows + TAIL, heads_here * VDIM), jnp.bfloat16),
        in_specs=[pl.BlockSpec(memory_space=pltpu.SMEM), vmem, vmem, vmem],
        out_specs=vmem,
        compiler_params=pltpu.CompilerParams(vmem_limit_bytes=VMEM_LIMIT),
        cost_estimate=pl.CostEstimate(
            flops=2 * heads_here * query_rows * keys.shape[0] * (keys.shape[1] + LATENT),
            bytes_accessed=4 * 1024 * 1024,
            transcendentals=heads_here * query_rows * keys.shape[0],
        ),
        name="attend",
    )(meta, q, keys, latent_up)


def project_kernel(groups, meta_ref, weight_ref, *refs):
    parts, outs = refs[:groups], refs[groups:]
    query_rows = outs[0].shape[0]
    width = outs[0].shape[1]
    heads_here = parts[0].shape[1] // VDIM
    col_index = meta_ref[2]
    mixed = []
    for j in range(heads_here):
        lanes = slice(j * VDIM, (j + 1) * VDIM)
        logs = []
        for part in parts:
            tail = part[query_rows:, lanes].astype(jnp.float32)
            line = tail[0:1] + tail[1:2] + tail[2:3]
            logs.append(jnp.transpose(jnp.broadcast_to(line, (LANES, query_rows))))
        top = functools.reduce(jnp.maximum, logs)
        scales = [jnp.exp2(v - top) for v in logs]
        total = functools.reduce(jnp.add, scales)
        value = functools.reduce(
            jnp.add, [s * part[:query_rows, lanes].astype(jnp.float32) for s, part in zip(scales, parts)]
        )
        mixed.append((value / total).astype(jnp.bfloat16))
    mixed = jnp.concatenate(mixed, axis=1)
    for step in range(groups):
        at = pl.multiple_of(lax.rem(col_index + step, groups) * width, width)
        columns = weight_ref[:, pl.ds(at, width)]
        outs[step][...] = jnp.dot(mixed, columns, preferred_element_type=jnp.float32).astype(
            jnp.bfloat16
        )


def project(parts, output_weight, meta, query_rows):
    groups = len(parts)
    vmem = pl.BlockSpec(memory_space=pltpu.VMEM)
    width = output_weight.shape[1] // groups
    return pl.pallas_call(
        functools.partial(project_kernel, groups),
        out_shape=[jax.ShapeDtypeStruct((query_rows, width), jnp.bfloat16)] * groups,
        in_specs=[pl.BlockSpec(memory_space=pltpu.SMEM)] + [vmem] * (1 + groups),
        out_specs=[vmem] * groups,
        compiler_params=pltpu.CompilerParams(vmem_limit_bytes=32 * 1024 * 1024),
        name="project",
    )(meta, output_weight, *parts)


def assemble_kernel(chips, meta_ref, *refs):
    blocks, (out_ref, sem) = refs[: 2 * chips], refs[2 * chips :]
    depth = blocks[0].shape[1]
    chip_index, core_index = meta_ref[3], meta_ref[4]
    copies = []
    for core_step in range(2):
        for step in range(chips):
            place = 2 * (chip_index ^ step) + (core_index ^ core_step)
            lanes = pl.ds(pl.multiple_of(place * depth, depth), depth)
            number = core_step * chips + step
            copies.append(
                pltpu.make_async_copy(blocks[number], out_ref.at[:, lanes], sem.at[number])
            )
    for copy in copies:
        copy.start()
    for copy in copies:
        copy.wait()


def assemble(blocks, meta):
    rows, depth = blocks[0].shape
    anywhere = pl.BlockSpec(memory_space=pl.ANY)
    return pl.pallas_call(
        functools.partial(assemble_kernel, len(blocks) // 2),
        out_shape=jax.ShapeDtypeStruct((rows, depth * len(blocks)), blocks[0].dtype),
        in_specs=[pl.BlockSpec(memory_space=pltpu.SMEM)] + [anywhere] * len(blocks),
        out_specs=pl.BlockSpec(memory_space=pltpu.VMEM),
        scratch_shapes=[pltpu.SemaphoreType.DMA((len(blocks),))],
        compiler_params=pltpu.CompilerParams(vmem_limit_bytes=VMEM_LIMIT),
        cost_estimate=pl.CostEstimate(
            flops=0, bytes_accessed=4 * rows * depth * len(blocks), transcendentals=0
        ),
        name="assemble",
    )(meta, *blocks)


def feed_kernel(groups, chips, order, meta_ref, weights_ref, *refs):
    tokens, refs = refs[:groups], refs[groups:]
    keeps, sends, (tokens_ref, active_ref) = refs[:groups], refs[groups : 2 * groups], refs[2 * groups :]
    width = tokens[0].shape[1]
    rows, model = tokens_ref.shape
    share = active_ref.shape[1]
    query_rows = rows // chips
    col_index = meta_ref[2]
    squares = jnp.zeros((rows, 1), jnp.float32)
    for s in range(groups):
        piece = tokens[s][...]
        at = pl.multiple_of(lax.rem(col_index + groups - s, groups) * width, width)
        tokens_ref[:, pl.ds(at, width)] = piece
        wide = piece.astype(jnp.float32)
        squares = squares + jnp.sum(wide * wide, axis=1, keepdims=True)
    scale = lax.rsqrt(squares / model + 1e-06)
    gate = lax.dot_general(
        tokens_ref[...], weights_ref[:share, :], NT, preferred_element_type=jnp.float32
    )
    up = lax.dot_general(
        tokens_ref[...], weights_ref[share : 2 * share, :], NT, preferred_element_type=jnp.float32
    )
    gate = gate * scale
    active = gate / (1.0 + jnp.exp(-gate)) * (up * scale)
    unit = lax.broadcasted_iota(jnp.int32, active.shape, 1)
    active_ref[...] = jnp.where(unit < meta_ref[5], 0.0, active).astype(jnp.bfloat16)
    for s in range(groups):
        at = pl.multiple_of(lax.rem(col_index + s, groups) * width, width)
        out = jnp.dot(
            active_ref[...],
            weights_ref[2 * share :, pl.ds(at, width)],
            preferred_element_type=jnp.float32,
        ).astype(jnp.bfloat16)
        kept, sent = halves(order[s], chips)
        for ref, steps in ((keeps[s], kept), (sends[s], sent)):
            for i, step in enumerate(steps):
                ref[i * query_rows : (i + 1) * query_rows, :] = out[
                    step * query_rows : (step + 1) * query_rows
                ]


def halves(bits, chips):
    if not bits:
        return [0], []
    return [s for s in range(chips) if not s & bits[0]], [s for s in range(chips) if s & bits[0]]


def feed(weights, tokens, meta, chips, order):
    groups = len(tokens)
    rows, width = tokens[0].shape
    share = weights.shape[0] // 3
    vmem = pl.BlockSpec(memory_space=pltpu.VMEM)
    kept, sent = halves(order[0], chips)
    query_rows = rows // chips
    shapes = [
        jax.ShapeDtypeStruct((max(len(steps), 1) * query_rows, width), jnp.bfloat16)
        for steps in (kept, sent)
    ]
    return pl.pallas_call(
        functools.partial(feed_kernel, groups, chips, order),
        out_shape=[shapes[0]] * groups + [shapes[1]] * groups,
        in_specs=[pl.BlockSpec(memory_space=pltpu.SMEM)] + [vmem] * (1 + groups),
        out_specs=[vmem] * (2 * groups),
        scratch_shapes=[
            pltpu.VMEM((rows, width * groups), jnp.bfloat16),
            pltpu.VMEM((rows, share), jnp.bfloat16),
        ],
        compiler_params=pltpu.CompilerParams(vmem_limit_bytes=VMEM_LIMIT),
        cost_estimate=pl.CostEstimate(
            flops=6 * rows * width * groups * share,
            bytes_accessed=6 * share * width * groups,
            transcendentals=rows * share,
        ),
        name="feed",
    )(meta, weights, *tokens)


def gather_rows(block, bits):
    query_rows = block.shape[0]
    steps = [0]
    for bit in bits:
        block = jnp.concatenate([block, exchange(block, "row", 2 * bit)], axis=0)
        steps = steps + [s ^ bit for s in steps]
    pieces = [block[steps.index(s) * query_rows :][:query_rows] for s in range(len(steps))]
    return block if steps == sorted(steps) else jnp.concatenate(pieces, axis=0)


def sum_rows(kept, sent, bits, query_rows):
    for i, bit in enumerate(bits):
        kept = kept.astype(jnp.float32) + exchange(sent, "row", 2 * bit).astype(jnp.float32)
        if i + 1 == len(bits):
            break
        left = [s for s in range(1 << len(bits)) if not any(s & b for b in bits[: i + 1])]
        pick = [
            [n for n, s in enumerate(left) if bool(s & bits[i + 1]) == away] for away in (False, True)
        ]
        kept, sent = [
            jnp.concatenate([kept[n * query_rows : (n + 1) * query_rows] for n in rows], axis=0)
            for rows in pick
        ]
        sent = sent.astype(jnp.bfloat16)
    return kept.astype(jnp.float32)


def on_device(
    queries,
    latent_pool,
    block_table,
    page_len,
    group_offset,
    hidden,
    latent_up,
    output_weight,
    gate_weight,
    up_weight,
    down_weight,
):
    cols = lax.axis_size("col")
    chips = lax.axis_size("row") // 2
    col_index = lax.axis_index("col")
    row_index = lax.axis_index("row")
    chip_index = row_index // 2
    core_index = row_index % 2
    query_rows, model = hidden.shape
    keys_here = latent_pool.shape[0] * latent_pool.shape[1]
    depth, units = gate_weight.shape
    by_unit = (gate_weight.T, up_weight.T, down_weight)
    if units % SUBLANES:
        by_unit = [jnp.pad(w, ((0, -units % SUBLANES), (0, 0))) for w in by_unit]
        units = by_unit[0].shape[0]
    share = -(-units // (chips * SUBLANES)) * SUBLANES
    width = model // cols

    def start_of(chip):
        return jnp.minimum(chip * share, units - share)

    meta = jnp.stack(
        [
            group_offset[0] + row_index * query_rows,
            col_index * keys_here,
            col_index,
            chip_index,
            core_index,
            chip_index * share - start_of(chip_index),
        ]
        + [start_of(chip_index ^ step) for step in range(chips)]
    ).astype(jnp.int32)
    meta = jnp.concatenate([meta, block_table, page_len])
    q, keys, up_here, shares = prepare(
        queries, latent_pool, latent_up, by_unit, meta, chips, share
    )
    early = range(1, chips // 2 + 1)
    late = range(chips // 2 + 1, chips)
    blocks = {s: exchange(shares[s], "row", 2 * s) for s in early}
    swapped = {0: exchange(shares[0], "row", 1)}

    payloads = [attend(s, cols, meta, q, keys, up_here) for s in range(cols)]
    parts = [payloads[0]] + [rotate(payloads[s], "col", s) for s in range(1, cols)]
    parts, blocks, swapped, later = lax.optimization_barrier(
        (parts, blocks, swapped, [shares[s] for s in late])
    )
    for s, share_out in zip(late, later):
        blocks[s] = exchange(share_out, "row", 2 * s)
    terms = project(parts, output_weight, meta, query_rows)
    for s in early:
        swapped[s] = exchange(blocks[s], "row", 1)
    here = lax.dynamic_slice_in_dim(hidden, col_index * width, width, 1).astype(jnp.float32)
    here = here + terms[0].astype(jnp.float32)
    for s in range(1, cols):
        here = here + rotate(terms[s], "col", s).astype(jnp.float32)
    here = here.astype(jnp.bfloat16)
    here, swapped = lax.optimization_barrier((here, swapped))
    for s in late:
        swapped[s] = exchange(blocks[s], "row", 1)
    blocks[0] = shares[0]
    blocks = [blocks[s] for s in range(chips)] + [swapped[s] for s in range(chips)]
    pieces = [here] + [rotate(here, "col", s) for s in range(1, cols)]
    attended = jnp.zeros((query_rows, model), jnp.bfloat16)
    for s in range(cols):
        at = ((col_index + cols - s) % cols) * width
        attended = lax.dynamic_update_slice_in_dim(attended, pieces[s], at, 1)

    rising = [1 << i for i in range(chips.bit_length() - 1)]
    order = [rising if s % 2 == 0 else rising[::-1] for s in range(cols)]
    tokens = [gather_rows(pieces[s], order[s]) for s in range(cols)]
    out = feed(assemble(blocks, meta), tokens, meta, chips, order)
    total = here.astype(jnp.float32)
    for s in list(range(1, cols)) + [0]:
        term = sum_rows(out[s], out[cols + s], order[s], query_rows)
        if s:
            term = rotate(term.astype(jnp.bfloat16), "col", s).astype(jnp.float32)
        total = total + term
    return (attended, total.astype(jnp.bfloat16))


def solution(mesh):
    placed = (
        P("row", None),
        P("col", None, None),
        P("col"),
        P("col"),
        P(),
        P("row", None),
        P(),
        P("col", None),
        P("row", "col"),
        P("row", "col"),
        P("col", "row"),
    )
    return jax.shard_map(
        on_device,
        mesh=mesh,
        in_specs=placed,
        out_specs=(P("row", None), P("row", "col")),
        check_vma=False,
    )
```

time: 210 us -> 127 us (0.60)
  waiting for transfers between devices: 85 us -> 34.5 us
  local copies, waits for them, and re-layouts: 29.6 us -> 1.97 us
  other arithmetic: 21.3 us -> 2.55 us
  starting transfers between devices: 36.6 us -> 51.2 us
  matrix products: 13.1 us -> 0 us
  Pallas kernels: 22.8 us -> 35.1 us
    ppermute x14 -> x23, waiting for transfers between devices: 54.6 us -> 15.2 us  [exchange(): return lax.ppermute(x, axis, [(i, i ^ step) for i in range(count)])]
    another operation x7 -> x0, other arithmetic: 14.1 us -> none  [the longest x2 9.12 us: on_device(): ins = jnp.stack([ins, exchange(ins, 'row', 1)])]
    dot_general x2 -> x0, matrix products: 13.1 us -> none  [the longest x1 8.46 us: on_device(): jnp.dot(activated, down_all, preferred_element_type=jnp.float32)]
    pallas_call x1 -> x7, Pallas kernels: 21.3 us -> 33.1 us  [the longest x4 16.7 us: attend(): pl.pallas_call(functools.partial(attend_kernel, step, groups), out_shape=...]
    ppermute x12, waiting for transfers between devices: 30.3 us -> 19.3 us  [rotate(): lax.ppermute(x, axis, [(i, (i + step) % count) for i in range(count)])]
    gather x3 -> x0, local copies, waits for them, and re-layouts: 9.42 us -> none  [the longest x1 6.38 us: on_device(): ins[cores[None, :], order[:, None]].reshape(2 * chips, 2, depth, share)]
    ppermute x14 -> x23, starting transfers between devices: 14.9 us -> 24.1 us  [exchange(): return lax.ppermute(x, axis, [(i, i ^ step) for i in range(count)])]
    slice x2 -> x6, local copies, waits for them, and re-layouts: 7.27 us -> 0.11 us  [the longest x4 0.08 us: sum_rows(): kept[n * query_rows:(n + 1) * query_rows]]
  transfers between devices with their start and end apart: 26 -> 35, of which waited for: 14 -> 13; matrix products, arithmetic and copies ran while one was open for 17% -> 2% of each run, Pallas kernels for 11% -> 15%
where the time goes in v2:
time: 127 us
  starting transfers between devices  51.2 us (40%)
  Pallas kernels  35.1 us (28%)
  waiting for transfers between devices  34.5 us (27%)
  other arithmetic  2.55 us (2%)
  local copies, waits for them, and re-layouts  1.97 us (2%)
  between operations  1.68 us (1%)
    ppermute x12, starting transfers between devices, rotate(): lax.ppermute(x, axis, [(i, (i + step) % count) for i in range(count)])  27.1 us
    ppermute x23, starting transfers between devices, exchange(): return lax.ppermute(x, axis, [(i, i ^ step) for i in range(count)])  24.1 us
    ppermute x12, waiting for transfers between devices, rotate(): lax.ppermute(x, axis, [(i, (i + step) % count) for i in range(count)])  19.3 us
    pallas_call x4, Pallas kernels, attend(): pl.pallas_call(functools.partial(attend_kernel, step, groups), out_shape=...  16.7 us
    ppermute x23, waiting for transfers between devices, exchange(): return lax.ppermute(x, axis, [(i, i ^ step) for i in range(count)])  15.2 us
    pallas_call x1, Pallas kernels, prepare(): pl.pallas_call(functools.partial(prepare_kernel, chips), out_shape=[pltpu...  7.45 us
    pallas_call x1, Pallas kernels, feed(): pl.pallas_call(functools.partial(feed_kernel, groups, chips, order), out_...  5.99 us
    pallas_call x1, Pallas kernels, assemble(): pl.pallas_call(functools.partial(assemble_kernel, len(blocks) // 2), out_...  2.98 us
  transfers between devices with their start and end apart: 35, of which 13 were waited for; matrix products, arithmetic and copies ran while one was open for 2% of the time, Pallas kernels for 15%

profile of v2, /device:TPU:0, one launch (start us, length us, event | category | flops | bytes accessed | tf_op | source)
XLA Modules:
  0.0 127.1 jit_solution(9507862277981988411)
XLA Ops:
  2.1 7.5 %prepare.1 = (bf16[2048,768]{1,0:T(8,128)(2,1)S(1)}, bf16[2048,768]{1,0:T(8,128)(2,1)S(1)}, bf16[512,4096]{1,0:T(8,128)(2,1)S(1)}, bf16[2064,256]{1,0:T(8,128)(2...) custom-call(s32[74]{0:T(128)S(1)} %concatenate.35.meta_ref, ...), custom_call_target="tpu_custom_call" | custom-call | tf_op jit(solution)/shard_map/prepare/pallas_call | solution.py:117
  9.5 3.0 %collective-permute-start.3 = (bf16[2064,256]{1,0:T(8,128)(2,1)S(1)}, bf16[2064,256]{1,0:T(8,128)(2,1)S(1)}, u32[]{:S(2)}, u32[]{:S(2)}) collective-permute-start(bf16[2064,256]{1,0:T(8,128)(2,1)S(1)} %get-tuple-element.36), channel_id=1, source_target_pairs={{0,8},{4,12},{8,0},{12,4},{16,24},{20,28},{24,16},{28,20},{1,9},{5... | collective-permute-start | bytes 3170312 | tf_op jit(solution)/shard_map/ppermute | solution.py:31
  14.0 4.2 %attend.5 = bf16[144,512]{1,0:T(8,128)(2,1)S(1)} custom-call(s32[74]{0:T(128)S(1)} %concatenate.35.meta_ref, bf16[2048,768]{1,0:T(8,128)(2,1)S(1)} %get-tuple-element.33.q_ref, bf16[2048,768]{1,0:T(8,128)(2,1)S(1)} %get-tuple-element.34.keys_ref, bf16[512,4096]{1,0:T(8,128)(2,1)S(1)} %get-tuple-element.35.up_ref), custom_call_target="tpu_custom_call" | custom-call | flops 2684354560 | bytes 4194304 | tf_op jit(solution)/shard_map/attend/pallas_call | solution.py:178
  18.2 1.6 %collective-permute-start = (bf16[144,512]{1,0:T(8,128)(2,1)S(1)}, bf16[144,512]{1,0:T(8,128)(2,1)S(1)}, u32[]{:S(2)}, u32[]{:S(2)}) collective-permute-start(bf16[144,512]{1,0:T(8,128)(2,1)S(1)} %attend.5), channel_id=1, source_target_pairs={{0,1},{1,2},{2,3},{3,0},{4,5},{5,6},{6,7},{7,4},{8,9},{9,10},{10,1... | collective-permute-start | bytes 442376 | tf_op jit(solution)/shard_map/ppermute | solution.py:36
  19.9 4.2 %attend.6 = bf16[144,512]{1,0:T(8,128)(2,1)S(1)} custom-call(s32[74]{0:T(128)S(1)} %concatenate.35.meta_ref, bf16[2048,768]{1,0:T(8,128)(2,1)S(1)} %get-tuple-element.33.q_ref, bf16[2048,768]{1,0:T(8,128)(2,1)S(1)} %get-tuple-element.34.keys_ref, bf16[512,4096]{1,0:T(8,128)(2,1)S(1)} %get-tuple-element.35.up_ref), custom_call_target="tpu_custom_call" | custom-call | flops 2684354560 | bytes 4194304 | tf_op jit(solution)/shard_map/attend/pallas_call | solution.py:178
  24.0 2.6 %collective-permute-start.1 = (bf16[144,512]{1,0:T(8,128)(2,1)S(1)}, bf16[144,512]{1,0:T(8,128)(2,1)S(1)}, u32[]{:S(2)}, u32[]{:S(2)}) collective-permute-start(bf16[144,512]{1,0:T(8,128)(2,1)S(1)} %attend.6), channel_id=1, source_target_pairs={{0,2},{1,3},{2,0},{3,1},{4,6},{5,7},{6,4},{7,5},{8,10},{9,11},{10,... | collective-permute-start | bytes 442376 | tf_op jit(solution)/shard_map/ppermute | solution.py:36
  26.7 4.2 %attend.7 = bf16[144,512]{1,0:T(8,128)(2,1)S(1)} custom-call(s32[74]{0:T(128)S(1)} %concatenate.35.meta_ref, bf16[2048,768]{1,0:T(8,128)(2,1)S(1)} %get-tuple-element.33.q_ref, bf16[2048,768]{1,0:T(8,128)(2,1)S(1)} %get-tuple-element.34.keys_ref, bf16[512,4096]{1,0:T(8,128)(2,1)S(1)} %get-tuple-element.35.up_ref), custom_call_target="tpu_custom_call" | custom-call | flops 2684354560 | bytes 4194304 | tf_op jit(solution)/shard_map/attend/pallas_call | solution.py:178
  30.9 1.6 %collective-permute-start.2 = (bf16[144,512]{1,0:T(8,128)(2,1)S(1)}, bf16[144,512]{1,0:T(8,128)(2,1)S(1)}, u32[]{:S(2)}, u32[]{:S(2)}) collective-permute-start(bf16[144,512]{1,0:T(8,128)(2,1)S(1)} %attend.7), channel_id=1, source_target_pairs={{0,3},{1,0},{2,1},{3,2},{4,7},{5,4},{6,5},{7,6},{8,11},{9,8},{10,9... | collective-permute-start | bytes 442376 | tf_op jit(solution)/shard_map/ppermute | solution.py:36
  32.5 4.2 %attend.4.refs_0_ = bf16[144,512]{1,0:T(8,128)(2,1)S(1)} custom-call(s32[74]{0:T(128)S(1)} %concatenate.35.meta_ref, bf16[2048,768]{1,0:T(8,128)(2,1)S(1)} %get-tuple-element.33.q_ref, bf16[2048,768]{1,0:T(8,128)(2,1)S(1)} %get-tuple-element.34.keys_ref, bf16[512,4096]{1,0:T(8,128)(2,1)S(1)} %get-tuple-element.35.up_ref), custom_call_target="tpu_custom_call" | custom-call | flops 2684354560 | bytes 4194304 | tf_op jit(solution)/shard_map/attend/pallas_call | solution.py:178
  40.3 2.0 %project.1 = (bf16[128,512]{1,0:T(8,128)(2,1)S(1)}, bf16[128,512]{1,0:T(8,128)(2,1)S(1)}, bf16[128,512]{1,0:T(8,128)(2,1)}, bf16[128,512]{1,0:T(8,128)(2,1)S(1)}) custom-call(s32[74]{0:T(128)S(1)} %concatenate.35.meta_ref, bf16[512,2048]{1,0:T(8,128)(2,1)S(1)} %copy-done, bf16[144,512]{1,0:T(8,128)(2,1)S(1)} %attend.4.refs_0_, ...), custom_call_target="tpu_custom_call" | custom-call | tf_op jit(solution)/shard_map/project/pallas_call | solution.py:227
  43.9 2.6 %collective-permute-start.7 = (bf16[128,512]{1,0:T(8,128)(2,1)}, bf16[128,512]{1,0:T(8,128)(2,1)}, u32[]{:S(2)}, u32[]{:S(2)}) collective-permute-start(bf16[128,512]{1,0:T(8,128)(2,1)} %get-tuple-element.46), channel_id=1, source_target_pairs={{0,2},{1,3},{2,0},{3,1},{4,6},{5,7},{6,4},{7,5},{8,10},{9,11},{10,... | collective-permute-start | bytes 393224 | tf_op jit(solution)/shard_map/ppermute | solution.py:36
  46.5 4.2 %collective-permute-done.6 = bf16[128,512]{1,0:T(8,128)(2,1)} collective-permute-done((bf16[128,512]{1,0:T(8,128)(2,1)S(1)}, bf16[128,512]{1,0:T(8,128)(2,1)}, u32[]{:S(2)}, u32[]{:S(2)}) %collective-permute-start.6) | collective-permute-done | bytes 131104 | tf_op jit(solution)/shard_map/ppermute | solution.py:36
  51.8 3.4 %collective-permute-done.7 = bf16[128,512]{1,0:T(8,128)(2,1)} collective-permute-done((bf16[128,512]{1,0:T(8,128)(2,1)}, bf16[128,512]{1,0:T(8,128)(2,1)}, u32[]{:S(2)}, u32[]{:S(2)}) %collective-permute-start.7) | collective-permute-done | bytes 131104 | tf_op jit(solution)/shard_map/ppermute | solution.py:36
  57.7 3.8 %collective-permute-start.13 = (bf16[128,512]{1,0:T(8,128)(2,1)S(1)}, bf16[128,512]{1,0:T(8,128)(2,1)S(1)}, u32[]{:S(2)}, u32[]{:S(2)}) collective-permute-start(bf16[128,512]{1,0:T(8,128)(2,1)S(1)} %add_convert_fusion), channel_id=1, source_target_pairs={{0,3},{1,0},{2,1},{3,2},{4,7},{5,4},{6,5},{7,6},{8,11},{9,8},{10,9... | collective-permute-start | bytes 393224 | tf_op jit(solution)/shard_map/ppermute | solution.py:36
  64.3 1.9 %collective-permute-start.11 = (bf16[128,512]{1,0:T(8,128)(2,1)S(1)}, bf16[128,512]{1,0:T(8,128)(2,1)S(1)}, u32[]{:S(2)}, u32[]{:S(2)}) collective-permute-start(bf16[128,512]{1,0:T(8,128)(2,1)S(1)} %add_convert_fusion), channel_id=1, source_target_pairs={{0,1},{1,2},{2,3},{3,0},{4,5},{5,6},{6,7},{7,4},{8,9},{9,10},{10,1... | collective-permute-start | bytes 393224 | tf_op jit(solution)/shard_map/ppermute | solution.py:36
  66.8 4.9 %collective-permute-done.12 = bf16[128,512]{1,0:T(8,128)(2,1)S(1)} collective-permute-done((bf16[128,512]{1,0:T(8,128)(2,1)S(1)}, bf16[128,512]{1,0:T(8,128)(2,1)S(1)}, u32[]{:S(2)}, u32[]{:S(2)}) %collective-permute-start.12) | collective-permute-done | bytes 131104 | tf_op jit(solution)/shard_map/ppermute | solution.py:36
  78.2 4.3 %collective-permute-done.18 = bf16[128,512]{1,0:T(8,128)(2,1)S(1)} collective-permute-done((bf16[128,512]{1,0:T(8,128)(2,1)S(1)}, bf16[128,512]{1,0:T(8,128)(2,1)S(1)}, u32[]{:S(2)}, u32[]{:S(2)}) %collective-permute-start.18) | collective-permute-done | bytes 131104 | tf_op jit(solution)/shard_map/ppermute | solution.py:31
  85.3 3.6 %collective-permute-done.19 = bf16[256,512]{1,0:T(8,128)(2,1)S(1)} collective-permute-done((bf16[256,512]{1,0:T(8,128)(2,1)S(1)}, bf16[256,512]{1,0:T(8,128)(2,1)S(1)}, u32[]{:S(2)}, u32[]{:S(2)}) %collective-permute-start.19) | collective-permute-done | bytes 262176 | tf_op jit(solution)/shard_map/ppermute | solution.py:31
  89.0 3.0 %assemble.1.weights_ref = bf16[2064,2048]{1,0:T(8,128)(2,1)S(1)} custom-call(s32[74]{0:T(128)S(1)} %concatenate.35.meta_ref, bf16[2064,256]{1,0:T(8,128)(2,1)S(1)} %get-tuple-element.38.refs_0_, bf16[2064,256]{1,0:T(8,128)(2,1)S(1)} %collective-permute-done.3.refs_1_, bf16[2064,256]{1,0:T(8,128)(2,1)S(1)} %collective-permute-done.4.refs_2_, ...), custom_call_target="tpu_custom_call" | custom-call | bytes 16908288 | tf_op jit(solution)/shard_map/assemble/pallas_call | solution.py:259
  92.0 6.0 %feed.1 = (bf16[256,512]{1,0:T(8,128)(2,1)S(1)}, bf16[256,512]{1,0:T(8,128)(2,1)S(1)}, bf16[256,512]{1,0:T(8,128)(2,1)S(1)}, bf16[256,512]{1,0:T(8,128)(2,1)S(1)...) custom-call(s32[74]{0:T(128)S(1)} %concatenate.35.meta_ref, ...), custom_call_target="tpu_custom_call" | custom-call | flops 4328521728 | bytes 8454144 | tf_op jit(solution)/shard_map/feed/pallas_call | solution.py:331
  102.3 4.2 %collective-permute-done.24 = bf16[256,512]{1,0:T(8,128)(2,1)S(1)} collective-permute-done((bf16[256,512]{1,0:T(8,128)(2,1)S(1)}, bf16[256,512]{1,0:T(8,128)(2,1)S(1)}, u32[]{:S(2)}, u32[]{:S(2)}) %collective-permute-start.24) | collective-permute-done | bytes 262176 | tf_op jit(solution)/shard_map/ppermute | solution.py:31
  112.5 6.6 %collective-permute-start.26 = (bf16[128,512]{1,0:T(8,128)(2,1)S(1)}, bf16[128,512]{1,0:T(8,128)(2,1)S(1)}, u32[]{:S(2)}, u32[]{:S(2)}) collective-permute-start(bf16[128,512]{1,0:T(8,128)(2,1)S(1)} %fusion.4), channel_id=1, source_target_pairs={{0,1},{1,2},{2,3},{3,0},{4,5},{5,6},{6,7},{7,4},{8,9},{9,10},{10,1... | collective-permute-start | bytes 393224 | tf_op jit(solution)/shard_map/ppermute | solution.py:36
  119.2 2.4 %collective-permute-start.32 = (bf16[128,512]{1,0:T(8,128)(2,1)S(1)}, bf16[128,512]{1,0:T(8,128)(2,1)S(1)}, u32[]{:S(2)}, u32[]{:S(2)}) collective-permute-start(bf16[128,512]{1,0:T(8,128)(2,1)S(1)} %fusion.2), channel_id=1, source_target_pairs={{0,3},{1,0},{2,1},{3,2},{4,7},{5,4},{6,5},{7,6},{8,11},{9,8},{10,9... | collective-permute-start | bytes 393224 | tf_op jit(solution)/shard_map/ppermute | solution.py:36
  121.7 4.6 %collective-permute-done.29 = bf16[128,512]{1,0:T(8,128)(2,1)S(1)} collective-permute-done((bf16[128,512]{1,0:T(8,128)(2,1)S(1)}, bf16[128,512]{1,0:T(8,128)(2,1)S(1)}, u32[]{:S(2)}, u32[]{:S(2)}) %collective-permute-start.29) | collective-permute-done | bytes 131104 | tf_op jit(solution)/shard_map/ppermute | solution.py:36
  (99 shorter events, 34.9 us)
Async XLA Ops:
  9.5 27.9 %collective-permute-start.3 = (bf16[2064,256]{1,0:T(8,128)(2,1)S(1)}, bf16[2064,256]{1,0:T(8,128)(2,1)S(1)}, u32[]{:S(2)}, u32[]{:S(2)}) collective-permute-start(bf16[2064,256]{1,0:T(8,128)(2,1)S(1)} %get-tuple-element.36), channel_id=1, source_target_pairs={{0,8},{4,12},{8,0},{12,4},{16,24},{20,28},{24,16},{28,20},{1,9},{5... | collective-permute-start | bytes 3170312 | tf_op jit(solution)/shard_map/ppermute | solution.py:31
  12.5 24.9 %collective-permute-start.4 = (bf16[2064,256]{1,0:T(8,128)(2,1)S(1)}, bf16[2064,256]{1,0:T(8,128)(2,1)S(1)}, u32[]{:S(2)}, u32[]{:S(2)}) collective-permute-start(bf16[2064,256]{1,0:T(8,128)(2,1)S(1)} %get-tuple-element.37), channel_id=1, source_target_pairs={{0,16},{4,20},{8,24},{12,28},{16,0},{20,4},{24,8},{28,12},{1,17},{... | collective-permute-start | bytes 3170312 | tf_op jit(solution)/shard_map/ppermute | solution.py:31
  14.0 23.4 %collective-permute-start.5 = (bf16[2064,256]{1,0:T(8,128)(2,1)S(1)}, bf16[2064,256]{1,0:T(8,128)(2,1)S(1)}, u32[]{:S(2)}, u32[]{:S(2)}) collective-permute-start(bf16[2064,256]{1,0:T(8,128)(2,1)S(1)} %get-tuple-element.38.refs_0_), channel_id=1, source_target_pairs={{0,4},{4,0},{8,12},{12,8},{16,20},{20,16},{24,28},{28,24},{1,5},{5... | collective-permute-start | bytes 3170312 | tf_op jit(solution)/shard_map/ppermute | solution.py:31
  18.2 12.6 %collective-permute-start = (bf16[144,512]{1,0:T(8,128)(2,1)S(1)}, bf16[144,512]{1,0:T(8,128)(2,1)S(1)}, u32[]{:S(2)}, u32[]{:S(2)}) collective-permute-start(bf16[144,512]{1,0:T(8,128)(2,1)S(1)} %attend.5), channel_id=1, source_target_pairs={{0,1},{1,2},{2,3},{3,0},{4,5},{5,6},{6,7},{7,4},{8,9},{9,10},{10,1... | collective-permute-start | bytes 442376 | tf_op jit(solution)/shard_map/ppermute | solution.py:36
  24.0 12.6 %collective-permute-start.1 = (bf16[144,512]{1,0:T(8,128)(2,1)S(1)}, bf16[144,512]{1,0:T(8,128)(2,1)S(1)}, u32[]{:S(2)}, u32[]{:S(2)}) collective-permute-start(bf16[144,512]{1,0:T(8,128)(2,1)S(1)} %attend.6), channel_id=1, source_target_pairs={{0,2},{1,3},{2,0},{3,1},{4,6},{5,7},{6,4},{7,5},{8,10},{9,11},{10,... | collective-permute-start | bytes 442376 | tf_op jit(solution)/shard_map/ppermute | solution.py:36
  38.4 19.3 %collective-permute-start.9 = (bf16[2064,256]{1,0:T(8,128)(2,1)S(1)}, bf16[2064,256]{1,0:T(8,128)(2,1)}, u32[]{:S(2)}, u32[]{:S(2)}) collective-permute-start(bf16[2064,256]{1,0:T(8,128)(2,1)S(1)} %collective-permute-done.3.refs_1_), channel_id=1, source_target_pairs={{0,4},{4,0},{8,12},{12,8},{16,20},{20,16},{24,28},{28,24},{1,5},{5... | collective-permute-start | bytes 3170312 | tf_op jit(solution)/shard_map/ppermute | solution.py:31
  38.4 19.3 %collective-permute-start.10 = (bf16[2064,256]{1,0:T(8,128)(2,1)S(1)}, bf16[2064,256]{1,0:T(8,128)(2,1)}, u32[]{:S(2)}, u32[]{:S(2)}) collective-permute-start(bf16[2064,256]{1,0:T(8,128)(2,1)S(1)} %collective-permute-done.4.refs_2_), channel_id=1, source_target_pairs={{0,4},{4,0},{8,12},{12,8},{16,20},{20,16},{24,28},{28,24},{1,5},{5... | collective-permute-start | bytes 3170312 | tf_op jit(solution)/shard_map/ppermute | solution.py:31
  38.9 27.9 %collective-permute-start.14 = (bf16[2064,256]{1,0:T(8,128)(2,1)}, bf16[2064,256]{1,0:T(8,128)(2,1)}, u32[]{:S(2)}, u32[]{:S(2)}) collective-permute-start(bf16[2064,256]{1,0:T(8,128)(2,1)} %get-tuple-element.52), channel_id=1, source_target_pairs={{0,24},{4,28},{8,16},{12,20},{16,8},{20,12},{24,0},{28,4},{1,25},{... | collective-permute-start | bytes 3170312 | tf_op jit(solution)/shard_map/ppermute | solution.py:31
  43.9 11.3 %collective-permute-start.7 = (bf16[128,512]{1,0:T(8,128)(2,1)}, bf16[128,512]{1,0:T(8,128)(2,1)}, u32[]{:S(2)}, u32[]{:S(2)}) collective-permute-start(bf16[128,512]{1,0:T(8,128)(2,1)} %get-tuple-element.46), channel_id=1, source_target_pairs={{0,2},{1,3},{2,0},{3,1},{4,6},{5,7},{6,4},{7,5},{8,10},{9,11},{10,... | collective-permute-start | bytes 393224 | tf_op jit(solution)/shard_map/ppermute | solution.py:36
  61.6 10.1 %collective-permute-start.12 = (bf16[128,512]{1,0:T(8,128)(2,1)S(1)}, bf16[128,512]{1,0:T(8,128)(2,1)S(1)}, u32[]{:S(2)}, u32[]{:S(2)}) collective-permute-start(bf16[128,512]{1,0:T(8,128)(2,1)S(1)} %add_convert_fusion), channel_id=1, source_target_pairs={{0,2},{1,3},{2,0},{3,1},{4,6},{5,7},{6,4},{7,5},{8,10},{9,11},{10,... | collective-permute-start | bytes 393224 | tf_op jit(solution)/shard_map/ppermute | solution.py:36
  62.8 10.4 %collective-permute-start.16 = (bf16[128,512]{1,0:T(8,128)(2,1)S(1)}, bf16[128,512]{1,0:T(8,128)(2,1)S(1)}, u32[]{:S(2)}, u32[]{:S(2)}) collective-permute-start(bf16[128,512]{1,0:T(8,128)(2,1)S(1)} %add_convert_fusion), channel_id=1, source_target_pairs={{0,8},{4,12},{8,0},{12,4},{16,24},{20,28},{24,16},{28,20},{1,9},{5... | collective-permute-start | bytes 393224 | tf_op jit(solution)/shard_map/ppermute | solution.py:31
  64.3 9.5 %collective-permute-start.11 = (bf16[128,512]{1,0:T(8,128)(2,1)S(1)}, bf16[128,512]{1,0:T(8,128)(2,1)S(1)}, u32[]{:S(2)}, u32[]{:S(2)}) collective-permute-start(bf16[128,512]{1,0:T(8,128)(2,1)S(1)} %add_convert_fusion), channel_id=1, source_target_pairs={{0,1},{1,2},{2,3},{3,0},{4,5},{5,6},{6,7},{7,4},{8,9},{9,10},{10,1... | collective-permute-start | bytes 393224 | tf_op jit(solution)/shard_map/ppermute | solution.py:36
  66.2 9.1 %collective-permute-start.22 = (bf16[128,512]{1,0:T(8,128)(2,1)S(1)}, bf16[128,512]{1,0:T(8,128)(2,1)S(1)}, u32[]{:S(2)}, u32[]{:S(2)}) collective-permute-start(bf16[128,512]{1,0:T(8,128)(2,1)S(1)} %collective-permute-done.13), channel_id=1, source_target_pairs={{0,16},{4,20},{8,24},{12,28},{16,0},{20,4},{24,8},{28,12},{1,17},{... | collective-permute-start | bytes 393224 | tf_op jit(solution)/shard_map/ppermute | solution.py:31
  66.8 22.2 %collective-permute-start.15 = (bf16[2064,256]{1,0:T(8,128)(2,1)}, bf16[2064,256]{1,0:T(8,128)(2,1)S(1)}, u32[]{:S(2)}, u32[]{:S(2)}) collective-permute-start(bf16[2064,256]{1,0:T(8,128)(2,1)} %collective-permute-done.14.refs_3_), channel_id=1, source_target_pairs={{0,4},{4,0},{8,12},{12,8},{16,20},{20,16},{24,28},{28,24},{1,5},{5... | collective-permute-start | bytes 3170312 | tf_op jit(solution)/shard_map/ppermute | solution.py:31
  73.2 10.4 %collective-permute-start.17 = (bf16[256,512]{1,0:T(8,128)(2,1)S(1)}, bf16[256,512]{1,0:T(8,128)(2,1)S(1)}, u32[]{:S(2)}, u32[]{:S(2)}) collective-permute-start(bf16[256,512]{1,0:T(8,128)(2,1)S(1)} %pad_maximum_fusion.4), channel_id=1, source_target_pairs={{0,16},{4,20},{8,24},{12,28},{16,0},{20,4},{24,8},{28,12},{1,17},{... | collective-permute-start | bytes 786440 | tf_op jit(solution)/shard_map/ppermute | solution.py:31
  73.8 8.6 %collective-permute-start.18 = (bf16[128,512]{1,0:T(8,128)(2,1)S(1)}, bf16[128,512]{1,0:T(8,128)(2,1)S(1)}, u32[]{:S(2)}, u32[]{:S(2)}) collective-permute-start(bf16[128,512]{1,0:T(8,128)(2,1)S(1)} %collective-permute-done.11), channel_id=1, source_target_pairs={{0,16},{4,20},{8,24},{12,28},{16,0},{20,4},{24,8},{28,12},{1,17},{... | collective-permute-start | bytes 393224 | tf_op jit(solution)/shard_map/ppermute | solution.py:31
  98.0 8.6 %collective-permute-start.24 = (bf16[256,512]{1,0:T(8,128)(2,1)S(1)}, bf16[256,512]{1,0:T(8,128)(2,1)S(1)}, u32[]{:S(2)}, u32[]{:S(2)}) collective-permute-start(bf16[256,512]{1,0:T(8,128)(2,1)S(1)} %get-tuple-element.57), channel_id=1, source_target_pairs={{0,16},{4,20},{8,24},{12,28},{16,0},{20,4},{24,8},{28,12},{1,17},{... | collective-permute-start | bytes 786440 | tf_op jit(solution)/shard_map/ppermute | solution.py:31
  99.3 8.9 %collective-permute-start.27 = (bf16[256,512]{1,0:T(8,128)(2,1)S(1)}, bf16[256,512]{1,0:T(8,128)(2,1)S(1)}, u32[]{:S(2)}, u32[]{:S(2)}) collective-permute-start(bf16[256,512]{1,0:T(8,128)(2,1)S(1)} %get-tuple-element.59), channel_id=1, source_target_pairs={{0,8},{4,12},{8,0},{12,4},{16,24},{20,28},{24,16},{28,20},{1,9},{5... | collective-permute-start | bytes 786440 | tf_op jit(solution)/shard_map/ppermute | solution.py:31
  100.2 9.8 %collective-permute-start.30 = (bf16[256,512]{1,0:T(8,128)(2,1)S(1)}, bf16[256,512]{1,0:T(8,128)(2,1)S(1)}, u32[]{:S(2)}, u32[]{:S(2)}) collective-permute-start(bf16[256,512]{1,0:T(8,128)(2,1)S(1)} %get-tuple-element.61), channel_id=1, source_target_pairs={{0,16},{4,20},{8,24},{12,28},{16,0},{20,4},{24,8},{28,12},{1,17},{... | collective-permute-start | bytes 786440 | tf_op jit(solution)/shard_map/ppermute | solution.py:31
  101.4 9.9 %collective-permute-start.33 = (bf16[256,512]{1,0:T(8,128)(2,1)S(1)}, bf16[256,512]{1,0:T(8,128)(2,1)S(1)}, u32[]{:S(2)}, u32[]{:S(2)}) collective-permute-start(bf16[256,512]{1,0:T(8,128)(2,1)S(1)} %get-tuple-element.63), channel_id=1, source_target_pairs={{0,8},{4,12},{8,0},{12,4},{16,24},{20,28},{24,16},{28,20},{1,9},{5... | collective-permute-start | bytes 786440 | tf_op jit(solution)/shard_map/ppermute | solution.py:31
  108.3 10.7 %collective-permute-start.28 = (bf16[128,512]{1,0:T(8,128)(2,1)S(1)}, bf16[128,512]{1,0:T(8,128)(2,1)S(1)}, u32[]{:S(2)}, u32[]{:S(2)}) collective-permute-start(bf16[128,512]{1,0:T(8,128)(2,1)S(1)} %slice.92), channel_id=1, source_target_pairs={{0,16},{4,20},{8,24},{12,28},{16,0},{20,4},{24,8},{28,12},{1,17},{... | collective-permute-start | bytes 393224 | tf_op jit(solution)/shard_map/ppermute | solution.py:31
  110.1 9.0 %collective-permute-start.31 = (bf16[128,512]{1,0:T(8,128)(2,1)S(1)}, bf16[128,512]{1,0:T(8,128)(2,1)S(1)}, u32[]{:S(2)}, u32[]{:S(2)}) collective-permute-start(bf16[128,512]{1,0:T(8,128)(2,1)S(1)} %slice.91), channel_id=1, source_target_pairs={{0,8},{4,12},{8,0},{12,4},{16,24},{20,28},{24,16},{28,20},{1,9},{5... | collective-permute-start | bytes 393224 | tf_op jit(solution)/shard_map/ppermute | solution.py:31
  111.5 10.2 %collective-permute-start.34 = (bf16[128,512]{1,0:T(8,128)(2,1)S(1)}, bf16[128,512]{1,0:T(8,128)(2,1)S(1)}, u32[]{:S(2)}, u32[]{:S(2)}) collective-permute-start(bf16[128,512]{1,0:T(8,128)(2,1)S(1)} %slice.90), channel_id=1, source_target_pairs={{0,16},{4,20},{8,24},{12,28},{16,0},{20,4},{24,8},{28,12},{1,17},{... | collective-permute-start | bytes 393224 | tf_op jit(solution)/shard_map/ppermute | solution.py:31
  112.5 9.2 %collective-permute-start.26 = (bf16[128,512]{1,0:T(8,128)(2,1)S(1)}, bf16[128,512]{1,0:T(8,128)(2,1)S(1)}, u32[]{:S(2)}, u32[]{:S(2)}) collective-permute-start(bf16[128,512]{1,0:T(8,128)(2,1)S(1)} %fusion.4), channel_id=1, source_target_pairs={{0,1},{1,2},{2,3},{3,0},{4,5},{5,6},{6,7},{7,4},{8,9},{9,10},{10,1... | collective-permute-start | bytes 393224 | tf_op jit(solution)/shard_map/ppermute | solution.py:36
  (19 other events, 142.8 us)

commit v3 on v2

v3 whole, which is shorter than its diff:
```python
import functools
import math

import jax
import jax.numpy as jnp
from jax import lax
from jax.experimental import pallas as pl
from jax.experimental.pallas import tpu as pltpu
from jax.sharding import PartitionSpec as P

H = 16
NOPE = 128
ROPE = 64
VDIM = 128
LATENT = 512
QK = NOPE + ROPE
HEAD_UP = NOPE + VDIM
LANES = 128
TAIL = 16
HIDDEN_SCORE = -1e30
VMEM_LIMIT = 24 * 1024 * 1024
PREPARE_LIMIT = 12 * 1024 * 1024
ASSEMBLE_LIMIT = 12 * 1024 * 1024
SUBLANES = 16
LOG2_SCALE = math.log2(math.e) / math.sqrt(QK)
NT = (((1,), (1,)), ((), ()))


def exchange(x, axis, step):
    count = lax.axis_size(axis)
    return lax.ppermute(x, axis, [(i, i ^ step) for i in range(count)])


def rotate(x, axis, step):
    count = lax.axis_size(axis)
    return lax.ppermute(x, axis, [(i, (i + step) % count) for i in range(count)])


def rows_of(ref, index, size):
    return ref[pl.ds(pl.multiple_of(index * size, size), size), :]


def prepare_kernel(
    offset_ref, table_hbm, len_hbm, queries_hbm, pool_hbm, up_hbm, *refs
):
    q_ref, keys_ref, up_ref, pages_ref, queries_ref, table_ref, len_ref, page_sem, sem = refs
    page_count, page_size, _ = pages_ref.shape
    query_rows = queries_ref.shape[0]

    scalar_copies = [
        pltpu.make_async_copy(source, target, sem.at[2 + i])
        for i, (source, target) in enumerate(
            ((table_hbm, table_ref), (len_hbm, len_ref))
        )
    ]
    for copy in scalar_copies:
        copy.start()

    queries_copy = pltpu.make_async_copy(queries_hbm, queries_ref, sem.at[0])
    up_copy = pltpu.make_async_copy(up_hbm, up_ref, sem.at[1])
    queries_copy.start()
    up_copy.start()
    for copy in scalar_copies:
        copy.wait()
    page_copies = [
        pltpu.make_async_copy(pool_hbm.at[table_ref[p]], pages_ref.at[p], page_sem.at[p])
        for p in range(page_count)
    ]
    for copy in page_copies:
        copy.start()
    first_query = offset_ref[0] + lax.axis_index("row") * query_rows
    first_key = lax.axis_index("col") * page_count * page_size

    slot = lax.broadcasted_iota(jnp.int32, (page_size, query_rows), 0)
    query_pos = first_query + lax.broadcasted_iota(jnp.int32, (page_size, query_rows), 1)
    for p in range(page_count):
        page_copies[p].wait()
        rows = pl.ds(p * page_size, page_size)
        page = pages_ref[p]
        keys_ref[rows, :LATENT] = page[:, :LATENT]
        keys_ref[rows, LATENT : LATENT + LANES] = jnp.concatenate(
            [page[:, LATENT:], jnp.zeros((page_size, LANES - ROPE), jnp.bfloat16)], axis=1
        )
        seen = (slot < len_ref[p]) & (first_key + p * page_size + slot <= query_pos)
        keys_ref[rows, LATENT + LANES :] = jnp.where(seen, 0.0, HIDDEN_SCORE).astype(jnp.bfloat16)

    eye = (
        lax.broadcasted_iota(jnp.int32, (query_rows, query_rows), 0)
        == lax.broadcasted_iota(jnp.int32, (query_rows, query_rows), 1)
    ).astype(jnp.bfloat16)
    queries_copy.wait()
    up_copy.wait()
    for h in range(H):
        rows = pl.ds(h * query_rows, query_rows)
        q_nope = queries_ref[:, h * QK : h * QK + NOPE]
        up_k = up_ref[:, h * HEAD_UP : h * HEAD_UP + NOPE]
        absorbed = lax.dot_general(q_nope, up_k, NT, preferred_element_type=jnp.float32)
        q_ref[rows, :LATENT] = absorbed.astype(jnp.bfloat16)
        q_rope = queries_ref[:, h * QK + NOPE : (h + 1) * QK]
        q_ref[rows, LATENT : LATENT + LANES] = jnp.concatenate(
            [q_rope, jnp.zeros((query_rows, LANES - ROPE), jnp.bfloat16)], axis=1
        )
        q_ref[rows, LATENT + LANES :] = eye


def cut_kernel(chips, gate_hbm, unit_hbm, down_hbm, *refs):
    shares, (share_sem,) = refs[:chips], refs[chips:]
    share = shares[0].shape[0] // 3
    units = gate_hbm.shape[0]
    chip_index = lax.axis_index("row") // 2
    share_copies = []
    for step in range(chips):
        at = share_start(chip_index ^ step, share, units)
        rows = pl.ds(pl.multiple_of(at, SUBLANES), share)
        for i, source in enumerate((gate_hbm, unit_hbm, down_hbm)):
            target = shares[step].at[pl.ds(i * share, share), :]
            share_copies.append(
                pltpu.make_async_copy(source.at[rows, :], target, share_sem.at[3 * step + i])
            )
    for copy in share_copies:
        copy.start()
    for copy in share_copies:
        copy.wait()


def cut(by_unit, chips, share):
    hbm = pl.BlockSpec(memory_space=pltpu.HBM)
    return pl.pallas_call(
        functools.partial(cut_kernel, chips),
        out_shape=[pltpu.VMEM((3 * share, by_unit[0].shape[1]), jnp.bfloat16)] * chips,
        in_specs=[hbm] * 3,
        out_specs=[pl.BlockSpec(memory_space=pltpu.VMEM)] * chips,
        scratch_shapes=[pltpu.SemaphoreType.DMA((3 * chips,))],
        compiler_params=pltpu.CompilerParams(vmem_limit_bytes=PREPARE_LIMIT),
        cost_estimate=pl.CostEstimate(flops=0, bytes_accessed=0, transcendentals=0),
        name="cut",
    )(*[pltpu.with_memory_space_constraint(x, pltpu.HBM) for x in by_unit])


def share_start(chip, share, units):
    return jnp.minimum(chip * share, units - share)


def prepare(block_table, page_len, group_offset, queries, latent_pool, latent_up):
    query_rows = queries.shape[0]
    page_count, page_size, cache_width = latent_pool.shape
    keys = page_count * page_size
    width = LATENT + LANES + query_rows
    vmem = pl.BlockSpec(memory_space=pltpu.VMEM)
    hbm = pl.BlockSpec(memory_space=pltpu.HBM)
    sources = (
        block_table, page_len, queries, latent_pool, latent_up
    )
    out = pl.pallas_call(
        prepare_kernel,
        out_shape=[
            pltpu.VMEM((H * query_rows, width), jnp.bfloat16),
            pltpu.VMEM((keys, width), jnp.bfloat16),
            pltpu.VMEM(latent_up.shape, jnp.bfloat16),
        ],
        in_specs=[pl.BlockSpec(memory_space=pltpu.SMEM)] + [hbm] * len(sources),
        out_specs=[vmem] * 3,
        scratch_shapes=[
            pltpu.VMEM((page_count, page_size, cache_width), jnp.bfloat16),
            pltpu.VMEM(queries.shape, jnp.bfloat16),
            pltpu.SMEM(block_table.shape, jnp.int32),
            pltpu.SMEM(page_len.shape, jnp.int32),
            pltpu.SemaphoreType.DMA((page_count,)),
            pltpu.SemaphoreType.DMA((4,)),
        ],
        compiler_params=pltpu.CompilerParams(vmem_limit_bytes=PREPARE_LIMIT),
        cost_estimate=pl.CostEstimate(flops=0, bytes_accessed=0, transcendentals=0),
        name="prepare",
    )(group_offset, *[pltpu.with_memory_space_constraint(x, pltpu.HBM) for x in sources])
    return out


def attend_kernel(step, groups, q_ref, keys_ref, up_ref, out_ref):
    heads_here = H // groups
    query_rows = q_ref.shape[0] // H
    group = lax.rem(lax.axis_index("col") + step, groups)
    q_rows = rows_of(q_ref, group, heads_here * query_rows)
    scores = lax.dot_general(q_rows, keys_ref[...], NT, preferred_element_type=jnp.float32)
    row_max = jnp.max(scores, axis=1, keepdims=True)
    weights = jnp.exp2((scores - row_max) * LOG2_SCALE)
    totals = jnp.sum(weights, axis=1, keepdims=True)
    context = jnp.dot(
        weights.astype(jnp.bfloat16), keys_ref[:, :LATENT], preferred_element_type=jnp.float32
    )
    context = (context / totals).astype(jnp.bfloat16)
    log_sum = row_max * LOG2_SCALE + jnp.log2(totals)
    tail = []
    for j in range(heads_here):
        own = slice(j * query_rows, (j + 1) * query_rows)
        at = pl.multiple_of((group * heads_here + j) * HEAD_UP + NOPE, LANES)
        up_v = up_ref[:, pl.ds(at, VDIM)]
        mixed = jnp.dot(context[own], up_v, preferred_element_type=jnp.float32)
        out_ref[:query_rows, j * VDIM : (j + 1) * VDIM] = mixed.astype(jnp.bfloat16)
        wide = jnp.broadcast_to(log_sum[own], (query_rows, LANES))
        tail.append(jnp.transpose(wide)[:1])
    tail = jnp.concatenate(tail, axis=1)
    high = tail.astype(jnp.bfloat16)
    rest = tail - high.astype(jnp.float32)
    middle = rest.astype(jnp.bfloat16)
    low = (rest - middle.astype(jnp.float32)).astype(jnp.bfloat16)
    parts = [high.astype(jnp.float32), middle.astype(jnp.float32), low.astype(jnp.float32)]
    parts.append(jnp.zeros((TAIL - 3, tail.shape[1]), jnp.float32))
    out_ref[query_rows:, :] = jnp.concatenate(parts, axis=0).astype(jnp.bfloat16)


def attend(step, groups, q, keys, latent_up):
    query_rows = q.shape[0] // H
    heads_here = H // groups
    vmem = pl.BlockSpec(memory_space=pltpu.VMEM)
    return pl.pallas_call(
        functools.partial(attend_kernel, step, groups),
        out_shape=jax.ShapeDtypeStruct((query_rows + TAIL, heads_here * VDIM), jnp.bfloat16),
        in_specs=[vmem, vmem, vmem],
        out_specs=vmem,
        compiler_params=pltpu.CompilerParams(vmem_limit_bytes=VMEM_LIMIT),
        cost_estimate=pl.CostEstimate(
            flops=7 * heads_here * query_rows * keys.shape[0] * (keys.shape[1] + LATENT) // 5,
            bytes_accessed=4 * 1024 * 1024,
            transcendentals=heads_here * query_rows * keys.shape[0],
        ),
        name="attend",
    )(q, keys, latent_up)


def project_kernel(groups, weight_ref, *refs):
    parts, outs = refs[:groups], refs[groups:]
    query_rows = outs[0].shape[0]
    width = outs[0].shape[1]
    heads_here = parts[0].shape[1] // VDIM
    col_index = lax.axis_index("col")
    mixed = []
    for j in range(heads_here):
        lanes = slice(j * VDIM, (j + 1) * VDIM)
        logs = []
        for part in parts:
            tail = part[query_rows:, lanes].astype(jnp.float32)
            line = tail[0:1] + tail[1:2] + tail[2:3]
            logs.append(jnp.transpose(jnp.broadcast_to(line, (LANES, query_rows))))
        top = functools.reduce(jnp.maximum, logs)
        scales = [jnp.exp2(v - top) for v in logs]
        total = functools.reduce(jnp.add, scales)
        value = functools.reduce(
            jnp.add, [s * part[:query_rows, lanes].astype(jnp.float32) for s, part in zip(scales, parts)]
        )
        mixed.append((value / total).astype(jnp.bfloat16))
    mixed = jnp.concatenate(mixed, axis=1)
    for step in range(groups):
        at = pl.multiple_of(lax.rem(col_index + step, groups) * width, width)
        columns = weight_ref[:, pl.ds(at, width)]
        outs[step][...] = jnp.dot(mixed, columns, preferred_element_type=jnp.float32).astype(
            jnp.bfloat16
        )


def project(parts, output_weight, query_rows):
    groups = len(parts)
    vmem = pl.BlockSpec(memory_space=pltpu.VMEM)
    width = output_weight.shape[1] // groups
    return pl.pallas_call(
        functools.partial(project_kernel, groups),
        out_shape=[jax.ShapeDtypeStruct((query_rows, width), jnp.bfloat16)] * groups,
        in_specs=[vmem] * (1 + groups),
        out_specs=[vmem] * groups,
        compiler_params=pltpu.CompilerParams(vmem_limit_bytes=32 * 1024 * 1024),
        name="project",
    )(output_weight, *parts)


def assemble_kernel(chips, groups, *refs):
    blocks, refs = refs[: 2 * chips], refs[2 * chips :]
    pieces, (in_ref, down_ref, attended_ref, sem) = refs[:groups], refs[groups:]
    depth = blocks[0].shape[1]
    width = pieces[0].shape[1]
    share = down_ref.shape[0]
    col_index = lax.axis_index("col")
    row_index = lax.axis_index("row")
    copies = []
    for core_step in range(2):
        for step in range(chips):
            number = core_step * chips + step
            at = (row_index ^ (2 * step + core_step)) * depth
            chunk, rest = at // width, lax.rem(at, width)
            arrives = lax.rem(col_index + groups - chunk, groups)
            leaves = lax.rem(chunk + groups - col_index, groups)
            for i, (ref, place, first, rows) in enumerate(
                ((in_ref, arrives, 0, 2 * share), (down_ref, leaves, 2 * share, share))
            ):
                lanes = pl.ds(pl.multiple_of(place * width + rest, depth), depth)
                source = blocks[number].at[pl.ds(first, rows), :]
                copies.append(
                    pltpu.make_async_copy(source, ref.at[:, lanes], sem.at[2 * number + i])
                )
    for copy in copies:
        copy.start()
    for s in range(groups):
        at = pl.multiple_of(lax.rem(col_index + groups - s, groups) * width, width)
        attended_ref[:, pl.ds(at, width)] = pieces[s][...]
    for copy in copies:
        copy.wait()


def assemble(blocks, pieces):
    rows, depth = blocks[0].shape
    share = rows // 3
    query_rows, width = pieces[0].shape
    model = depth * len(blocks)
    vmem = pl.BlockSpec(memory_space=pltpu.VMEM)
    return pl.pallas_call(
        functools.partial(assemble_kernel, len(blocks) // 2, len(pieces)),
        out_shape=[
            pltpu.VMEM((2 * share, model), jnp.bfloat16),
            pltpu.VMEM((share, model), jnp.bfloat16),
            jax.ShapeDtypeStruct((query_rows, model), jnp.bfloat16),
        ],
        in_specs=[vmem] * (len(blocks) + len(pieces)),
        out_specs=[vmem] * 3,
        scratch_shapes=[pltpu.SemaphoreType.DMA((2 * len(blocks),))],
        compiler_params=pltpu.CompilerParams(vmem_limit_bytes=ASSEMBLE_LIMIT),
        cost_estimate=pl.CostEstimate(
            flops=0, bytes_accessed=8 * rows * model, transcendentals=0
        ),
        name="assemble",
    )(*[pltpu.with_memory_space_constraint(block, pltpu.VMEM) for block in blocks], *pieces)


def gate_up(tokens, weights):
    together = jnp.concatenate(tokens, axis=1) if len(tokens) > 1 else tokens[0]
    sums = lax.dot_general(together, weights, NT, preferred_element_type=jnp.float32)
    squares = 0.0
    for token in tokens:
        wide = token.astype(jnp.float32)
        squares = squares + jnp.sum(wide * wide, axis=1, keepdims=True)
    return sums, squares


def feed_first_kernel(order, in_ref, *refs):
    sides, (sums_ref, squares_ref) = refs[:-2], refs[-2:]
    count = len(sides) // len(order)
    tokens = [
        join_rows(sides[i * count : (i + 1) * count], bits) for i, bits in enumerate(order)
    ]
    columns = sum(token.shape[1] for token in tokens)
    sums_ref[...], squares_ref[...] = gate_up(tokens, in_ref[:, :columns])


def feed_first(weights, tokens, order):
    rows, width = sum(side.shape[0] for side in tokens[0]), tokens[0][0].shape[1]
    sides = [side for token in tokens for side in token]
    vmem = pl.BlockSpec(memory_space=pltpu.VMEM)
    return pl.pallas_call(
        functools.partial(feed_first_kernel, order),
        out_shape=[
            pltpu.VMEM((rows, weights.shape[0]), jnp.float32),
            pltpu.VMEM((rows, 1), jnp.float32),
        ],
        in_specs=[vmem] * (1 + len(sides)),
        out_specs=[vmem] * 2,
        compiler_params=pltpu.CompilerParams(vmem_limit_bytes=VMEM_LIMIT),
        cost_estimate=pl.CostEstimate(
            flops=4 * rows * width * len(tokens) * weights.shape[0],
            bytes_accessed=1024 * 1024,
            transcendentals=0,
        ),
        name="feed_first",
    )(weights, *sides)


def feed_kernel(groups, chips, units, order, in_ref, down_ref, sums_ref, squares_ref, *refs):
    sides, refs = refs[: -2 * groups - 1], refs[-2 * groups - 1 :]
    keeps, sends, (active_ref,) = refs[:groups], refs[groups : 2 * groups], refs[2 * groups :]
    token = join_rows(sides, order[-1])
    rows, width = token.shape
    share, model = down_ref.shape
    query_rows = rows // chips
    sums, squares = gate_up([token], in_ref[:, model - width :])
    sums = sums + sums_ref[...]
    scale = lax.rsqrt((squares + squares_ref[...]) / model + 1e-06)
    gate = sums[:, :share] * scale
    active = gate / (1.0 + jnp.exp(-gate)) * (sums[:, share:] * scale)
    chip_index = lax.axis_index("row") // 2
    repeated = chip_index * share - share_start(chip_index, share, units)
    unit = lax.broadcasted_iota(jnp.int32, active.shape, 1)
    active_ref[...] = jnp.where(unit < repeated, 0.0, active).astype(jnp.bfloat16)
    for s in range(groups):
        out = jnp.dot(
            active_ref[...],
            down_ref[:, s * width : (s + 1) * width],
            preferred_element_type=jnp.float32,
        ).astype(jnp.bfloat16)
        kept, sent = halves(order[s], chips)
        for ref, steps in ((keeps[s], kept), (sends[s], sent)):
            for i, step in enumerate(steps):
                ref[i * query_rows : (i + 1) * query_rows, :] = out[
                    step * query_rows : (step + 1) * query_rows
                ]


def halves(bits, chips):
    if not bits:
        return [0], []
    return [s for s in range(chips) if not s & bits[0]], [s for s in range(chips) if s & bits[0]]


def feed(weights, down, partial, token, units, chips, order):
    rows, width = sum(side.shape[0] for side in token), token[0].shape[1]
    share, model = down.shape
    groups = model // width
    vmem = pl.BlockSpec(memory_space=pltpu.VMEM)
    kept, sent = halves(order[0], chips)
    query_rows = rows // chips
    shapes = [
        jax.ShapeDtypeStruct((max(len(steps), 1) * query_rows, width), jnp.bfloat16)
        for steps in (kept, sent)
    ]
    return pl.pallas_call(
        functools.partial(feed_kernel, groups, chips, units, order),
        out_shape=[shapes[0]] * groups + [shapes[1]] * groups,
        in_specs=[vmem] * (4 + len(token)),
        out_specs=[vmem] * (2 * groups),
        scratch_shapes=[pltpu.VMEM((rows, share), jnp.bfloat16)],
        compiler_params=pltpu.CompilerParams(vmem_limit_bytes=VMEM_LIMIT),
        cost_estimate=pl.CostEstimate(
            flops=2 * rows * model * share, bytes_accessed=1024 * 1024, transcendentals=0
        ),
        name="feed",
    )(weights, down, *partial, *token)


def gather_rows(block, bits, got):
    sides = [block, got]
    for bit in bits[1:]:
        block = jnp.concatenate(sides, axis=0)
        sides = [block, exchange(block, "row", 2 * bit)]
    return sides


def join_rows(sides, bits):
    steps = [0]
    for bit in bits:
        steps = steps + [s ^ bit for s in steps]
    rows = sides[0].shape[0] * len(sides) // len(steps)
    each = [side[at : at + rows, :] for side in sides for at in range(0, side.shape[0], rows)]
    return jnp.concatenate([each[steps.index(s)] for s in sorted(steps)], axis=0)


def sum_rows(kept, got, bits, query_rows):
    kept = kept.astype(jnp.float32) + got.astype(jnp.float32)
    for i, bit in enumerate(bits[1:], 1):
        left = [s for s in range(1 << len(bits)) if not any(s & b for b in bits[:i])]
        stays, goes = [
            jnp.concatenate(
                [
                    kept[n * query_rows : (n + 1) * query_rows]
                    for n, s in enumerate(left)
                    if bool(s & bit) == away
                ],
                axis=0,
            )
            for away in (False, True)
        ]
        kept = stays + exchange(goes.astype(jnp.bfloat16), "row", 2 * bit).astype(jnp.float32)
    return kept


def on_device(
    queries,
    latent_pool,
    block_table,
    page_len,
    group_offset,
    hidden,
    latent_up,
    output_weight,
    gate_weight,
    up_weight,
    down_weight,
):
    cols = lax.axis_size("col")
    chips = lax.axis_size("row") // 2
    col_index = lax.axis_index("col")
    query_rows, model = hidden.shape
    depth, units = gate_weight.shape
    by_unit = (gate_weight.T, up_weight.T, down_weight)
    if units % SUBLANES:
        by_unit = [jnp.pad(w, ((0, -units % SUBLANES), (0, 0))) for w in by_unit]
        units = by_unit[0].shape[0]
    share = -(-units // (chips * SUBLANES)) * SUBLANES
    width = model // cols

    shares = cut(by_unit, chips, share)
    q, keys, up_here = prepare(
        block_table, page_len, group_offset, queries, latent_pool, latent_up
    )
    early = range(1, chips // 2 + 1)
    late = range(chips // 2 + 1, chips)
    blocks = {s: exchange(shares[s], "row", 2 * s) for s in early}
    swapped = {0: exchange(shares[0], "row", 1)}

    payloads = [attend(s, cols, q, keys, up_here) for s in range(cols)]
    payloads[0], last = lax.optimization_barrier((payloads[0], [shares[s] for s in late]))
    parts = [payloads[0]] + [rotate(payloads[s], "col", s) for s in range(1, cols)]
    late_blocks = {s: exchange(share_out, "row", 2 * s) for s, share_out in zip(late, last)}
    terms = project(parts, output_weight, query_rows)
    terms, swapped, blocks = lax.optimization_barrier((terms, swapped, blocks))
    blocks.update(late_blocks)
    for s in early:
        swapped[s] = exchange(blocks[s], "row", 1)
    here = lax.dynamic_slice_in_dim(hidden, col_index * width, width, 1).astype(jnp.float32)
    here = here + terms[0].astype(jnp.float32)
    for s in range(1, cols):
        here = here + rotate(terms[s], "col", s).astype(jnp.float32)
    here = here.astype(jnp.bfloat16)
    here, swapped = lax.optimization_barrier((here, swapped))

    rising = [1 << i for i in range(chips.bit_length() - 1)]
    order = [rising if s % 2 == 0 else rising[::-1] for s in range(cols)]
    pieces = [here] + [rotate(here, "col", s) for s in range(1, cols)]
    got = [exchange(pieces[s], "row", 2 * order[s][0]) for s in range(cols)]
    got, blocks = lax.optimization_barrier((got, blocks))
    for s in late:
        swapped[s] = exchange(blocks[s], "row", 1)
    blocks[0] = shares[0]
    blocks = [blocks[s] for s in range(chips)] + [swapped[s] for s in range(chips)]
    tokens = [gather_rows(pieces[s], order[s], got[s]) for s in range(cols)]
    weights, down, attended = assemble(blocks, pieces)
    partial = feed_first(weights, tokens[:-1], order[:-1])
    out = feed(weights, down, partial, tokens[-1], units, chips, order)
    total = here.astype(jnp.float32)
    outward = range(cols - 1, 0, -1)
    got = {s: exchange(out[cols + s], "row", 2 * order[s][0]) for s in outward}
    got[0] = exchange(out[cols], "row", 2 * order[0][0])
    terms = {s: sum_rows(out[s], got[s], order[s], query_rows) for s in outward}
    for s in outward:
        total = total + rotate(terms[s].astype(jnp.bfloat16), "col", s).astype(jnp.float32)
    total = total + sum_rows(out[0], got[0], order[0], query_rows)
    return (attended, total.astype(jnp.bfloat16))


def solution(mesh):
    placed = (
        P("row", None),
        P("col", None, None),
        P("col"),
        P("col"),
        P(),
        P("row", None),
        P(),
        P("col", None),
        P("row", "col"),
        P("row", "col"),
        P("col", "row"),
    )
    return jax.shard_map(
        on_device,
        mesh=mesh,
        in_specs=placed,
        out_specs=(P("row", None), P("row", "col")),
        check_vma=False,
    )
```

time: 127 us -> 123 us (0.969)
  starting transfers between devices: 51.2 us -> 46.7 us
  waiting for transfers between devices: 34.5 us -> 37.6 us
  Pallas kernels: 35.1 us -> 33.7 us
    ppermute x12, starting transfers between devices: 27.1 us -> 22.3 us  [rotate(): lax.ppermute(x, axis, [(i, (i + step) % count) for i in range(count)])]
    ppermute x23, waiting for transfers between devices: 15.2 us -> 17.8 us  [exchange(): return lax.ppermute(x, axis, [(i, i ^ step) for i in range(count)])]
    pallas_call x4, Pallas kernels: 16.7 us -> 14.5 us  [attend(): pl.pallas_call(functools.partial(attend_kernel, step, groups), out_shape=...]
    pallas_call x3 -> x5, Pallas kernels: 16.4 us -> 17.7 us  [the longest x1 4.47 us: prepare(): pl.pallas_call(prepare_kernel, out_shape=[pltpu.VMEM((H * query_rows, wid...]
  transfers between devices with their start and end apart: 35 -> 35, of which waited for: 13 -> 14; matrix products, arithmetic and copies ran while one was open for 2% -> 1% of each run, Pallas kernels for 15% -> 22%
where the time goes in v3:
time: 123 us
  starting transfers between devices  46.7 us (38%)
  waiting for transfers between devices  37.6 us (31%)
  Pallas kernels  33.7 us (27%)
  other arithmetic  2.31 us (2%)
  between operations  1.55 us (1%)
    ppermute x23, starting transfers between devices, exchange(): return lax.ppermute(x, axis, [(i, i ^ step) for i in range(count)])  24.4 us
    ppermute x12, starting transfers between devices, rotate(): lax.ppermute(x, axis, [(i, (i + step) % count) for i in range(count)])  22.3 us
    ppermute x12, waiting for transfers between devices, rotate(): lax.ppermute(x, axis, [(i, (i + step) % count) for i in range(count)])  19.9 us
    ppermute x23, waiting for transfers between devices, exchange(): return lax.ppermute(x, axis, [(i, i ^ step) for i in range(count)])  17.8 us
    pallas_call x4, Pallas kernels, attend(): pl.pallas_call(functools.partial(attend_kernel, step, groups), out_shape=...  14.5 us
    pallas_call x1, Pallas kernels, prepare(): pl.pallas_call(prepare_kernel, out_shape=[pltpu.VMEM((H * query_rows, wid...  4.47 us
    pallas_call x1, Pallas kernels, assemble(): pl.pallas_call(functools.partial(assemble_kernel, len(blocks) // 2, len(p...  4.39 us
    pallas_call x1, Pallas kernels, cut(): pl.pallas_call(functools.partial(cut_kernel, chips), out_shape=[pltpu.VME...  3.27 us
  transfers between devices with their start and end apart: 35, of which 14 were waited for; matrix products, arithmetic and copies ran while one was open for 1% of the time, Pallas kernels for 22%

profile of v3, /device:TPU:0, one launch (start us, length us, event | category | flops | bytes accessed | tf_op | source)
XLA Modules:
  0.0 122.7 jit_solution(1901610148446174297)
XLA Ops:
  0.6 3.3 %cut.1 = (bf16[2064,256]{1,0:T(8,128)(2,1)S(1)}, bf16[2064,256]{1,0:T(8,128)(2,1)S(1)}, bf16[2064,256]{1,0:T(8,128)(2,1)S(1)}, bf16[2064,256]{1,0:T(8,128)(2,1)}) custom-call(bf16[2736,256]{1,0:T(8,128)(2,1)} %bitcast.2, bf16[2736,256]{1,0:T(8,128)(2,1)} %bitcast.3, bf16[2736,256]{1,0:T(8,128)(2,1)} %down_hbm.1), custom_call_target="tpu_custom_call" | custom-call | tf_op jit(solution)/shard_map/cut/pallas_call | solution.py:128
  4.4 2.6 %collective-permute-start.4 = (bf16[2064,256]{1,0:T(8,128)(2,1)S(1)}, bf16[2064,256]{1,0:T(8,128)(2,1)S(1)}, u32[]{:S(2)}, u32[]{:S(2)}) collective-permute-start(bf16[2064,256]{1,0:T(8,128)(2,1)S(1)} %get-tuple-element.56), channel_id=1, source_target_pairs={{0,8},{4,12},{8,0},{12,4},{16,24},{20,28},{24,16},{28,20},{1,9},{5... | collective-permute-start | bytes 3170312 | tf_op jit(solution)/shard_map/ppermute | solution.py:31
  9.2 4.5 %prepare.1 = (bf16[2048,768]{1,0:T(8,128)(2,1)S(1)}, bf16[2048,768]{1,0:T(8,128)(2,1)S(1)}, bf16[512,4096]{1,0:T(8,128)(2,1)S(1)}) custom-call(s32[1]{0:T(128)S(6)} %copy.17.offset_ref, s32[32]{0:T(128)} %table_hbm.1, s32[32]{0:T(128)} %len_hbm.1, bf16[128,3072]{1,0:T(8,128)(2,1)} %queries_hbm.1, bf16[32,64,576]{2,1,0:T(8,128)(2,1)} %pool_hbm.1, ...), custom_call_target="tpu_custom_call" | custom-call | tf_op jit(solution)/shard_map/prepare/pallas_call | solution.py:154
  13.6 3.6 %attend.5 = bf16[144,512]{1,0:T(8,128)(2,1)S(1)} custom-call(bf16[2048,768]{1,0:T(8,128)(2,1)S(1)} %get-tuple-element.47.q_ref, bf16[2048,768]{1,0:T(8,128)(2,1)S(1)} %get-tuple-element.48.keys_ref, bf16[512,4096]{1,0:T(8,128)(2,1)S(1)} %get-tuple-element.49.up_ref), custom_call_target="tpu_custom_call" | custom-call | flops 1879048192 | bytes 4194304 | tf_op jit(solution)/shard_map/attend/pallas_call | solution.py:215
  18.9 3.6 %attend.6 = bf16[144,512]{1,0:T(8,128)(2,1)S(1)} custom-call(bf16[2048,768]{1,0:T(8,128)(2,1)S(1)} %get-tuple-element.47.q_ref, bf16[2048,768]{1,0:T(8,128)(2,1)S(1)} %get-tuple-element.48.keys_ref, bf16[512,4096]{1,0:T(8,128)(2,1)S(1)} %get-tuple-element.49.up_ref), custom_call_target="tpu_custom_call" | custom-call | flops 1879048192 | bytes 4194304 | tf_op jit(solution)/shard_map/attend/pallas_call | solution.py:215
  22.5 2.6 %collective-permute-start.1 = (bf16[144,512]{1,0:T(8,128)(2,1)S(1)}, bf16[144,512]{1,0:T(8,128)(2,1)S(1)}, u32[]{:S(2)}, u32[]{:S(2)}) collective-permute-start(bf16[144,512]{1,0:T(8,128)(2,1)S(1)} %attend.6), channel_id=1, source_target_pairs={{0,2},{1,3},{2,0},{3,1},{4,6},{5,7},{6,4},{7,5},{8,10},{9,11},{10,... | collective-permute-start | bytes 442376 | tf_op jit(solution)/shard_map/ppermute | solution.py:36
  25.2 3.6 %attend.7 = bf16[144,512]{1,0:T(8,128)(2,1)S(1)} custom-call(bf16[2048,768]{1,0:T(8,128)(2,1)S(1)} %get-tuple-element.47.q_ref, bf16[2048,768]{1,0:T(8,128)(2,1)S(1)} %get-tuple-element.48.keys_ref, bf16[512,4096]{1,0:T(8,128)(2,1)S(1)} %get-tuple-element.49.up_ref), custom_call_target="tpu_custom_call" | custom-call | flops 1879048192 | bytes 4194304 | tf_op jit(solution)/shard_map/attend/pallas_call | solution.py:215
  30.5 3.6 %attend.4.refs_0_ = bf16[144,512]{1,0:T(8,128)(2,1)S(1)} custom-call(bf16[2048,768]{1,0:T(8,128)(2,1)S(1)} %get-tuple-element.47.q_ref, bf16[2048,768]{1,0:T(8,128)(2,1)S(1)} %get-tuple-element.48.keys_ref, bf16[512,4096]{1,0:T(8,128)(2,1)S(1)} %get-tuple-element.49.up_ref), custom_call_target="tpu_custom_call" | custom-call | flops 1879048192 | bytes 4194304 | tf_op jit(solution)/shard_map/attend/pallas_call | solution.py:215
  37.8 2.3 %collective-permute-start.8 = (bf16[128,512]{1,0:T(8,128)(2,1)S(1)}, bf16[128,512]{1,0:T(8,128)(2,1)S(1)}, u32[]{:S(2)}, u32[]{:S(2)}) collective-permute-start(bf16[128,512]{1,0:T(8,128)(2,1)S(1)} %get-tuple-element.61), channel_id=1, source_target_pairs={{0,3},{1,0},{2,1},{3,2},{4,7},{5,4},{6,5},{7,6},{8,11},{9,8},{10,9... | collective-permute-start | bytes 393224 | tf_op jit(solution)/shard_map/ppermute | solution.py:36
  40.1 3.9 %collective-permute-done.8 = bf16[128,512]{1,0:T(8,128)(2,1)S(1)} collective-permute-done((bf16[128,512]{1,0:T(8,128)(2,1)S(1)}, bf16[128,512]{1,0:T(8,128)(2,1)S(1)}, u32[]{:S(2)}, u32[]{:S(2)}) %collective-permute-start.8) | collective-permute-done | bytes 131104 | tf_op jit(solution)/shard_map/ppermute | solution.py:36
  44.6 6.9 %collective-permute-done.7 = bf16[128,512]{1,0:T(8,128)(2,1)} collective-permute-done((bf16[128,512]{1,0:T(8,128)(2,1)}, bf16[128,512]{1,0:T(8,128)(2,1)}, u32[]{:S(2)}, u32[]{:S(2)}) %collective-permute-start.7) | collective-permute-done | bytes 131104 | tf_op jit(solution)/shard_map/ppermute | solution.py:36
  53.3 2.4 %collective-permute-start.14 = (bf16[128,512]{1,0:T(8,128)(2,1)S(1)}, bf16[128,512]{1,0:T(8,128)(2,1)S(1)}, u32[]{:S(2)}, u32[]{:S(2)}) collective-permute-start(bf16[128,512]{1,0:T(8,128)(2,1)S(1)} %add_convert_fusion.refs_8_), channel_id=1, source_target_pairs={{0,2},{1,3},{2,0},{3,1},{4,6},{5,7},{6,4},{7,5},{8,10},{9,11},{10,... | collective-permute-start | bytes 393224 | tf_op jit(solution)/shard_map/ppermute | solution.py:36
  55.7 2.5 %collective-permute-start.16 = (bf16[128,512]{1,0:T(8,128)(2,1)S(1)}, bf16[128,512]{1,0:T(8,128)(2,1)S(1)}, u32[]{:S(2)}, u32[]{:S(2)}) collective-permute-start(bf16[128,512]{1,0:T(8,128)(2,1)S(1)} %add_convert_fusion.refs_8_), channel_id=1, source_target_pairs={{0,3},{1,0},{2,1},{3,2},{4,7},{5,4},{6,5},{7,6},{8,11},{9,8},{10,9... | collective-permute-start | bytes 393224 | tf_op jit(solution)/shard_map/ppermute | solution.py:36
  62.6 2.3 %collective-permute-done.14.refs_10_ = bf16[128,512]{1,0:T(8,128)(2,1)S(1)} collective-permute-done((bf16[128,512]{1,0:T(8,128)(2,1)S(1)}, bf16[128,512]{1,0:T(8,128)(2,1)S(1)}, u32[]{:S(2)}, u32[]{:S(2)}) %collective-permute-start.14) | collective-permute-done | bytes 131104 | tf_op jit(solution)/shard_map/ppermute | solution.py:36
  75.7 4.4 %assemble.1 = (bf16[1376,2048]{1,0:T(8,128)(2,1)S(1)}, bf16[688,2048]{1,0:T(8,128)(2,1)S(1)}, bf16[128,2048]{1,0:T(8,128)(2,1)}) custom-call(bf16[2064,256]{1,0:T(8,128)(2,1)S(1)} %get-tuple-element.46.refs_0_, bf16[2064,256]{1,0:T(8,128)(2,1)S(1)} %collective-permute-done.4.refs_1_, bf16[2064,256]{1,0:T(8,128)(2,1)} %collective-permute-done.5.refs_2_, ...), custom_call_target="tpu_custom_call" | custom-call | bytes 33816576 | tf_op jit(solution)/shard_map/assemble/pallas_call | solution.py:313
  82.1 3.6 %collective-permute-done.22.refs_5_ = bf16[256,512]{1,0:T(8,128)(2,1)S(1)} collective-permute-done((bf16[256,512]{1,0:T(8,128)(2,1)S(1)}, bf16[256,512]{1,0:T(8,128)(2,1)S(1)}, u32[]{:S(2)}, u32[]{:S(2)}) %collective-permute-start.22) | collective-permute-done | bytes 262176 | tf_op jit(solution)/shard_map/ppermute | solution.py:31
  85.7 2.6 %feed_first.1 = (f32[512,1376]{1,0:T(8,128)S(1)}, f32[512,1]{1,0:T(8,128)S(1)}) custom-call(bf16[1376,2048]{1,0:T(8,128)(2,1)S(1)} %get-tuple-element.74.in_ref, bf16[256,512]{1,0:T(8,128)(2,1)S(1)} %constant_dynamic-update-slice_fusion.refs_0_, bf16[256,512]{1,0:T(8,128)(2,1)S(1)} %collective-permute-done.20.refs_1_, ...), custom_call_target="tpu_custom_call" | custom-call | flops 4328521728 | bytes 1048576 | tf_op jit(solution)/shard_map/feed_first/pallas_call | solution.py:355
  88.4 2.9 %feed.1 = (bf16[256,512]{1,0:T(8,128)(2,1)S(1)}, bf16[256,512]{1,0:T(8,128)(2,1)S(1)}, bf16[256,512]{1,0:T(8,128)(2,1)S(1)}, bf16[256,512]{1,0:T(8,128)(2,1)S(1)...) custom-call(bf16[1376,2048]{1,0:T(8,128)(2,1)S(1)} %get-tuple-elemen, ...), custom_call_target="tpu_custom_call" | custom-call | flops 1442840576 | bytes 1048576 | tf_op jit(solution)/shard_map/feed/pallas_call | solution.py:420
  95.4 5.2 %collective-permute-done.33 = bf16[256,512]{1,0:T(8,128)(2,1)S(1)} collective-permute-done((bf16[256,512]{1,0:T(8,128)(2,1)S(1)}, bf16[256,512]{1,0:T(8,128)(2,1)S(1)}, u32[]{:S(2)}, u32[]{:S(2)}) %collective-permute-start.33) | collective-permute-done | bytes 262176 | tf_op jit(solution)/shard_map/ppermute | solution.py:31
  103.0 3.2 %collective-permute-done.27 = bf16[256,512]{1,0:T(8,128)(2,1)S(1)} collective-permute-done((bf16[256,512]{1,0:T(8,128)(2,1)S(1)}, bf16[256,512]{1,0:T(8,128)(2,1)S(1)}, u32[]{:S(2)}, u32[]{:S(2)}) %collective-permute-start.27) | collective-permute-done | bytes 262176 | tf_op jit(solution)/shard_map/ppermute | solution.py:31
  108.6 2.4 %collective-permute-start.32 = (bf16[128,512]{1,0:T(8,128)(2,1)S(1)}, bf16[128,512]{1,0:T(8,128)(2,1)S(1)}, u32[]{:S(2)}, u32[]{:S(2)}) collective-permute-start(bf16[128,512]{1,0:T(8,128)(2,1)S(1)} %fusion.2), channel_id=1, source_target_pairs={{0,1},{1,2},{2,3},{3,0},{4,5},{5,6},{6,7},{7,4},{8,9},{9,10},{10,1... | collective-permute-start | bytes 393224 | tf_op jit(solution)/shard_map/ppermute | solution.py:36
  111.4 3.7 %collective-permute-start.29 = (bf16[128,512]{1,0:T(8,128)(2,1)S(1)}, bf16[128,512]{1,0:T(8,128)(2,1)S(1)}, u32[]{:S(2)}, u32[]{:S(2)}) collective-permute-start(bf16[128,512]{1,0:T(8,128)(2,1)S(1)} %fusion.3), channel_id=1, source_target_pairs={{0,2},{1,3},{2,0},{3,1},{4,6},{5,7},{6,4},{7,5},{8,10},{9,11},{10,... | collective-permute-start | bytes 393224 | tf_op jit(solution)/shard_map/ppermute | solution.py:36
  115.1 2.5 %collective-permute-start.26 = (bf16[128,512]{1,0:T(8,128)(2,1)S(1)}, bf16[128,512]{1,0:T(8,128)(2,1)S(1)}, u32[]{:S(2)}, u32[]{:S(2)}) collective-permute-start(bf16[128,512]{1,0:T(8,128)(2,1)S(1)} %fusion.4), channel_id=1, source_target_pairs={{0,3},{1,0},{2,1},{3,2},{4,7},{5,4},{6,5},{7,6},{8,11},{9,8},{10,9... | collective-permute-start | bytes 393224 | tf_op jit(solution)/shard_map/ppermute | solution.py:36
  117.6 4.3 %collective-permute-done.29 = bf16[128,512]{1,0:T(8,128)(2,1)S(1)} collective-permute-done((bf16[128,512]{1,0:T(8,128)(2,1)S(1)}, bf16[128,512]{1,0:T(8,128)(2,1)S(1)}, u32[]{:S(2)}, u32[]{:S(2)}) %collective-permute-start.29) | collective-permute-done | bytes 131104 | tf_op jit(solution)/shard_map/ppermute | solution.py:36
  (81 shorter events, 38.6 us)
Async XLA Ops:
  3.9 32.8 %collective-permute-start.3 = (bf16[2064,256]{1,0:T(8,128)(2,1)S(1)}, bf16[2064,256]{1,0:T(8,128)(2,1)S(1)}, u32[]{:S(2)}, u32[]{:S(2)}) collective-permute-start(bf16[2064,256]{1,0:T(8,128)(2,1)S(1)} %get-tuple-element.46.refs_0_), channel_id=1, source_target_pairs={{0,4},{4,0},{8,12},{12,8},{16,20},{20,16},{24,28},{28,24},{1,5},{5... | collective-permute-start | bytes 3170312 | tf_op jit(solution)/shard_map/ppermute | solution.py:31
  4.4 32.3 %collective-permute-start.4 = (bf16[2064,256]{1,0:T(8,128)(2,1)S(1)}, bf16[2064,256]{1,0:T(8,128)(2,1)S(1)}, u32[]{:S(2)}, u32[]{:S(2)}) collective-permute-start(bf16[2064,256]{1,0:T(8,128)(2,1)S(1)} %get-tuple-element.56), channel_id=1, source_target_pairs={{0,8},{4,12},{8,0},{12,4},{16,24},{20,28},{24,16},{28,20},{1,9},{5... | collective-permute-start | bytes 3170312 | tf_op jit(solution)/shard_map/ppermute | solution.py:31
  7.0 29.7 %collective-permute-start.5 = (bf16[2064,256]{1,0:T(8,128)(2,1)S(1)}, bf16[2064,256]{1,0:T(8,128)(2,1)}, u32[]{:S(2)}, u32[]{:S(2)}) collective-permute-start(bf16[2064,256]{1,0:T(8,128)(2,1)S(1)} %get-tuple-element.57), channel_id=1, source_target_pairs={{0,16},{4,20},{8,24},{12,28},{16,0},{20,4},{24,8},{28,12},{1,17},{... | collective-permute-start | bytes 3170312 | tf_op jit(solution)/shard_map/ppermute | solution.py:31
  17.3 11.5 %collective-permute-start = (bf16[144,512]{1,0:T(8,128)(2,1)S(1)}, bf16[144,512]{1,0:T(8,128)(2,1)S(1)}, u32[]{:S(2)}, u32[]{:S(2)}) collective-permute-start(bf16[144,512]{1,0:T(8,128)(2,1)S(1)} %attend.5), channel_id=1, source_target_pairs={{0,1},{1,2},{2,3},{3,0},{4,5},{5,6},{6,7},{7,4},{8,9},{9,10},{10,1... | collective-permute-start | bytes 442376 | tf_op jit(solution)/shard_map/ppermute | solution.py:36
  22.5 11.5 %collective-permute-start.1 = (bf16[144,512]{1,0:T(8,128)(2,1)S(1)}, bf16[144,512]{1,0:T(8,128)(2,1)S(1)}, u32[]{:S(2)}, u32[]{:S(2)}) collective-permute-start(bf16[144,512]{1,0:T(8,128)(2,1)S(1)} %attend.6), channel_id=1, source_target_pairs={{0,2},{1,3},{2,0},{3,1},{4,6},{5,7},{6,4},{7,5},{8,10},{9,11},{10,... | collective-permute-start | bytes 442376 | tf_op jit(solution)/shard_map/ppermute | solution.py:36
  36.7 16.0 %collective-permute-start.9 = (bf16[2064,256]{1,0:T(8,128)(2,1)S(1)}, bf16[2064,256]{1,0:T(8,128)(2,1)}, u32[]{:S(2)}, u32[]{:S(2)}) collective-permute-start(bf16[2064,256]{1,0:T(8,128)(2,1)S(1)} %collective-permute-done.4.refs_1_), channel_id=1, source_target_pairs={{0,4},{4,0},{8,12},{12,8},{16,20},{20,16},{24,28},{28,24},{1,5},{5... | collective-permute-start | bytes 3170312 | tf_op jit(solution)/shard_map/ppermute | solution.py:31
  36.8 15.9 %collective-permute-start.10 = (bf16[2064,256]{1,0:T(8,128)(2,1)}, bf16[2064,256]{1,0:T(8,128)(2,1)}, u32[]{:S(2)}, u32[]{:S(2)}) collective-permute-start(bf16[2064,256]{1,0:T(8,128)(2,1)} %collective-permute-done.5.refs_2_), channel_id=1, source_target_pairs={{0,4},{4,0},{8,12},{12,8},{16,20},{20,16},{24,28},{28,24},{1,5},{5... | collective-permute-start | bytes 3170312 | tf_op jit(solution)/shard_map/ppermute | solution.py:31
  37.3 30.5 %collective-permute-start.18 = (bf16[2064,256]{1,0:T(8,128)(2,1)}, bf16[2064,256]{1,0:T(8,128)(2,1)}, u32[]{:S(2)}, u32[]{:S(2)}) collective-permute-start(bf16[2064,256]{1,0:T(8,128)(2,1)} %get-tuple-element.66), channel_id=1, source_target_pairs={{0,24},{4,28},{8,16},{12,20},{16,8},{20,12},{24,0},{28,4},{1,25},{... | collective-permute-start | bytes 3170312 | tf_op jit(solution)/shard_map/ppermute | solution.py:31
  40.1 11.4 %collective-permute-start.7 = (bf16[128,512]{1,0:T(8,128)(2,1)}, bf16[128,512]{1,0:T(8,128)(2,1)}, u32[]{:S(2)}, u32[]{:S(2)}) collective-permute-start(bf16[128,512]{1,0:T(8,128)(2,1)} %get-tuple-element.60), channel_id=1, source_target_pairs={{0,2},{1,3},{2,0},{3,1},{4,6},{5,7},{6,4},{7,5},{8,10},{9,11},{10,... | collective-permute-start | bytes 393224 | tf_op jit(solution)/shard_map/ppermute | solution.py:36
  52.7 8.3 %collective-permute-start.12 = (bf16[128,512]{1,0:T(8,128)(2,1)S(1)}, bf16[128,512]{1,0:T(8,128)(2,1)S(1)}, u32[]{:S(2)}, u32[]{:S(2)}) collective-permute-start(bf16[128,512]{1,0:T(8,128)(2,1)S(1)} %add_convert_fusion.refs_8_), channel_id=1, source_target_pairs={{0,1},{1,2},{2,3},{3,0},{4,5},{5,6},{6,7},{7,4},{8,9},{9,10},{10,1... | collective-permute-start | bytes 393224 | tf_op jit(solution)/shard_map/ppermute | solution.py:36
  53.3 11.5 %collective-permute-start.14 = (bf16[128,512]{1,0:T(8,128)(2,1)S(1)}, bf16[128,512]{1,0:T(8,128)(2,1)S(1)}, u32[]{:S(2)}, u32[]{:S(2)}) collective-permute-start(bf16[128,512]{1,0:T(8,128)(2,1)S(1)} %add_convert_fusion.refs_8_), channel_id=1, source_target_pairs={{0,2},{1,3},{2,0},{3,1},{4,6},{5,7},{6,4},{7,5},{8,10},{9,11},{10,... | collective-permute-start | bytes 393224 | tf_op jit(solution)/shard_map/ppermute | solution.py:36
  55.7 10.6 %collective-permute-start.16 = (bf16[128,512]{1,0:T(8,128)(2,1)S(1)}, bf16[128,512]{1,0:T(8,128)(2,1)S(1)}, u32[]{:S(2)}, u32[]{:S(2)}) collective-permute-start(bf16[128,512]{1,0:T(8,128)(2,1)S(1)} %add_convert_fusion.refs_8_), channel_id=1, source_target_pairs={{0,3},{1,0},{2,1},{3,2},{4,7},{5,4},{6,5},{7,6},{8,11},{9,8},{10,9... | collective-permute-start | bytes 393224 | tf_op jit(solution)/shard_map/ppermute | solution.py:36
  58.2 9.6 %collective-permute-start.11 = (bf16[128,512]{1,0:T(8,128)(2,1)S(1)}, bf16[128,512]{1,0:T(8,128)(2,1)S(1)}, u32[]{:S(2)}, u32[]{:S(2)}) collective-permute-start(bf16[128,512]{1,0:T(8,128)(2,1)S(1)} %add_convert_fusion.refs_8_), channel_id=1, source_target_pairs={{0,8},{4,12},{8,0},{12,4},{16,24},{20,28},{24,16},{28,20},{1,9},{5... | collective-permute-start | bytes 393224 | tf_op jit(solution)/shard_map/ppermute | solution.py:31
  71.3 9.2 %collective-permute-start.20 = (bf16[256,512]{1,0:T(8,128)(2,1)S(1)}, bf16[256,512]{1,0:T(8,128)(2,1)S(1)}, u32[]{:S(2)}, u32[]{:S(2)}) collective-permute-start(bf16[256,512]{1,0:T(8,128)(2,1)S(1)} %constant_dynamic-update-slice_fusion.refs_0_), channel_id=1, source_target_pairs={{0,16},{4,20},{8,24},{12,28},{16,0},{20,4},{24,8},{28,12},{1,17},{... | collective-permute-start | bytes 786440 | tf_op jit(solution)/shard_map/ppermute | solution.py:31
  72.9 9.2 %collective-permute-start.21 = (bf16[256,512]{1,0:T(8,128)(2,1)S(1)}, bf16[256,512]{1,0:T(8,128)(2,1)S(1)}, u32[]{:S(2)}, u32[]{:S(2)}) collective-permute-start(bf16[256,512]{1,0:T(8,128)(2,1)S(1)} %constant_dynamic-update-slice_fusion.2.refs_2_), channel_id=1, source_target_pairs={{0,8},{4,12},{8,0},{12,4},{16,24},{20,28},{24,16},{28,20},{1,9},{5... | collective-permute-start | bytes 786440 | tf_op jit(solution)/shard_map/ppermute | solution.py:31
  73.5 12.2 %collective-permute-start.22 = (bf16[256,512]{1,0:T(8,128)(2,1)S(1)}, bf16[256,512]{1,0:T(8,128)(2,1)S(1)}, u32[]{:S(2)}, u32[]{:S(2)}) collective-permute-start(bf16[256,512]{1,0:T(8,128)(2,1)S(1)} %constant_dynamic-update-slice_fusion.4.refs_4_), channel_id=1, source_target_pairs={{0,16},{4,20},{8,24},{12,28},{16,0},{20,4},{24,8},{28,12},{1,17},{... | collective-permute-start | bytes 786440 | tf_op jit(solution)/shard_map/ppermute | solution.py:31
  74.2 14.2 %collective-permute-start.23 = (bf16[256,512]{1,0:T(8,128)(2,1)S(1)}, bf16[256,512]{1,0:T(8,128)(2,1)S(1)}, u32[]{:S(2)}, u32[]{:S(2)}) collective-permute-start(bf16[256,512]{1,0:T(8,128)(2,1)S(1)} %constant_dynamic-update-slice_fusion.6.refs_0_), channel_id=1, source_target_pairs={{0,8},{4,12},{8,0},{12,4},{16,24},{20,28},{24,16},{28,20},{1,9},{5... | collective-permute-start | bytes 786440 | tf_op jit(solution)/shard_map/ppermute | solution.py:31
  91.3 9.3 %collective-permute-start.33 = (bf16[256,512]{1,0:T(8,128)(2,1)S(1)}, bf16[256,512]{1,0:T(8,128)(2,1)S(1)}, u32[]{:S(2)}, u32[]{:S(2)}) collective-permute-start(bf16[256,512]{1,0:T(8,128)(2,1)S(1)} %get-tuple-element.89), channel_id=1, source_target_pairs={{0,8},{4,12},{8,0},{12,4},{16,24},{20,28},{24,16},{28,20},{1,9},{5... | collective-permute-start | bytes 786440 | tf_op jit(solution)/shard_map/ppermute | solution.py:31
  91.9 10.3 %collective-permute-start.30 = (bf16[256,512]{1,0:T(8,128)(2,1)S(1)}, bf16[256,512]{1,0:T(8,128)(2,1)S(1)}, u32[]{:S(2)}, u32[]{:S(2)}) collective-permute-start(bf16[256,512]{1,0:T(8,128)(2,1)S(1)} %get-tuple-element.87), channel_id=1, source_target_pairs={{0,16},{4,20},{8,24},{12,28},{16,0},{20,4},{24,8},{28,12},{1,17},{... | collective-permute-start | bytes 786440 | tf_op jit(solution)/shard_map/ppermute | solution.py:31
  93.4 12.8 %collective-permute-start.27 = (bf16[256,512]{1,0:T(8,128)(2,1)S(1)}, bf16[256,512]{1,0:T(8,128)(2,1)S(1)}, u32[]{:S(2)}, u32[]{:S(2)}) collective-permute-start(bf16[256,512]{1,0:T(8,128)(2,1)S(1)} %get-tuple-element.85), channel_id=1, source_target_pairs={{0,8},{4,12},{8,0},{12,4},{16,24},{20,28},{24,16},{28,20},{1,9},{5... | collective-permute-start | bytes 786440 | tf_op jit(solution)/shard_map/ppermute | solution.py:31
  94.9 13.0 %collective-permute-start.24 = (bf16[256,512]{1,0:T(8,128)(2,1)S(1)}, bf16[256,512]{1,0:T(8,128)(2,1)S(1)}, u32[]{:S(2)}, u32[]{:S(2)}) collective-permute-start(bf16[256,512]{1,0:T(8,128)(2,1)S(1)} %get-tuple-element.83), channel_id=1, source_target_pairs={{0,16},{4,20},{8,24},{12,28},{16,0},{20,4},{24,8},{28,12},{1,17},{... | collective-permute-start | bytes 786440 | tf_op jit(solution)/shard_map/ppermute | solution.py:31
  100.7 16.9 %collective-permute-start.34 = (bf16[128,512]{1,0:T(8,128)(2,1)S(1)}, bf16[128,512]{1,0:T(8,128)(2,1)S(1)}, u32[]{:S(2)}, u32[]{:S(2)}) collective-permute-start(bf16[128,512]{1,0:T(8,128)(2,1)S(1)} %slice.62), channel_id=1, source_target_pairs={{0,16},{4,20},{8,24},{12,28},{16,0},{20,4},{24,8},{28,12},{1,17},{... | collective-permute-start | bytes 393224 | tf_op jit(solution)/shard_map/ppermute | solution.py:31
  108.6 9.0 %collective-permute-start.32 = (bf16[128,512]{1,0:T(8,128)(2,1)S(1)}, bf16[128,512]{1,0:T(8,128)(2,1)S(1)}, u32[]{:S(2)}, u32[]{:S(2)}) collective-permute-start(bf16[128,512]{1,0:T(8,128)(2,1)S(1)} %fusion.2), channel_id=1, source_target_pairs={{0,1},{1,2},{2,3},{3,0},{4,5},{5,6},{6,7},{7,4},{8,9},{9,10},{10,1... | collective-permute-start | bytes 393224 | tf_op jit(solution)/shard_map/ppermute | solution.py:36
  111.4 10.6 %collective-permute-start.29 = (bf16[128,512]{1,0:T(8,128)(2,1)S(1)}, bf16[128,512]{1,0:T(8,128)(2,1)S(1)}, u32[]{:S(2)}, u32[]{:S(2)}) collective-permute-start(bf16[128,512]{1,0:T(8,128)(2,1)S(1)} %fusion.3), channel_id=1, source_target_pairs={{0,2},{1,3},{2,0},{3,1},{4,6},{5,7},{6,4},{7,5},{8,10},{9,11},{10,... | collective-permute-start | bytes 393224 | tf_op jit(solution)/shard_map/ppermute | solution.py:36
  (13 other events, 71.9 us)

commit v4 on v3

--- a/solution.py
+++ b/solution.py
@@ -22,6 +22,7 @@
 PREPARE_LIMIT = 12 * 1024 * 1024
 ASSEMBLE_LIMIT = 12 * 1024 * 1024
 SUBLANES = 16
+UP_PARTS = 4
 LOG2_SCALE = math.log2(math.e) / math.sqrt(QK)
 NT = (((1,), (1,)), ((), ()))
 
@@ -43,7 +44,7 @@
 def prepare_kernel(
     offset_ref, table_hbm, len_hbm, queries_hbm, pool_hbm, up_hbm, *refs
 ):
-    q_ref, keys_ref, up_ref, pages_ref, queries_ref, table_ref, len_ref, page_sem, sem = refs
+    q_ref, keys_ref, up_ref, pages_ref, queries_ref, table_ref, len_ref, page_sem, up_sem, sem = refs
     page_count, page_size, _ = pages_ref.shape
     query_rows = queries_ref.shape[0]
 
@@ -57,9 +58,16 @@
         copy.start()
 
     queries_copy = pltpu.make_async_copy(queries_hbm, queries_ref, sem.at[0])
-    up_copy = pltpu.make_async_copy(up_hbm, up_ref, sem.at[1])
+    part = up_ref.shape[0] // UP_PARTS
+    up_copies = [
+        pltpu.make_async_copy(
+            up_hbm.at[pl.ds(i * part, part), :], up_ref.at[pl.ds(i * part, part), :], up_sem.at[i]
+        )
+        for i in range(UP_PARTS)
+    ]
     queries_copy.start()
-    up_copy.start()
+    for copy in up_copies:
+        copy.start()
     for copy in scalar_copies:
         copy.wait()
     page_copies = [
@@ -89,7 +97,8 @@
         == lax.broadcasted_iota(jnp.int32, (query_rows, query_rows), 1)
     ).astype(jnp.bfloat16)
     queries_copy.wait()
-    up_copy.wait()
+    for copy in up_copies:
+        copy.wait()
     for h in range(H):
         rows = pl.ds(h * query_rows, query_rows)
         q_nope = queries_ref[:, h * QK : h * QK + NOPE]
@@ -166,6 +175,7 @@
             pltpu.SMEM(block_table.shape, jnp.int32),
             pltpu.SMEM(page_len.shape, jnp.int32),
             pltpu.SemaphoreType.DMA((page_count,)),
+            pltpu.SemaphoreType.DMA((UP_PARTS,)),
             pltpu.SemaphoreType.DMA((4,)),
         ],
         compiler_params=pltpu.CompilerParams(vmem_limit_bytes=PREPARE_LIMIT),

time: 123 us -> 123 us (level)
  no operation moved by 1% of the time
where the time goes in v4:
time: 123 us
  starting transfers between devices  46.7 us (38%)
  waiting for transfers between devices  37.6 us (31%)
  Pallas kernels  33.8 us (27%)
  other arithmetic  2.31 us (2%)
  between operations  1.55 us (1%)
    ppermute x23, starting transfers between devices, exchange(): return lax.ppermute(x, axis, [(i, i ^ step) for i in range(count)])  24.5 us
    ppermute x12, starting transfers between devices, rotate(): lax.ppermute(x, axis, [(i, (i + step) % count) for i in range(count)])  22.2 us
    ppermute x12, waiting for transfers between devices, rotate(): lax.ppermute(x, axis, [(i, (i + step) % count) for i in range(count)])  19.8 us
    ppermute x23, waiting for transfers between devices, exchange(): return lax.ppermute(x, axis, [(i, i ^ step) for i in range(count)])  17.8 us
    pallas_call x4, Pallas kernels, attend(): pl.pallas_call(functools.partial(attend_kernel, step, groups), out_shape=...  14.5 us
    pallas_call x1, Pallas kernels, prepare(): pl.pallas_call(prepare_kernel, out_shape=[pltpu.VMEM((H * query_rows, wid...  4.56 us
    pallas_call x1, Pallas kernels, assemble(): pl.pallas_call(functools.partial(assemble_kernel, len(blocks) // 2, len(p...  4.39 us
    pallas_call x1, Pallas kernels, cut(): pl.pallas_call(functools.partial(cut_kernel, chips), out_shape=[pltpu.VME...  3.27 us
  transfers between devices with their start and end apart: 35, of which 14 were waited for; matrix products, arithmetic and copies ran while one was open for 1% of the time, Pallas kernels for 22%

profile of v4, /device:TPU:0, one launch (start us, length us, event | category | flops | bytes accessed | tf_op | source)
XLA Modules:
  0.0 122.8 jit_solution(8078602392420798479)
XLA Ops:
  0.6 3.3 %cut.1 = (bf16[2064,256]{1,0:T(8,128)(2,1)S(1)}, bf16[2064,256]{1,0:T(8,128)(2,1)S(1)}, bf16[2064,256]{1,0:T(8,128)(2,1)S(1)}, bf16[2064,256]{1,0:T(8,128)(2,1)}) custom-call(bf16[2736,256]{1,0:T(8,128)(2,1)} %bitcast.2, bf16[2736,256]{1,0:T(8,128)(2,1)} %bitcast.3, bf16[2736,256]{1,0:T(8,128)(2,1)} %down_hbm.1), custom_call_target="tpu_custom_call" | custom-call | tf_op jit(solution)/shard_map/cut/pallas_call | solution.py:137
  4.4 2.6 %collective-permute-start.4 = (bf16[2064,256]{1,0:T(8,128)(2,1)S(1)}, bf16[2064,256]{1,0:T(8,128)(2,1)S(1)}, u32[]{:S(2)}, u32[]{:S(2)}) collective-permute-start(bf16[2064,256]{1,0:T(8,128)(2,1)S(1)} %get-tuple-element.56), channel_id=1, source_target_pairs={{0,8},{4,12},{8,0},{12,4},{16,24},{20,28},{24,16},{28,20},{1,9},{5... | collective-permute-start | bytes 3170312 | tf_op jit(solution)/shard_map/ppermute | solution.py:32
  9.2 4.6 %prepare.1 = (bf16[2048,768]{1,0:T(8,128)(2,1)S(1)}, bf16[2048,768]{1,0:T(8,128)(2,1)S(1)}, bf16[512,4096]{1,0:T(8,128)(2,1)S(1)}) custom-call(s32[1]{0:T(128)S(6)} %copy.17.offset_ref, s32[32]{0:T(128)} %table_hbm.1, s32[32]{0:T(128)} %len_hbm.1, bf16[128,3072]{1,0:T(8,128)(2,1)} %queries_hbm.1, bf16[32,64,576]{2,1,0:T(8,128)(2,1)} %pool_hbm.1, ...), custom_call_target="tpu_custom_call" | custom-call | tf_op jit(solution)/shard_map/prepare/pallas_call | solution.py:163
  13.7 3.6 %attend.5 = bf16[144,512]{1,0:T(8,128)(2,1)S(1)} custom-call(bf16[2048,768]{1,0:T(8,128)(2,1)S(1)} %get-tuple-element.47.q_ref, bf16[2048,768]{1,0:T(8,128)(2,1)S(1)} %get-tuple-element.48.keys_ref, bf16[512,4096]{1,0:T(8,128)(2,1)S(1)} %get-tuple-element.49.up_ref), custom_call_target="tpu_custom_call" | custom-call | flops 1879048192 | bytes 4194304 | tf_op jit(solution)/shard_map/attend/pallas_call | solution.py:225
  19.0 3.6 %attend.6 = bf16[144,512]{1,0:T(8,128)(2,1)S(1)} custom-call(bf16[2048,768]{1,0:T(8,128)(2,1)S(1)} %get-tuple-element.47.q_ref, bf16[2048,768]{1,0:T(8,128)(2,1)S(1)} %get-tuple-element.48.keys_ref, bf16[512,4096]{1,0:T(8,128)(2,1)S(1)} %get-tuple-element.49.up_ref), custom_call_target="tpu_custom_call" | custom-call | flops 1879048192 | bytes 4194304 | tf_op jit(solution)/shard_map/attend/pallas_call | solution.py:225
  22.6 2.7 %collective-permute-start.1 = (bf16[144,512]{1,0:T(8,128)(2,1)S(1)}, bf16[144,512]{1,0:T(8,128)(2,1)S(1)}, u32[]{:S(2)}, u32[]{:S(2)}) collective-permute-start(bf16[144,512]{1,0:T(8,128)(2,1)S(1)} %attend.6), channel_id=1, source_target_pairs={{0,2},{1,3},{2,0},{3,1},{4,6},{5,7},{6,4},{7,5},{8,10},{9,11},{10,... | collective-permute-start | bytes 442376 | tf_op jit(solution)/shard_map/ppermute | solution.py:37
  25.3 3.6 %attend.7 = bf16[144,512]{1,0:T(8,128)(2,1)S(1)} custom-call(bf16[2048,768]{1,0:T(8,128)(2,1)S(1)} %get-tuple-element.47.q_ref, bf16[2048,768]{1,0:T(8,128)(2,1)S(1)} %get-tuple-element.48.keys_ref, bf16[512,4096]{1,0:T(8,128)(2,1)S(1)} %get-tuple-element.49.up_ref), custom_call_target="tpu_custom_call" | custom-call | flops 1879048192 | bytes 4194304 | tf_op jit(solution)/shard_map/attend/pallas_call | solution.py:225
  30.5 3.6 %attend.4.refs_0_ = bf16[144,512]{1,0:T(8,128)(2,1)S(1)} custom-call(bf16[2048,768]{1,0:T(8,128)(2,1)S(1)} %get-tuple-element.47.q_ref, bf16[2048,768]{1,0:T(8,128)(2,1)S(1)} %get-tuple-element.48.keys_ref, bf16[512,4096]{1,0:T(8,128)(2,1)S(1)} %get-tuple-element.49.up_ref), custom_call_target="tpu_custom_call" | custom-call | flops 1879048192 | bytes 4194304 | tf_op jit(solution)/shard_map/attend/pallas_call | solution.py:225
  37.9 2.3 %collective-permute-start.8 = (bf16[128,512]{1,0:T(8,128)(2,1)S(1)}, bf16[128,512]{1,0:T(8,128)(2,1)S(1)}, u32[]{:S(2)}, u32[]{:S(2)}) collective-permute-start(bf16[128,512]{1,0:T(8,128)(2,1)S(1)} %get-tuple-element.61), channel_id=1, source_target_pairs={{0,3},{1,0},{2,1},{3,2},{4,7},{5,4},{6,5},{7,6},{8,11},{9,8},{10,9... | collective-permute-start | bytes 393224 | tf_op jit(solution)/shard_map/ppermute | solution.py:37
  40.1 3.9 %collective-permute-done.8 = bf16[128,512]{1,0:T(8,128)(2,1)S(1)} collective-permute-done((bf16[128,512]{1,0:T(8,128)(2,1)S(1)}, bf16[128,512]{1,0:T(8,128)(2,1)S(1)}, u32[]{:S(2)}, u32[]{:S(2)}) %collective-permute-start.8) | collective-permute-done | bytes 131104 | tf_op jit(solution)/shard_map/ppermute | solution.py:37
  44.7 6.9 %collective-permute-done.7 = bf16[128,512]{1,0:T(8,128)(2,1)} collective-permute-done((bf16[128,512]{1,0:T(8,128)(2,1)}, bf16[128,512]{1,0:T(8,128)(2,1)}, u32[]{:S(2)}, u32[]{:S(2)}) %collective-permute-start.7) | collective-permute-done | bytes 131104 | tf_op jit(solution)/shard_map/ppermute | solution.py:37
  53.3 2.4 %collective-permute-start.14 = (bf16[128,512]{1,0:T(8,128)(2,1)S(1)}, bf16[128,512]{1,0:T(8,128)(2,1)S(1)}, u32[]{:S(2)}, u32[]{:S(2)}) collective-permute-start(bf16[128,512]{1,0:T(8,128)(2,1)S(1)} %add_convert_fusion.refs_8_), channel_id=1, source_target_pairs={{0,2},{1,3},{2,0},{3,1},{4,6},{5,7},{6,4},{7,5},{8,10},{9,11},{10,... | collective-permute-start | bytes 393224 | tf_op jit(solution)/shard_map/ppermute | solution.py:37
  55.7 2.5 %collective-permute-start.16 = (bf16[128,512]{1,0:T(8,128)(2,1)S(1)}, bf16[128,512]{1,0:T(8,128)(2,1)S(1)}, u32[]{:S(2)}, u32[]{:S(2)}) collective-permute-start(bf16[128,512]{1,0:T(8,128)(2,1)S(1)} %add_convert_fusion.refs_8_), channel_id=1, source_target_pairs={{0,3},{1,0},{2,1},{3,2},{4,7},{5,4},{6,5},{7,6},{8,11},{9,8},{10,9... | collective-permute-start | bytes 393224 | tf_op jit(solution)/shard_map/ppermute | solution.py:37
  62.6 2.2 %collective-permute-done.14.refs_10_ = bf16[128,512]{1,0:T(8,128)(2,1)S(1)} collective-permute-done((bf16[128,512]{1,0:T(8,128)(2,1)S(1)}, bf16[128,512]{1,0:T(8,128)(2,1)S(1)}, u32[]{:S(2)}, u32[]{:S(2)}) %collective-permute-start.14) | collective-permute-done | bytes 131104 | tf_op jit(solution)/shard_map/ppermute | solution.py:37
  75.8 4.4 %assemble.1 = (bf16[1376,2048]{1,0:T(8,128)(2,1)S(1)}, bf16[688,2048]{1,0:T(8,128)(2,1)S(1)}, bf16[128,2048]{1,0:T(8,128)(2,1)}) custom-call(bf16[2064,256]{1,0:T(8,128)(2,1)S(1)} %get-tuple-element.46.refs_0_, bf16[2064,256]{1,0:T(8,128)(2,1)S(1)} %collective-permute-done.4.refs_1_, bf16[2064,256]{1,0:T(8,128)(2,1)} %collective-permute-done.5.refs_2_, ...), custom_call_target="tpu_custom_call" | custom-call | bytes 33816576 | tf_op jit(solution)/shard_map/assemble/pallas_call | solution.py:323
  82.2 3.6 %collective-permute-done.22.refs_5_ = bf16[256,512]{1,0:T(8,128)(2,1)S(1)} collective-permute-done((bf16[256,512]{1,0:T(8,128)(2,1)S(1)}, bf16[256,512]{1,0:T(8,128)(2,1)S(1)}, u32[]{:S(2)}, u32[]{:S(2)}) %collective-permute-start.22) | collective-permute-done | bytes 262176 | tf_op jit(solution)/shard_map/ppermute | solution.py:32
  85.8 2.6 %feed_first.1 = (f32[512,1376]{1,0:T(8,128)S(1)}, f32[512,1]{1,0:T(8,128)S(1)}) custom-call(bf16[1376,2048]{1,0:T(8,128)(2,1)S(1)} %get-tuple-element.74.in_ref, bf16[256,512]{1,0:T(8,128)(2,1)S(1)} %constant_dynamic-update-slice_fusion.refs_0_, bf16[256,512]{1,0:T(8,128)(2,1)S(1)} %collective-permute-done.20.refs_1_, ...), custom_call_target="tpu_custom_call" | custom-call | flops 4328521728 | bytes 1048576 | tf_op jit(solution)/shard_map/feed_first/pallas_call | solution.py:365
  88.5 2.9 %feed.1 = (bf16[256,512]{1,0:T(8,128)(2,1)S(1)}, bf16[256,512]{1,0:T(8,128)(2,1)S(1)}, bf16[256,512]{1,0:T(8,128)(2,1)S(1)}, bf16[256,512]{1,0:T(8,128)(2,1)S(1)...) custom-call(bf16[1376,2048]{1,0:T(8,128)(2,1)S(1)} %get-tuple-elemen, ...), custom_call_target="tpu_custom_call" | custom-call | flops 1442840576 | bytes 1048576 | tf_op jit(solution)/shard_map/feed/pallas_call | solution.py:430
  95.5 5.2 %collective-permute-done.33 = bf16[256,512]{1,0:T(8,128)(2,1)S(1)} collective-permute-done((bf16[256,512]{1,0:T(8,128)(2,1)S(1)}, bf16[256,512]{1,0:T(8,128)(2,1)S(1)}, u32[]{:S(2)}, u32[]{:S(2)}) %collective-permute-start.33) | collective-permute-done | bytes 262176 | tf_op jit(solution)/shard_map/ppermute | solution.py:32
  103.1 3.2 %collective-permute-done.27 = bf16[256,512]{1,0:T(8,128)(2,1)S(1)} collective-permute-done((bf16[256,512]{1,0:T(8,128)(2,1)S(1)}, bf16[256,512]{1,0:T(8,128)(2,1)S(1)}, u32[]{:S(2)}, u32[]{:S(2)}) %collective-permute-start.27) | collective-permute-done | bytes 262176 | tf_op jit(solution)/shard_map/ppermute | solution.py:32
  108.7 2.4 %collective-permute-start.32 = (bf16[128,512]{1,0:T(8,128)(2,1)S(1)}, bf16[128,512]{1,0:T(8,128)(2,1)S(1)}, u32[]{:S(2)}, u32[]{:S(2)}) collective-permute-start(bf16[128,512]{1,0:T(8,128)(2,1)S(1)} %fusion.2), channel_id=1, source_target_pairs={{0,1},{1,2},{2,3},{3,0},{4,5},{5,6},{6,7},{7,4},{8,9},{9,10},{10,1... | collective-permute-start | bytes 393224 | tf_op jit(solution)/shard_map/ppermute | solution.py:37
  111.5 3.7 %collective-permute-start.29 = (bf16[128,512]{1,0:T(8,128)(2,1)S(1)}, bf16[128,512]{1,0:T(8,128)(2,1)S(1)}, u32[]{:S(2)}, u32[]{:S(2)}) collective-permute-start(bf16[128,512]{1,0:T(8,128)(2,1)S(1)} %fusion.3), channel_id=1, source_target_pairs={{0,2},{1,3},{2,0},{3,1},{4,6},{5,7},{6,4},{7,5},{8,10},{9,11},{10,... | collective-permute-start | bytes 393224 | tf_op jit(solution)/shard_map/ppermute | solution.py:37
  115.2 2.5 %collective-permute-start.26 = (bf16[128,512]{1,0:T(8,128)(2,1)S(1)}, bf16[128,512]{1,0:T(8,128)(2,1)S(1)}, u32[]{:S(2)}, u32[]{:S(2)}) collective-permute-start(bf16[128,512]{1,0:T(8,128)(2,1)S(1)} %fusion.4), channel_id=1, source_target_pairs={{0,3},{1,0},{2,1},{3,2},{4,7},{5,4},{6,5},{7,6},{8,11},{9,8},{10,9... | collective-permute-start | bytes 393224 | tf_op jit(solution)/shard_map/ppermute | solution.py:37
  117.7 4.3 %collective-permute-done.29 = bf16[128,512]{1,0:T(8,128)(2,1)S(1)} collective-permute-done((bf16[128,512]{1,0:T(8,128)(2,1)S(1)}, bf16[128,512]{1,0:T(8,128)(2,1)S(1)}, u32[]{:S(2)}, u32[]{:S(2)}) %collective-permute-start.29) | collective-permute-done | bytes 131104 | tf_op jit(solution)/shard_map/ppermute | solution.py:37
  (81 shorter events, 38.6 us)
Async XLA Ops:
  3.9 32.9 %collective-permute-start.3 = (bf16[2064,256]{1,0:T(8,128)(2,1)S(1)}, bf16[2064,256]{1,0:T(8,128)(2,1)S(1)}, u32[]{:S(2)}, u32[]{:S(2)}) collective-permute-start(bf16[2064,256]{1,0:T(8,128)(2,1)S(1)} %get-tuple-element.46.refs_0_), channel_id=1, source_target_pairs={{0,4},{4,0},{8,12},{12,8},{16,20},{20,16},{24,28},{28,24},{1,5},{5... | collective-permute-start | bytes 3170312 | tf_op jit(solution)/shard_map/ppermute | solution.py:32
  4.4 32.4 %collective-permute-start.4 = (bf16[2064,256]{1,0:T(8,128)(2,1)S(1)}, bf16[2064,256]{1,0:T(8,128)(2,1)S(1)}, u32[]{:S(2)}, u32[]{:S(2)}) collective-permute-start(bf16[2064,256]{1,0:T(8,128)(2,1)S(1)} %get-tuple-element.56), channel_id=1, source_target_pairs={{0,8},{4,12},{8,0},{12,4},{16,24},{20,28},{24,16},{28,20},{1,9},{5... | collective-permute-start | bytes 3170312 | tf_op jit(solution)/shard_map/ppermute | solution.py:32
  7.0 29.8 %collective-permute-start.5 = (bf16[2064,256]{1,0:T(8,128)(2,1)S(1)}, bf16[2064,256]{1,0:T(8,128)(2,1)}, u32[]{:S(2)}, u32[]{:S(2)}) collective-permute-start(bf16[2064,256]{1,0:T(8,128)(2,1)S(1)} %get-tuple-element.57), channel_id=1, source_target_pairs={{0,16},{4,20},{8,24},{12,28},{16,0},{20,4},{24,8},{28,12},{1,17},{... | collective-permute-start | bytes 3170312 | tf_op jit(solution)/shard_map/ppermute | solution.py:32
  17.4 11.6 %collective-permute-start = (bf16[144,512]{1,0:T(8,128)(2,1)S(1)}, bf16[144,512]{1,0:T(8,128)(2,1)S(1)}, u32[]{:S(2)}, u32[]{:S(2)}) collective-permute-start(bf16[144,512]{1,0:T(8,128)(2,1)S(1)} %attend.5), channel_id=1, source_target_pairs={{0,1},{1,2},{2,3},{3,0},{4,5},{5,6},{6,7},{7,4},{8,9},{9,10},{10,1... | collective-permute-start | bytes 442376 | tf_op jit(solution)/shard_map/ppermute | solution.py:37
  22.6 11.5 %collective-permute-start.1 = (bf16[144,512]{1,0:T(8,128)(2,1)S(1)}, bf16[144,512]{1,0:T(8,128)(2,1)S(1)}, u32[]{:S(2)}, u32[]{:S(2)}) collective-permute-start(bf16[144,512]{1,0:T(8,128)(2,1)S(1)} %attend.6), channel_id=1, source_target_pairs={{0,2},{1,3},{2,0},{3,1},{4,6},{5,7},{6,4},{7,5},{8,10},{9,11},{10,... | collective-permute-start | bytes 442376 | tf_op jit(solution)/shard_map/ppermute | solution.py:37
  36.8 16.0 %collective-permute-start.9 = (bf16[2064,256]{1,0:T(8,128)(2,1)S(1)}, bf16[2064,256]{1,0:T(8,128)(2,1)}, u32[]{:S(2)}, u32[]{:S(2)}) collective-permute-start(bf16[2064,256]{1,0:T(8,128)(2,1)S(1)} %collective-permute-done.4.refs_1_), channel_id=1, source_target_pairs={{0,4},{4,0},{8,12},{12,8},{16,20},{20,16},{24,28},{28,24},{1,5},{5... | collective-permute-start | bytes 3170312 | tf_op jit(solution)/shard_map/ppermute | solution.py:32
  36.9 15.9 %collective-permute-start.10 = (bf16[2064,256]{1,0:T(8,128)(2,1)}, bf16[2064,256]{1,0:T(8,128)(2,1)}, u32[]{:S(2)}, u32[]{:S(2)}) collective-permute-start(bf16[2064,256]{1,0:T(8,128)(2,1)} %collective-permute-done.5.refs_2_), channel_id=1, source_target_pairs={{0,4},{4,0},{8,12},{12,8},{16,20},{20,16},{24,28},{28,24},{1,5},{5... | collective-permute-start | bytes 3170312 | tf_op jit(solution)/shard_map/ppermute | solution.py:32
  37.4 30.5 %collective-permute-start.18 = (bf16[2064,256]{1,0:T(8,128)(2,1)}, bf16[2064,256]{1,0:T(8,128)(2,1)}, u32[]{:S(2)}, u32[]{:S(2)}) collective-permute-start(bf16[2064,256]{1,0:T(8,128)(2,1)} %get-tuple-element.66), channel_id=1, source_target_pairs={{0,24},{4,28},{8,16},{12,20},{16,8},{20,12},{24,0},{28,4},{1,25},{... | collective-permute-start | bytes 3170312 | tf_op jit(solution)/shard_map/ppermute | solution.py:32
  40.1 11.4 %collective-permute-start.7 = (bf16[128,512]{1,0:T(8,128)(2,1)}, bf16[128,512]{1,0:T(8,128)(2,1)}, u32[]{:S(2)}, u32[]{:S(2)}) collective-permute-start(bf16[128,512]{1,0:T(8,128)(2,1)} %get-tuple-element.60), channel_id=1, source_target_pairs={{0,2},{1,3},{2,0},{3,1},{4,6},{5,7},{6,4},{7,5},{8,10},{9,11},{10,... | collective-permute-start | bytes 393224 | tf_op jit(solution)/shard_map/ppermute | solution.py:37
  52.8 8.3 %collective-permute-start.12 = (bf16[128,512]{1,0:T(8,128)(2,1)S(1)}, bf16[128,512]{1,0:T(8,128)(2,1)S(1)}, u32[]{:S(2)}, u32[]{:S(2)}) collective-permute-start(bf16[128,512]{1,0:T(8,128)(2,1)S(1)} %add_convert_fusion.refs_8_), channel_id=1, source_target_pairs={{0,1},{1,2},{2,3},{3,0},{4,5},{5,6},{6,7},{7,4},{8,9},{9,10},{10,1... | collective-permute-start | bytes 393224 | tf_op jit(solution)/shard_map/ppermute | solution.py:37
  53.3 11.5 %collective-permute-start.14 = (bf16[128,512]{1,0:T(8,128)(2,1)S(1)}, bf16[128,512]{1,0:T(8,128)(2,1)S(1)}, u32[]{:S(2)}, u32[]{:S(2)}) collective-permute-start(bf16[128,512]{1,0:T(8,128)(2,1)S(1)} %add_convert_fusion.refs_8_), channel_id=1, source_target_pairs={{0,2},{1,3},{2,0},{3,1},{4,6},{5,7},{6,4},{7,5},{8,10},{9,11},{10,... | collective-permute-start | bytes 393224 | tf_op jit(solution)/shard_map/ppermute | solution.py:37
  55.7 10.6 %collective-permute-start.16 = (bf16[128,512]{1,0:T(8,128)(2,1)S(1)}, bf16[128,512]{1,0:T(8,128)(2,1)S(1)}, u32[]{:S(2)}, u32[]{:S(2)}) collective-permute-start(bf16[128,512]{1,0:T(8,128)(2,1)S(1)} %add_convert_fusion.refs_8_), channel_id=1, source_target_pairs={{0,3},{1,0},{2,1},{3,2},{4,7},{5,4},{6,5},{7,6},{8,11},{9,8},{10,9... | collective-permute-start | bytes 393224 | tf_op jit(solution)/shard_map/ppermute | solution.py:37
  58.3 9.6 %collective-permute-start.11 = (bf16[128,512]{1,0:T(8,128)(2,1)S(1)}, bf16[128,512]{1,0:T(8,128)(2,1)S(1)}, u32[]{:S(2)}, u32[]{:S(2)}) collective-permute-start(bf16[128,512]{1,0:T(8,128)(2,1)S(1)} %add_convert_fusion.refs_8_), channel_id=1, source_target_pairs={{0,8},{4,12},{8,0},{12,4},{16,24},{20,28},{24,16},{28,20},{1,9},{5... | collective-permute-start | bytes 393224 | tf_op jit(solution)/shard_map/ppermute | solution.py:32
  71.4 9.2 %collective-permute-start.20 = (bf16[256,512]{1,0:T(8,128)(2,1)S(1)}, bf16[256,512]{1,0:T(8,128)(2,1)S(1)}, u32[]{:S(2)}, u32[]{:S(2)}) collective-permute-start(bf16[256,512]{1,0:T(8,128)(2,1)S(1)} %constant_dynamic-update-slice_fusion.refs_0_), channel_id=1, source_target_pairs={{0,16},{4,20},{8,24},{12,28},{16,0},{20,4},{24,8},{28,12},{1,17},{... | collective-permute-start | bytes 786440 | tf_op jit(solution)/shard_map/ppermute | solution.py:32
  73.0 9.2 %collective-permute-start.21 = (bf16[256,512]{1,0:T(8,128)(2,1)S(1)}, bf16[256,512]{1,0:T(8,128)(2,1)S(1)}, u32[]{:S(2)}, u32[]{:S(2)}) collective-permute-start(bf16[256,512]{1,0:T(8,128)(2,1)S(1)} %constant_dynamic-update-slice_fusion.2.refs_2_), channel_id=1, source_target_pairs={{0,8},{4,12},{8,0},{12,4},{16,24},{20,28},{24,16},{28,20},{1,9},{5... | collective-permute-start | bytes 786440 | tf_op jit(solution)/shard_map/ppermute | solution.py:32
  73.6 12.2 %collective-permute-start.22 = (bf16[256,512]{1,0:T(8,128)(2,1)S(1)}, bf16[256,512]{1,0:T(8,128)(2,1)S(1)}, u32[]{:S(2)}, u32[]{:S(2)}) collective-permute-start(bf16[256,512]{1,0:T(8,128)(2,1)S(1)} %constant_dynamic-update-slice_fusion.4.refs_4_), channel_id=1, source_target_pairs={{0,16},{4,20},{8,24},{12,28},{16,0},{20,4},{24,8},{28,12},{1,17},{... | collective-permute-start | bytes 786440 | tf_op jit(solution)/shard_map/ppermute | solution.py:32
  74.2 14.2 %collective-permute-start.23 = (bf16[256,512]{1,0:T(8,128)(2,1)S(1)}, bf16[256,512]{1,0:T(8,128)(2,1)S(1)}, u32[]{:S(2)}, u32[]{:S(2)}) collective-permute-start(bf16[256,512]{1,0:T(8,128)(2,1)S(1)} %constant_dynamic-update-slice_fusion.6.refs_0_), channel_id=1, source_target_pairs={{0,8},{4,12},{8,0},{12,4},{16,24},{20,28},{24,16},{28,20},{1,9},{5... | collective-permute-start | bytes 786440 | tf_op jit(solution)/shard_map/ppermute | solution.py:32
  91.4 9.3 %collective-permute-start.33 = (bf16[256,512]{1,0:T(8,128)(2,1)S(1)}, bf16[256,512]{1,0:T(8,128)(2,1)S(1)}, u32[]{:S(2)}, u32[]{:S(2)}) collective-permute-start(bf16[256,512]{1,0:T(8,128)(2,1)S(1)} %get-tuple-element.89), channel_id=1, source_target_pairs={{0,8},{4,12},{8,0},{12,4},{16,24},{20,28},{24,16},{28,20},{1,9},{5... | collective-permute-start | bytes 786440 | tf_op jit(solution)/shard_map/ppermute | solution.py:32
  92.0 10.4 %collective-permute-start.30 = (bf16[256,512]{1,0:T(8,128)(2,1)S(1)}, bf16[256,512]{1,0:T(8,128)(2,1)S(1)}, u32[]{:S(2)}, u32[]{:S(2)}) collective-permute-start(bf16[256,512]{1,0:T(8,128)(2,1)S(1)} %get-tuple-element.87), channel_id=1, source_target_pairs={{0,16},{4,20},{8,24},{12,28},{16,0},{20,4},{24,8},{28,12},{1,17},{... | collective-permute-start | bytes 786440 | tf_op jit(solution)/shard_map/ppermute | solution.py:32
  93.5 12.8 %collective-permute-start.27 = (bf16[256,512]{1,0:T(8,128)(2,1)S(1)}, bf16[256,512]{1,0:T(8,128)(2,1)S(1)}, u32[]{:S(2)}, u32[]{:S(2)}) collective-permute-start(bf16[256,512]{1,0:T(8,128)(2,1)S(1)} %get-tuple-element.85), channel_id=1, source_target_pairs={{0,8},{4,12},{8,0},{12,4},{16,24},{20,28},{24,16},{28,20},{1,9},{5... | collective-permute-start | bytes 786440 | tf_op jit(solution)/shard_map/ppermute | solution.py:32
  95.0 13.0 %collective-permute-start.24 = (bf16[256,512]{1,0:T(8,128)(2,1)S(1)}, bf16[256,512]{1,0:T(8,128)(2,1)S(1)}, u32[]{:S(2)}, u32[]{:S(2)}) collective-permute-start(bf16[256,512]{1,0:T(8,128)(2,1)S(1)} %get-tuple-element.83), channel_id=1, source_target_pairs={{0,16},{4,20},{8,24},{12,28},{16,0},{20,4},{24,8},{28,12},{1,17},{... | collective-permute-start | bytes 786440 | tf_op jit(solution)/shard_map/ppermute | solution.py:32
  100.8 16.9 %collective-permute-start.34 = (bf16[128,512]{1,0:T(8,128)(2,1)S(1)}, bf16[128,512]{1,0:T(8,128)(2,1)S(1)}, u32[]{:S(2)}, u32[]{:S(2)}) collective-permute-start(bf16[128,512]{1,0:T(8,128)(2,1)S(1)} %slice.62), channel_id=1, source_target_pairs={{0,16},{4,20},{8,24},{12,28},{16,0},{20,4},{24,8},{28,12},{1,17},{... | collective-permute-start | bytes 393224 | tf_op jit(solution)/shard_map/ppermute | solution.py:32
  108.7 9.0 %collective-permute-start.32 = (bf16[128,512]{1,0:T(8,128)(2,1)S(1)}, bf16[128,512]{1,0:T(8,128)(2,1)S(1)}, u32[]{:S(2)}, u32[]{:S(2)}) collective-permute-start(bf16[128,512]{1,0:T(8,128)(2,1)S(1)} %fusion.2), channel_id=1, source_target_pairs={{0,1},{1,2},{2,3},{3,0},{4,5},{5,6},{6,7},{7,4},{8,9},{9,10},{10,1... | collective-permute-start | bytes 393224 | tf_op jit(solution)/shard_map/ppermute | solution.py:37
  111.5 10.5 %collective-permute-start.29 = (bf16[128,512]{1,0:T(8,128)(2,1)S(1)}, bf16[128,512]{1,0:T(8,128)(2,1)S(1)}, u32[]{:S(2)}, u32[]{:S(2)}) collective-permute-start(bf16[128,512]{1,0:T(8,128)(2,1)S(1)} %fusion.3), channel_id=1, source_target_pairs={{0,2},{1,3},{2,0},{3,1},{4,6},{5,7},{6,4},{7,5},{8,10},{9,11},{10,... | collective-permute-start | bytes 393224 | tf_op jit(solution)/shard_map/ppermute | solution.py:37
  (13 other events, 71.9 us)
